TPU v7x, 128 devices: a whole 4x4x4 slice. The times are simulated.
128 devices in a mesh: ctx: 8 (over y_lo, x), dp: 2 (over core), fsdp: 8 (over z, y_hi).
Axes of the slice: x: 4, y: 4 (y_hi: 2, y_lo: 2; y = y_hi * 2 + y_lo), z: 4, core: 2. Of those that a mesh axis runs over, the one named last changes fastest.
Arguments:
- inputs: float32 [16, 1024, 768], P(('dp', 'fsdp'), 'ctx'), may hold values from -6 to 6
- positions: int32 [16, 1024], P(('dp', 'fsdp'), 'ctx'), may hold values from 0 to 1023, as said below
- cotangent: float32 [16, 1024, 768], P(('dp', 'fsdp'), 'ctx'), may hold values from -6 to 6
- w_qkv: bfloat16 [2, 768, 2304], P(None, 'fsdp'), may hold values from -0.21875 to 0.21875
- b_qkv: bfloat16 [2, 2304], P(None, 'fsdp'), may hold values from -3 to 3
- w_out: bfloat16 [2, 768, 768], P(None, 'fsdp'), may hold values from -0.875 to 0.875
- b_out: bfloat16 [2, 768], P(None, 'fsdp'), may hold values from -1.75 to 1.75
- w_up: bfloat16 [2, 768, 3072], P(None, 'fsdp'), may hold values from -0.21875 to 0.21875
- b_up: bfloat16 [2, 3072], P(None, 'fsdp'), may hold values from -3 to 3
- w_down: bfloat16 [2, 3072, 768], P(None, 'fsdp'), may hold values from -0.109375 to 0.109375
- b_down: bfloat16 [2, 768], P(None, 'fsdp'), may hold values from -1.75 to 1.75
- ln_gain: bfloat16 [2, 768], P(None, 'fsdp'), may hold values from 0.5 to 1.5
- ln_bias: bfloat16 [2, 768], P(None, 'fsdp'), may hold values from -1.75 to 1.75
Outputs:
- outputs: float32 [16, 1024, 768], P(('dp', 'fsdp'), 'ctx')
- grad_inputs: float32 [16, 1024, 768], P(('dp', 'fsdp'), 'ctx')
- grad_w_qkv: float32 [2, 768, 2304], P(None, 'fsdp')
- grad_b_qkv: float32 [2, 2304], P(None, 'fsdp')
- grad_w_out: float32 [2, 768, 768], P(None, 'fsdp')
- grad_b_out: float32 [2, 768], P(None, 'fsdp')
- grad_w_up: float32 [2, 768, 3072], P(None, 'fsdp')
- grad_b_up: float32 [2, 3072], P(None, 'fsdp')
- grad_w_down: float32 [2, 3072, 768], P(None, 'fsdp')
- grad_b_down: float32 [2, 768], P(None, 'fsdp')
- grad_gain: float32 [2, 768], P(None, 'fsdp')
- grad_shift: float32 [2, 768], P(None, 'fsdp')
Inputs may be any that keep to these rules, and one draw needn't show every extreme that they name: Each row is one sequence's positions in stored order, made of 16 blocks of 64 consecutive positions. The row's stored tokens come in consecutive pairs of blocks; the blocks of a pair are position blocks b and 15 - b, in either order; which b goes to which pair is drawn afresh for each row. Every position appears once in a row.
All inputs are finite; a program needn't handle non-finite values.
Results may differ from a plain program's by a relative error of at most 0.02.
Values may be sent and summed in bfloat16 or wider, within the bound.
A program may use at most 192 MiB of HBM per device.

v0:
```python
import jax
import jax.numpy as jnp
from jax import lax
from jax.sharding import PartitionSpec as P

HEAD_DIM = 64
ROT = 16
LAYERS = 2


epsilon = 1e-05


def rotary(values, places):
    half_rot = ROT // 2
    frequency = 10000.0 ** (-2.0 * jnp.arange(half_rot, dtype=jnp.float32) / ROT)
    angles = places.astype(jnp.float32)[..., None] * frequency
    cosine = jnp.cos(angles)[..., None, :]
    sine_part = jnp.sin(angles)[..., None, :]
    first_half = values[..., :half_rot]
    second = values[..., half_rot:ROT]
    return jnp.concatenate(
        [
            first_half * cosine - second * sine_part,
            second * cosine + first_half * sine_part,
            values[..., ROT:],
        ],
        axis=-1,
    )


def norm_part(stream, gain_vec, shift_vec):
    row_mean = jnp.mean(stream, axis=-1, keepdims=True)
    centred = stream - row_mean
    row_var = jnp.mean(centred * centred, axis=-1, keepdims=True)
    return centred * lax.rsqrt(row_var + epsilon) * gain_vec + shift_vec


def gelu_exact(values):
    return jax.nn.gelu(values, approximate=False)


def gather_weights(shards, index_layer):
    return (
        lax.all_gather(shards[0][index_layer], "fsdp", axis=0, tiled=True),
        lax.all_gather(shards[1][index_layer], "fsdp", axis=0, tiled=True),
        lax.all_gather(shards[2][index_layer], "fsdp", axis=0, tiled=True),
        lax.all_gather(shards[3][index_layer], "fsdp", axis=0, tiled=True),
        lax.all_gather(shards[4][index_layer], "fsdp", axis=0, tiled=True),
        lax.all_gather(shards[5][index_layer], "fsdp", axis=0, tiled=True),
        lax.all_gather(shards[6][index_layer], "fsdp", axis=0, tiled=True),
        lax.all_gather(shards[7][index_layer], "fsdp", axis=0, tiled=True),
        lax.all_gather(shards[8][index_layer], "fsdp", axis=0, tiled=True),
        lax.all_gather(shards[9][index_layer], "fsdp", axis=0, tiled=True),
    )


def gather_weights_again(shards, index_layer):
    return (
        lax.all_gather(shards[0][index_layer], "fsdp", axis=0, tiled=True),
        lax.all_gather(shards[1][index_layer], "fsdp", axis=0, tiled=True),
        lax.all_gather(shards[2][index_layer], "fsdp", axis=0, tiled=True),
        lax.all_gather(shards[3][index_layer], "fsdp", axis=0, tiled=True),
        lax.all_gather(shards[4][index_layer], "fsdp", axis=0, tiled=True),
        lax.all_gather(shards[5][index_layer], "fsdp", axis=0, tiled=True),
        lax.all_gather(shards[6][index_layer], "fsdp", axis=0, tiled=True),
        lax.all_gather(shards[7][index_layer], "fsdp", axis=0, tiled=True),
        lax.all_gather(shards[8][index_layer], "fsdp", axis=0, tiled=True),
        lax.all_gather(shards[9][index_layer], "fsdp", axis=0, tiled=True),
    )


def reduce_grads(parts):
    reduced = (
        lax.psum_scatter(
            parts[0].astype(jnp.bfloat16), "fsdp", scatter_dimension=0, tiled=True
        ).astype(jnp.float32),
        lax.psum_scatter(
            parts[1].astype(jnp.bfloat16), "fsdp", scatter_dimension=0, tiled=True
        ).astype(jnp.float32),
        lax.psum_scatter(
            parts[2].astype(jnp.bfloat16), "fsdp", scatter_dimension=0, tiled=True
        ).astype(jnp.float32),
        lax.psum_scatter(
            parts[3].astype(jnp.bfloat16), "fsdp", scatter_dimension=0, tiled=True
        ).astype(jnp.float32),
        lax.psum_scatter(
            parts[4].astype(jnp.bfloat16), "fsdp", scatter_dimension=0, tiled=True
        ).astype(jnp.float32),
        lax.psum_scatter(
            parts[5].astype(jnp.bfloat16), "fsdp", scatter_dimension=0, tiled=True
        ).astype(jnp.float32),
        lax.psum_scatter(
            parts[6].astype(jnp.bfloat16), "fsdp", scatter_dimension=0, tiled=True
        ).astype(jnp.float32),
        lax.psum_scatter(
            parts[7].astype(jnp.bfloat16), "fsdp", scatter_dimension=0, tiled=True
        ).astype(jnp.float32),
        lax.psum_scatter(
            parts[8].astype(jnp.bfloat16), "fsdp", scatter_dimension=0, tiled=True
        ).astype(jnp.float32),
        lax.psum_scatter(
            parts[9].astype(jnp.bfloat16), "fsdp", scatter_dimension=0, tiled=True
        ).astype(jnp.float32),
    )
    summed = (
        lax.psum(reduced[0].astype(jnp.bfloat16), ("ctx", "dp")).astype(jnp.float32),
        lax.psum(reduced[1].astype(jnp.bfloat16), ("ctx", "dp")).astype(jnp.float32),
        lax.psum(reduced[2].astype(jnp.bfloat16), ("ctx", "dp")).astype(jnp.float32),
        lax.psum(reduced[3].astype(jnp.bfloat16), ("ctx", "dp")).astype(jnp.float32),
        lax.psum(reduced[4].astype(jnp.bfloat16), ("ctx", "dp")).astype(jnp.float32),
        lax.psum(reduced[5].astype(jnp.bfloat16), ("ctx", "dp")).astype(jnp.float32),
        lax.psum(reduced[6].astype(jnp.bfloat16), ("ctx", "dp")).astype(jnp.float32),
        lax.psum(reduced[7].astype(jnp.bfloat16), ("ctx", "dp")).astype(jnp.float32),
        lax.psum(reduced[8].astype(jnp.bfloat16), ("ctx", "dp")).astype(jnp.float32),
        lax.psum(reduced[9].astype(jnp.bfloat16), ("ctx", "dp")).astype(jnp.float32),
    )
    return summed


def project_local(stream, places, weights):
    w_qkv, b_qkv, w_out, b_out, w_up, b_up, w_down, b_down, gain_vec, shift_vec = weights
    seqs, local, width = stream.shape
    heads = width // HEAD_DIM
    normed = norm_part(stream, gain_vec.astype(jnp.float32), shift_vec.astype(jnp.float32))
    normed_low = normed.astype(jnp.bfloat16)
    qkv_proj = jnp.einsum(
        "std,de->ste", normed_low, w_qkv, preferred_element_type=jnp.float32
    ) + b_qkv.astype(jnp.float32)
    grouped = qkv_proj.reshape(seqs, local, heads, 3, HEAD_DIM)
    query = grouped[:, :, :, 0, :]
    key_part = grouped[:, :, :, 1, :]
    value_low = grouped[:, :, :, 2, :].reshape(seqs, local, width).astype(jnp.bfloat16)
    query_rot = (rotary(query, places) * HEAD_DIM ** (-0.5)).astype(jnp.bfloat16)
    key_rot = rotary(key_part, places).astype(jnp.bfloat16).reshape(seqs, local, width)
    hidden_pre = jnp.einsum(
        "std,df->stf", normed_low, w_up, preferred_element_type=jnp.float32
    ) + b_up.astype(jnp.float32)
    return (normed_low, query_rot, key_rot, value_low, hidden_pre)


def attention_out(query_rot, key_pair, places, places_all):
    seqs, local, heads, head_dim = query_rot.shape
    key_heads = key_pair[0].reshape(seqs, -1, heads, head_dim)
    value_heads = key_pair[1].reshape(seqs, -1, heads, head_dim)
    scores = jnp.einsum("sqhd,skhd->shqk", query_rot, key_heads, preferred_element_type=jnp.float32)
    causal_mask = (places[:, :, None] >= places_all[:, None, :])[:, None]
    scores = jnp.where(causal_mask, scores, -jnp.inf)
    row_max = jnp.max(scores, axis=-1, keepdims=True)
    expos = jnp.exp(scores - row_max)
    probs = expos / jnp.sum(expos, axis=-1, keepdims=True)
    probs_low = probs.astype(jnp.bfloat16)
    attended = jnp.einsum(
        "shqk,skhd->sqhd", probs_low, value_heads, preferred_element_type=jnp.float32
    )
    attended_low = attended.reshape(seqs, local, heads * head_dim).astype(jnp.bfloat16)
    return (probs, probs_low, key_heads, value_heads, attended_low)


def layer_forward(stream, places, places_all, weights, key_pair, query_rot, hidden_pre):
    w_qkv, b_qkv, w_out, b_out, w_up, b_up, w_down, b_down, gain_vec, shift_vec = weights
    probs, probs_low, key_heads, value_heads, attended_low = attention_out(
        query_rot, key_pair, places, places_all
    )
    hidden_low = gelu_exact(hidden_pre).astype(jnp.bfloat16)
    branch = jnp.einsum("std,de->ste", attended_low, w_out, preferred_element_type=jnp.float32)
    branch = branch + jnp.einsum(
        "stf,fe->ste", hidden_low, w_down, preferred_element_type=jnp.float32
    )
    return stream + (branch + b_out.astype(jnp.float32) + b_down.astype(jnp.float32))


def layer_backward(stream, grad_next, places, places_all, weights, key_pair, local_parts):
    w_qkv, b_qkv, w_out, b_out, w_up, b_up, w_down, b_down, gain_vec, shift_vec = weights
    normed_low, query_rot, key_rot, value_low, hidden_pre = local_parts
    seqs, local, width = stream.shape
    heads = width // HEAD_DIM
    probs, probs_low, key_heads, value_heads, attended_low = attention_out(
        query_rot, key_pair, places, places_all
    )
    hidden_act, gelu_back = jax.vjp(gelu_exact, hidden_pre)
    hidden_low = hidden_act.astype(jnp.bfloat16)
    grad_low = grad_next.astype(jnp.bfloat16)
    grad_b_branch = jnp.sum(grad_low.astype(jnp.float32), axis=(0, 1))
    grad_w_out = jnp.einsum(
        "std,ste->de", attended_low, grad_low, preferred_element_type=jnp.float32
    )
    grad_w_down = jnp.einsum(
        "stf,ste->fe", hidden_low, grad_low, preferred_element_type=jnp.float32
    )
    grad_attended = jnp.einsum(
        "ste,de->std", grad_low, w_out, preferred_element_type=jnp.float32
    ).astype(jnp.bfloat16)
    grad_hidden = jnp.einsum("ste,fe->stf", grad_low, w_down, preferred_element_type=jnp.float32)
    grad_pre = gelu_back(grad_hidden)[0].astype(jnp.bfloat16)
    grad_b_up = jnp.sum(grad_pre.astype(jnp.float32), axis=(0, 1))
    grad_w_up = jnp.einsum("std,stf->df", normed_low, grad_pre, preferred_element_type=jnp.float32)
    grad_normed = jnp.einsum("stf,df->std", grad_pre, w_up, preferred_element_type=jnp.float32)
    grad_heads = grad_attended.reshape(seqs, local, heads, HEAD_DIM)
    grad_probs = jnp.einsum(
        "sqhd,skhd->shqk", grad_heads, value_heads, preferred_element_type=jnp.float32
    )
    grad_scores = (
        probs * (grad_probs - jnp.sum(grad_probs * probs, axis=-1, keepdims=True))
    ).astype(jnp.bfloat16)
    grad_query_rot = jnp.einsum(
        "shqk,skhd->sqhd", grad_scores, key_heads, preferred_element_type=jnp.float32
    )
    grad_key_all = jnp.einsum(
        "shqk,sqhd->skhd", grad_scores, query_rot, preferred_element_type=jnp.float32
    ).reshape(seqs, -1, width)
    grad_value_all = jnp.einsum(
        "shqk,sqhd->skhd", probs_low, grad_heads, preferred_element_type=jnp.float32
    ).reshape(seqs, -1, width)
    grad_key_rot, grad_value = (
        lax.psum_scatter(grad_key_all, "ctx", scatter_dimension=1, tiled=True),
        lax.psum_scatter(grad_value_all, "ctx", scatter_dimension=1, tiled=True),
    )
    unused, rotary_back = jax.vjp(
        lambda values: rotary(values, places),
        jnp.zeros((seqs, local, heads, HEAD_DIM), jnp.float32),
    )
    grad_query = rotary_back(grad_query_rot * HEAD_DIM ** (-0.5))[0]
    grad_key = rotary_back(grad_key_rot.reshape(seqs, local, heads, HEAD_DIM))[0]
    grad_value_heads = grad_value.reshape(seqs, local, heads, HEAD_DIM)
    grad_qkv = (
        jnp.stack([grad_query, grad_key, grad_value_heads], axis=3)
        .reshape(seqs, local, 3 * width)
        .astype(jnp.bfloat16)
    )
    grad_b_qkv = jnp.sum(grad_qkv.astype(jnp.float32), axis=(0, 1))
    grad_w_qkv = jnp.einsum("std,ste->de", normed_low, grad_qkv, preferred_element_type=jnp.float32)
    grad_normed = grad_normed + jnp.einsum(
        "ste,de->std", grad_qkv, w_qkv, preferred_element_type=jnp.float32
    )
    unused_norm, norm_back = jax.vjp(
        norm_part, stream, gain_vec.astype(jnp.float32), shift_vec.astype(jnp.float32)
    )
    grad_stream, grad_gain, grad_shift = norm_back(grad_normed)
    summed = reduce_grads(
        (
            grad_w_qkv,
            grad_b_qkv,
            grad_w_out,
            grad_b_branch,
            grad_w_up,
            grad_b_up,
            grad_w_down,
            grad_b_branch,
            grad_gain,
            grad_shift,
        )
    )
    return (grad_next + grad_stream, summed)


def body(
    inputs,
    positions,
    cotangent,
    w_qkv,
    b_qkv,
    w_out,
    b_out,
    w_up,
    b_up,
    w_down,
    b_down,
    ln_gain,
    ln_bias,
):
    shards = (w_qkv, b_qkv, w_out, b_out, w_up, b_up, w_down, b_down, ln_gain, ln_bias)
    places_all = lax.all_gather(positions, "ctx", axis=1, tiled=True)
    saved_streams = []
    saved_weights = []
    saved_keys = []
    stream = inputs
    for index_layer in range(LAYERS):
        weights = gather_weights(shards, index_layer)
        normed_low, query_rot, key_rot, value_low, hidden_pre = project_local(
            stream, positions, weights
        )
        key_pair = (
            lax.all_gather(key_rot, "ctx", axis=1, tiled=True),
            lax.all_gather(value_low, "ctx", axis=1, tiled=True),
        )
        saved_streams.append(stream)
        saved_weights.append(weights)
        saved_keys.append(key_pair)
        stream = layer_forward(
            stream, positions, places_all, weights, key_pair, query_rot, hidden_pre
        )
    grad_stream = cotangent
    collected = [None] * LAYERS
    for index_layer in reversed(range(LAYERS)):
        weights = gather_weights_again(shards, index_layer)
        local_parts = project_local(saved_streams[index_layer], positions, weights)
        key_pair = (
            lax.all_gather(local_parts[2], "ctx", axis=1, tiled=True),
            lax.all_gather(local_parts[3], "ctx", axis=1, tiled=True),
        )
        grad_stream, layer_grads = layer_backward(
            saved_streams[index_layer],
            grad_stream,
            positions,
            places_all,
            weights,
            key_pair,
            local_parts,
        )
        collected[index_layer] = layer_grads
    stacked = tuple((jnp.stack([collected[i][j] for i in range(LAYERS)]) for j in range(10)))
    return (stream, grad_stream) + stacked


def solution(mesh):
    in_specs = (
        P(("dp", "fsdp"), "ctx", None),
        P(("dp", "fsdp"), "ctx"),
        P(("dp", "fsdp"), "ctx", None),
        P(None, "fsdp", None),
        P(None, "fsdp"),
        P(None, "fsdp", None),
        P(None, "fsdp"),
        P(None, "fsdp", None),
        P(None, "fsdp"),
        P(None, "fsdp", None),
        P(None, "fsdp"),
        P(None, "fsdp"),
        P(None, "fsdp"),
    )
    out_specs = (
        P(("dp", "fsdp"), "ctx", None),
        P(("dp", "fsdp"), "ctx", None),
        P(None, "fsdp", None),
        P(None, "fsdp"),
        P(None, "fsdp", None),
        P(None, "fsdp"),
        P(None, "fsdp", None),
        P(None, "fsdp"),
        P(None, "fsdp", None),
        P(None, "fsdp"),
        P(None, "fsdp"),
        P(None, "fsdp"),
    )
    return jax.shard_map(body, mesh=mesh, in_specs=in_specs, out_specs=out_specs, check_vma=False)
```

profile of v0, /device:TPU:1, one launch (start us, length us, event | category | flops | bytes accessed | tf_op | source)
XLA Modules:
  0.0 1755.2 jit_solution(14597403301071327141)
XLA Ops:
  17.1 37.2 %all-reduce.35 = (bf16[768]{0:T(1024)(128)(2,1)S(1)}, bf16[768]{0:T(1024)(128)(2,1)S(1)}, bf16[2304]{0:T(1024)(128)(2,1)S(1)}, bf16[768]{0:T(1024)(128)(2,1)S(1)...) all-reduce(bf16[768]{0:T(1024)(128)(2,1)S(1)} %dynamic-update-slice, ...), channel_id=3, replica_groups=mesh['ctx'=8,'dp'=2,'fsdp'=8] {'fsdp'}, use_global_device_ids=true, to_apply=%add.13 | all-reduce | flops 9216 | bytes 36864
  165.1 68.3 %all-gather.47.cloned.1.call-done = bf16[1,3072,768]{2,1,0:T(8,128)(2,1)} async-done(((bf16[1,384,768]{2,1,0:T(8,128)(2,1)}), bf16[1,3072,768]{2,1,0:T(8,128)(2,1)}) %all-gather.47.cloned.1.call-update) | async-done | bytes 4718608 | tf_op jit(solution)/shard_map/all_gather | solution.py:51
  236.5 34.3 %all-gather.35.cloned.1.call-done = bf16[1,1024,768]{1,2,0:T(8,128)(2,1)} async-done(((bf16[1,128,768]{1,2,0:T(8,128)(2,1)}), bf16[1,1024,768]{1,2,0:T(8,128)(2,1)}) %all-gather.35.cloned.1.call-update) | async-done | bytes 1572880 | tf_op jit(solution)/shard_map/all_gather | solution.py:284
  277.1 38.2 %all-gather.33.cloned.1.call-done = bf16[1,1024,768]{1,2,0:T(8,128)(2,1)} async-done(((bf16[1,128,768]{1,2,0:T(8,128)(2,1)}), bf16[1,1024,768]{1,2,0:T(8,128)(2,1)}) %all-gather.33.cloned.1.call-update) | async-done | bytes 1572880 | tf_op jit(solution)/shard_map/all_gather | solution.py:285
  319.9 48.9 %all-gather.43.cloned.1.call-done = bf16[1,768,768]{2,1,0:T(8,128)(2,1)} async-done(((bf16[1,96,768]{2,1,0:T(8,128)(2,1)}), bf16[1,768,768]{2,1,0:T(8,128)(2,1)}) %all-gather.43.cloned.1.call-update) | async-done | bytes 1179664 | tf_op jit(solution)/shard_map/all_gather | solution.py:47
  371.5 65.2 %all-gather.49.cloned.1.call-done = bf16[1,768,2304]{2,1,0:T(8,128)(2,1)} async-done(((bf16[1,96,2304]{2,1,0:T(8,128)(2,1)}), bf16[1,768,2304]{2,1,0:T(8,128)(2,1)}) %all-gather.49.cloned.1.call-update) | async-done | bytes 3538960 | tf_op jit(solution)/shard_map/all_gather | solution.py:45
  443.6 39.7 %all-gather.51.cloned.1.call-done = bf16[1,768,768]{2,1,0:T(8,128)(2,1)} async-done(((bf16[1,96,768]{2,1,0:T(8,128)(2,1)}), bf16[1,768,768]{2,1,0:T(8,128)(2,1)}) %all-gather.51.cloned.1.call-update) | async-done | bytes 1179664 | tf_op jit(solution)/shard_map/all_gather | solution.py:47
  485.3 36.7 %all-gather.39.cloned.1.call-done = bf16[1,1024,768]{1,2,0:T(8,128)(2,1)} async-done(((bf16[1,128,768]{1,2,0:T(8,128)(2,1)}), bf16[1,1024,768]{1,2,0:T(8,128)(2,1)}) %all-gather.39.cloned.1.call-update) | async-done | bytes 1572880 | tf_op jit(solution)/shard_map/all_gather | solution.py:284
  528.4 38.1 %all-gather.37.cloned.1.call-done = bf16[1,1024,768]{1,2,0:T(8,128)(2,1)} async-done(((bf16[1,128,768]{1,2,0:T(8,128)(2,1)}), bf16[1,1024,768]{1,2,0:T(8,128)(2,1)}) %all-gather.37.cloned.1.call-update) | async-done | bytes 1572880 | tf_op jit(solution)/shard_map/all_gather | solution.py:285
  608.2 42.0 %all-gather.53.cloned.1.call-done = bf16[1,768,3072]{2,1,0:T(8,128)(2,1)} async-done(((bf16[1,96,3072]{2,1,0:T(8,128)(2,1)}), bf16[1,768,3072]{2,1,0:T(8,128)(2,1)}) %all-gather.53.cloned.1.call-update) | async-done | bytes 4718608 | tf_op jit(solution)/shard_map/all_gather | solution.py:49
  658.5 67.5 %all-gather.55.cloned.1.call-done = bf16[1,3072,768]{2,1,0:T(8,128)(2,1)} async-done(((bf16[1,384,768]{2,1,0:T(8,128)(2,1)}), bf16[1,3072,768]{2,1,0:T(8,128)(2,1)}) %all-gather.55.cloned.1.call-update) | async-done | bytes 4718608 | tf_op jit(solution)/shard_map/all_gather | solution.py:51
  772.5 44.4 %reduce-scatter.15.cloned.1.call-done = f32[1,128,768]{1,2,0:T(8,128)} async-done(((f32[1,1024,768]{1,2,0:T(8,128)}), f32[1,128,768]{1,2,0:T(8,128)}) %reduce-scatter.15.cloned.1.call-update) | async-done | bytes 393232 | tf_op jit(solution)/shard_map/reduce_scatter | solution.py:217
  883.3 43.2 %reduce-scatter.19.cloned.1.call-done = f32[1,128,768]{1,2,0:T(8,128)} async-done(((f32[1,1024,768]{1,2,0:T(8,128)}), f32[1,128,768]{1,2,0:T(8,128)}) %reduce-scatter.19.cloned.1.call-update) | async-done | bytes 393232 | tf_op jit(solution)/shard_map/reduce_scatter | solution.py:217
  935.5 69.2 %reduce-scatter.27.cloned.1.call-done = bf16[96,768]{1,0:T(8,128)(2,1)} async-done(((bf16[768,768]{1,0:T(8,128)(2,1)}), bf16[96,768]{1,0:T(8,128)(2,1)}) %reduce-scatter.27.cloned.1.call-update) | async-done | bytes 147472 | tf_op jit(solution)/shard_map/reduce_scatter | solution.py:81
  1004.7 91.4 %reduce-scatter.35.cloned.1.call-done = bf16[384,768]{1,0:T(8,128)(2,1)} async-done(((bf16[3072,768]{1,0:T(8,128)(2,1)}), bf16[384,768]{1,0:T(8,128)(2,1)}) %reduce-scatter.35.cloned.1.call-update) | async-done | bytes 589840 | tf_op jit(solution)/shard_map/reduce_scatter | solution.py:93
  1096.1 90.1 %reduce-scatter.31.cloned.1.call-done = bf16[96,3072]{1,0:T(8,128)(2,1)} async-done(((bf16[768,3072]{1,0:T(8,128)(2,1)}), bf16[96,3072]{1,0:T(8,128)(2,1)}) %reduce-scatter.31.cloned.1.call-update) | async-done | bytes 589840 | tf_op jit(solution)/shard_map/reduce_scatter | solution.py:87
  1186.2 73.9 %reduce-scatter.25.cloned.1.call-done = bf16[96,768]{1,0:T(8,128)(2,1)} async-done(((bf16[768,768]{1,0:T(8,128)(2,1)}), bf16[96,768]{1,0:T(8,128)(2,1)}) %reduce-scatter.25.cloned.1.call-update) | async-done | bytes 147472 | tf_op jit(solution)/shard_map/reduce_scatter | solution.py:81
  1260.1 84.6 %reduce-scatter.23.cloned.1.call-done = bf16[96,2304]{1,0:T(8,128)(2,1)} async-done(((bf16[768,2304]{1,0:T(8,128)(2,1)}), bf16[96,2304]{1,0:T(8,128)(2,1)}) %reduce-scatter.23.cloned.1.call-update) | async-done | bytes 442384 | tf_op jit(solution)/shard_map/reduce_scatter | solution.py:75
  1344.7 90.5 %reduce-scatter.33.cloned.1.call-done = bf16[384,768]{1,0:T(8,128)(2,1)} async-done(((bf16[3072,768]{1,0:T(8,128)(2,1)}), bf16[384,768]{1,0:T(8,128)(2,1)}) %reduce-scatter.33.cloned.1.call-update) | async-done | bytes 589840 | tf_op jit(solution)/shard_map/reduce_scatter | solution.py:93
  1435.3 90.3 %reduce-scatter.29.cloned.1.call-done = bf16[96,3072]{1,0:T(8,128)(2,1)} async-done(((bf16[768,3072]{1,0:T(8,128)(2,1)}), bf16[96,3072]{1,0:T(8,128)(2,1)}) %reduce-scatter.29.cloned.1.call-update) | async-done | bytes 589840 | tf_op jit(solution)/shard_map/reduce_scatter | solution.py:87
  1525.6 83.2 %reduce-scatter.21.cloned.1.call-done = bf16[96,2304]{1,0:T(8,128)(2,1)} async-done(((bf16[768,2304]{1,0:T(8,128)(2,1)}), bf16[96,2304]{1,0:T(8,128)(2,1)}) %reduce-scatter.21.cloned.1.call-update) | async-done | bytes 442384 | tf_op jit(solution)/shard_map/reduce_scatter | solution.py:75
  1627.0 35.2 %all-reduce.34 = (bf16[768]{0:T(1024)(128)(2,1)S(1)}, bf16[768]{0:T(1024)(128)(2,1)S(1)}, bf16[2304]{0:T(1024)(128)(2,1)S(1)}, bf16[2304]{0:T(1024)(128)(2,1)S(1...) all-reduce(bf16[768]{0:T(1024)(128)(2,1)} %copy-done.68, ...), channel_id=21, replica_groups=mesh['ctx'=8,'dp'=2,'fsdp'=8] {'fsdp'}, use_global_device_ids=true, to_apply=%add.21 | all-reduce | flops 16896 | bytes 67584
  1663.0 37.1 %all-reduce.32 = (bf16[1,288]{1,0:T(2,128)(2,1)S(1)}, bf16[1,288]{1,0:T(2,128)(2,1)S(1)}, bf16[1,96]{1,0:T(2,128)(2,1)S(1)}, bf16[1,96]{1,0:T(2,128)(2,1)S(1)}, ...) all-reduce(bf16[1,288]{1,0:T(2,128)(2,1)S(1)} %stack.158, ...), channel_id=1, replica_groups=mesh['ctx'=8,'dp'=2,'fsdp'=8] {'ctx','dp'}, use_global_device_ids=true, to_apply=%region_27.28 | all-reduce | flops 1920 | bytes 7680 | tf_op jit(solution)/shard_map/psum | solution.py:108
  1706.5 33.7 %all-reduce.38.cloned.1.call-done = (bf16[1,96,2304]{2,1,0:T(8,128)(2,1)}, bf16[1,96,2304]{2,1,0:T(8,128)(2,1)}, bf16[1,96,768]{2,1,0:T(8,128)(2,1)}, bf16[1,96,...) async-done(((bf16[1,96,2304]{2,1,0:T(8,128)(2,1)}, ...) | async-done | bytes 3538960 | tf_op jit(solution)/shard_map/psum | solution.py:107
  (408 shorter events, 353.4 us)
Async XLA Ops:
  9.5 147.4 %all-gather.45.cloned.1.call-start = ((), (), s32[]{:S(2)}) async-start(), calls=%async_computation.30 | async-start | bytes 5308416 | tf_op jit(solution)/shard_map/all_gather | solution.py:49
  10.7 222.7 %all-gather.47.cloned.1.call-start = ((), (), s32[]{:S(2)}) async-start(), calls=%async_computation.31 | async-start | bytes 5308416 | tf_op jit(solution)/shard_map/all_gather | solution.py:51
  12.3 258.6 %all-gather.35.cloned.1.call-start = ((), (), s32[]{:S(2)}) async-start(), calls=%async_computation.13 | async-start | bytes 1769472 | tf_op jit(solution)/shard_map/all_gather | solution.py:284
  84.0 231.3 %all-gather.33.cloned.1.call-start = ((), (), s32[]{:S(2)}) async-start(), calls=%async_computation.12 | async-start | bytes 1769472 | tf_op jit(solution)/shard_map/all_gather | solution.py:285
  84.8 284.0 %all-gather.43.cloned.1.call-start = ((), (), s32[]{:S(2)}) async-start(), calls=%async_computation.29 | async-start | bytes 1327104 | tf_op jit(solution)/shard_map/all_gather | solution.py:47
  85.7 351.0 %all-gather.49.cloned.1.call-start = ((), (), s32[]{:S(2)}) async-start(), calls=%async_computation.32 | async-start | bytes 3981312 | tf_op jit(solution)/shard_map/all_gather | solution.py:45
  86.4 396.9 %all-gather.51.cloned.1.call-start = ((), (), s32[]{:S(2)}) async-start(), calls=%async_computation.33 | async-start | bytes 1327104 | tf_op jit(solution)/shard_map/all_gather | solution.py:47
  87.2 434.9 %all-gather.39.cloned.1.call-start = ((), (), s32[]{:S(2)}) async-start(), calls=%async_computation.15 | async-start | bytes 1769472 | tf_op jit(solution)/shard_map/all_gather | solution.py:284
  440.6 125.9 %all-gather.37.cloned.1.call-start = ((), (), s32[]{:S(2)}) async-start(), calls=%async_computation.14 | async-start | bytes 1769472 | tf_op jit(solution)/shard_map/all_gather | solution.py:285
  441.4 208.7 %all-gather.53.cloned.1.call-start = ((), (), s32[]{:S(2)}) async-start(), calls=%async_computation.34 | async-start | bytes 5308416 | tf_op jit(solution)/shard_map/all_gather | solution.py:49
  442.2 283.9 %all-gather.55.cloned.1.call-start = ((), (), s32[]{:S(2)}) async-start(), calls=%async_computation.35 | async-start | bytes 5308416 | tf_op jit(solution)/shard_map/all_gather | solution.py:51
  442.8 325.9 %reduce-scatter.13.cloned.1.call-start = ((), (), s32[]{:S(2)}) async-start(), calls=%async_computation.16 | async-start | bytes 3538944 | tf_op jit(solution)/shard_map/reduce_scatter | solution.py:216
  575.7 241.2 %reduce-scatter.15.cloned.1.call-start = ((), (), s32[]{:S(2)}) async-start(), calls=%async_computation.17 | async-start | bytes 3538944 | tf_op jit(solution)/shard_map/reduce_scatter | solution.py:217
  580.9 300.5 %reduce-scatter.17.cloned.1.call-start = ((), (), s32[]{:S(2)}) async-start(), calls=%async_computation.18 | async-start | bytes 3538944 | tf_op jit(solution)/shard_map/reduce_scatter | solution.py:216
  832.8 93.7 %reduce-scatter.19.cloned.1.call-start = ((), (), s32[]{:S(2)}) async-start(), calls=%async_computation.19 | async-start | bytes 3538944 | tf_op jit(solution)/shard_map/reduce_scatter | solution.py:217
  838.8 165.9 %reduce-scatter.27.cloned.1.call-start = ((), (), s32[]{:S(2)}) async-start(), calls=%async_computation.23 | async-start | bytes 1327104 | tf_op jit(solution)/shard_map/reduce_scatter | solution.py:81
  845.6 250.5 %reduce-scatter.35.cloned.1.call-start = ((), (), s32[]{:S(2)}) async-start(), calls=%async_computation.27 | async-start | bytes 5308416 | tf_op jit(solution)/shard_map/reduce_scatter | solution.py:93
  850.6 335.6 %reduce-scatter.31.cloned.1.call-start = ((), (), s32[]{:S(2)}) async-start(), calls=%async_computation.25 | async-start | bytes 5308416 | tf_op jit(solution)/shard_map/reduce_scatter | solution.py:87
  856.3 403.8 %reduce-scatter.25.cloned.1.call-start = ((), (), s32[]{:S(2)}) async-start(), calls=%async_computation.22 | async-start | bytes 1327104 | tf_op jit(solution)/shard_map/reduce_scatter | solution.py:81
  858.8 486.0 %reduce-scatter.23.cloned.1.call-start = ((), (), s32[]{:S(2)}) async-start(), calls=%async_computation.21 | async-start | bytes 3981312 | tf_op jit(solution)/shard_map/reduce_scatter | solution.py:75
  862.8 572.5 %reduce-scatter.33.cloned.1.call-start = ((), (), s32[]{:S(2)}) async-start(), calls=%async_computation.26 | async-start | bytes 5308416 | tf_op jit(solution)/shard_map/reduce_scatter | solution.py:93
  867.6 658.0 %reduce-scatter.29.cloned.1.call-start = ((), (), s32[]{:S(2)}) async-start(), calls=%async_computation.24 | async-start | bytes 5308416 | tf_op jit(solution)/shard_map/reduce_scatter | solution.py:87
  877.9 731.0 %reduce-scatter.21.cloned.1.call-start = ((), (), s32[]{:S(2)}) async-start(), calls=%async_computation.20 | async-start | bytes 3981312 | tf_op jit(solution)/shard_map/reduce_scatter | solution.py:75
  932.3 808.0 %all-reduce.38.cloned.1.call-start = ((), (), s32[]{:S(2)}) async-start(), calls=%async_computation.36 | async-start | bytes 7077888 | tf_op jit(solution)/shard_map/psum | solution.py:107
  (95 other events, 3832.6 us)
Sparse Core Ops, SparseCore 0:
  10.9 69.1 all-gather.40
  83.0 73.8 all-gather.44
  159.7 73.6 all-gather.46
  272.9 42.4 all-gather.32
  317.5 51.3 all-gather.42
  371.1 65.5 all-gather.48
  439.0 44.2 all-gather.50
  484.9 37.1 all-gather.38
  524.1 42.4 all-gather.36
  569.4 80.7 all-gather.52
  652.3 73.6 all-gather.54
  728.5 40.1 reduce-scatter.12
  771.0 45.8 reduce-scatter.14
  832.9 45.8 reduce-scatter.16
  881.1 45.3 reduce-scatter.18
  930.6 74.0 reduce-scatter.26
  1008.5 87.6 reduce-scatter.34
  1100.0 86.1 reduce-scatter.30
  1189.7 70.3 reduce-scatter.24
  1264.0 80.7 reduce-scatter.22
  1348.7 86.5 reduce-scatter.32
  1439.2 86.3 reduce-scatter.28
  1529.3 79.4 reduce-scatter.20
  1612.0 128.2 all-reduce.37
  (1 shorter events, 35.4 us)
where the time goes:
time: 1760 us
  waiting for transfers between devices  1360 us (77%)
  blocking collectives  176 us (10%)
  matrix products  138 us (8%)
  other arithmetic  29.9 us (2%)
  local copies, waits for them, and re-layouts  28.1 us (2%)
  between operations  18.8 us (1%)
    reduce_scatter x2, waiting for transfers between devices, reduce_grads(): lax.psum_scatter(parts[6].astype(jnp.bfloat16), 'fsdp', scatter_dimension...  182 us
    reduce_scatter x2, waiting for transfers between devices, reduce_grads(): lax.psum_scatter(parts[4].astype(jnp.bfloat16), 'fsdp', scatter_dimension...  180 us
    reduce_scatter x2, waiting for transfers between devices, reduce_grads(): lax.psum_scatter(parts[0].astype(jnp.bfloat16), 'fsdp', scatter_dimension...  168 us
    reduce_scatter x2, waiting for transfers between devices, reduce_grads(): lax.psum_scatter(parts[2].astype(jnp.bfloat16), 'fsdp', scatter_dimension...  143 us
    all_gather x2, waiting for transfers between devices, gather_weights(): lax.all_gather(shards[6][index_layer], 'fsdp', axis=0, tiled=True)  136 us
    all_gather x2, waiting for transfers between devices, gather_weights(): lax.all_gather(shards[0][index_layer], 'fsdp', axis=0, tiled=True)  90.3 us
    all_gather x2, waiting for transfers between devices, gather_weights(): lax.all_gather(shards[2][index_layer], 'fsdp', axis=0, tiled=True)  88.6 us
    reduce_scatter x2, waiting for transfers between devices, layer_backward(): lax.psum_scatter(grad_value_all, 'ctx', scatter_dimension=1, tiled=True)  87.5 us
  transfers between devices with their start and end apart: 25, of which 24 were waited for; matrix products, arithmetic and copies ran while one was open for 9% of the time, Pallas kernels for 0%

commit v1 on v0

v1 whole, which is shorter than its diff:
```python
import functools

import jax
import jax.numpy as jnp
from jax import lax
from jax.experimental import pallas as pl
from jax.experimental.pallas import tpu as pltpu
from jax.sharding import PartitionSpec as P

MESH = pl.DeviceIdType.MESH
HEAD_DIM = 64
ROT = 16
LAYERS = 2
D = 768
FF = 3072
N = 8
TOK = 128
SEQ = 1024
HALF = 384
epsilon = 1e-05
BF = jnp.bfloat16
F32 = jnp.float32
ANY = pl.BlockSpec(memory_space=pl.ANY)


def dot(a, b, dims):
    return lax.dot_general(a, b, (dims, ((), ())), preferred_element_type=F32)


def meet(devices):
    barrier = pltpu.get_barrier_semaphore()
    for device in devices:
        pl.semaphore_signal(barrier, inc=1, device_id=device, device_id_type=MESH)
    pl.semaphore_wait(barrier, len(devices))


def push(src, dst, send, recv, device):
    copy = pltpu.make_async_remote_copy(
        src_ref=src, dst_ref=dst, send_sem=send, recv_sem=recv, device_id=device, device_id_type=MESH
    )
    copy.start()
    return copy


def others(axis, index):
    return [{axis: lax.rem(index + d, N)} for d in range(1, N)]


class Group:
    def __init__(self, axis):
        self.axis = axis
        index = lax.axis_index(axis)
        self.r, self.h = (index % 4, index // 4) if axis == "ctx" else (index // 2, index % 2)
        self.right = {axis: self.slot(1, 0)}
        self.left = {axis: self.slot(3, 0)}
        self.pair = {axis: self.slot(0, 1)}

    def slot(self, dr, dh):
        r, h = lax.rem(self.r + dr, 4), lax.rem(self.h + dh, 2)
        return h * 4 + r if self.axis == "ctx" else r * 2 + h

    def neighbours(self):
        return [self.right, self.left, self.pair]


GATHERS = 9


def gather_steps(group, own, at, cut, rows, send, recv):
    head, tail = pl.ds(0, cut), pl.ds(cut, rows - cut)

    def go(i, src, dst, device):
        return push(src, dst, send.at[i], recv.at[i], device)

    me, twin = group.slot(0, 0), group.slot(0, 1)
    c0 = go(0, own, at(me), group.right)
    c1 = go(1, own, at(me), group.left)
    c2 = go(2, own, at(me), group.pair)
    c0.wait_recv()
    behind = at(group.slot(3, 0)).at[head]
    c3 = go(3, behind, behind, group.right)
    c1.wait_recv()
    ahead = at(group.slot(1, 0)).at[tail]
    c4 = go(4, ahead, ahead, group.left)
    c2.wait_recv()
    c5 = go(5, at(twin), at(twin), group.right)
    c6 = go(6, at(twin), at(twin), group.left)
    c5.wait_recv()
    behind = at(group.slot(3, 1)).at[head]
    c7 = go(7, behind, behind, group.right)
    c6.wait_recv()
    ahead = at(group.slot(1, 1)).at[tail]
    c8 = go(8, ahead, ahead, group.left)
    for copy in (c3, c4, c7, c8):
        copy.wait_recv()
    for copy in (c0, c1, c2, c3, c4, c5, c6, c7, c8):
        copy.wait_send()


SCATTERS = 13


def scatter_scratch(rows, cut, width):
    return [
        pltpu.VMEM((2, cut, width), BF),
        pltpu.VMEM((2, rows - cut, width), BF),
        pltpu.VMEM((2, cut, width), BF),
        pltpu.VMEM((2, rows - cut, width), BF),
        pltpu.VMEM((2, rows, width), BF),
        pltpu.VMEM((2, rows, width), BF),
        pltpu.VMEM((rows, width), BF),
        pltpu.VMEM((rows, width), BF),
    ]


def scatter_steps(group, src, cut, rows, buffers, send, recv):
    in_right, in_left, st_left, st_right, from_right, from_left, st_pair, from_pair = buffers
    head, tail = pl.ds(0, cut), pl.ds(cut, rows - cut)
    copies = []

    def go(a, b, device):
        i = len(copies)
        copy = push(a, b, send.at[i], recv.at[i], device)
        copies.append(copy)
        return copy

    hs = (1, 0)
    far = []
    for n, h in enumerate(hs):
        block = src.at[group.slot(2, h)]
        far.append(
            (
                go(block.at[head], in_right.at[n], group.left),
                go(block.at[tail], in_left.at[n], group.right),
            )
        )
    near = []
    for n, h in enumerate(hs):
        near.append(
            [
                go(src.at[group.slot(3, h)].at[tail], from_right.at[n].at[tail], group.left),
                go(src.at[group.slot(1, h)].at[head], from_left.at[n].at[head], group.right),
            ]
        )
    for n, h in enumerate(hs):
        far[n][0].wait_recv()
        st_left[n] = (src[group.slot(3, h), head].astype(F32) + in_right[n].astype(F32)).astype(BF)
        near[n].append(go(st_left.at[n], from_right.at[n].at[head], group.left))
        far[n][1].wait_recv()
        st_right[n] = (src[group.slot(1, h), tail].astype(F32) + in_left[n].astype(F32)).astype(BF)
        near[n].append(go(st_right.at[n], from_left.at[n].at[tail], group.right))
    total = None
    for n, h in enumerate(hs):
        for copy in near[n]:
            copy.wait_recv()
        total = src[group.slot(0, h)].astype(F32) + from_right[n].astype(F32) + from_left[n].astype(F32)
        if n == 0:
            st_pair[...] = total.astype(BF)
            last = go(st_pair, from_pair, group.pair)
    last.wait_recv()
    total = total + from_pair[...].astype(F32)
    for copy in copies:
        copy.wait_send()
    return total


def sems(count):
    return [pltpu.SemaphoreType.DMA((count,)), pltpu.SemaphoreType.DMA((count,))]


def params(collective_id):
    return pltpu.CompilerParams(
        collective_id=collective_id, has_side_effects=True, vmem_limit_bytes=32 * 1024 * 1024
    )


def gather_kernel(src, dst, send, recv, own):
    group = Group("ctx")
    local = pltpu.make_async_copy(src, dst.at[group.slot(0, 0)], own)
    local.start()
    meet(group.neighbours())
    gather_steps(group, src, lambda slot: dst.at[slot], TOK // 2, TOK, send, recv)
    local.wait()


def gather_ctx(block, collective_id):
    return pl.pallas_call(
        gather_kernel,
        out_shape=jax.ShapeDtypeStruct((N,) + block.shape, block.dtype),
        in_specs=[ANY],
        out_specs=ANY,
        scratch_shapes=sems(GATHERS) + [pltpu.SemaphoreType.DMA],
        compiler_params=params(collective_id),
    )(block)


def scatter_kernel(src, dst, *rest):
    *buffers, send, recv = rest
    group = Group("ctx")
    meet(group.neighbours())
    dst[...] = scatter_steps(group, src, TOK // 2, TOK, buffers, send, recv)


def scatter_ctx(parts, collective_id):
    vmem = pl.BlockSpec(memory_space=pltpu.VMEM)
    return pl.pallas_call(
        scatter_kernel,
        out_shape=jax.ShapeDtypeStruct(parts.shape[1:], F32),
        in_specs=[vmem],
        out_specs=vmem,
        scratch_shapes=scatter_scratch(TOK, TOK // 2, D) + sems(SCATTERS),
        compiler_params=params(collective_id),
    )(parts)


PIECE = 64
W_LAYER = 96 + PIECE
W_ROWS = LAYERS * W_LAYER + 16


def weights_kernel(
    src, places, cols_all, pieces_all, places_all, held, mixed, got, send, recv, send_z, recv_z, own
):
    c, f, k = lax.axis_index("ctx"), lax.axis_index("fsdp"), lax.axis_index("dp")
    group = Group("fsdp")
    cs = others("ctx", c)
    core = {"dp": 1 - k}
    first = pltpu.make_async_copy(src.at[k], held.at[f], own.at[0])
    first.start()
    mark = pltpu.make_async_copy(places, places_all.at[c], own.at[1])
    mark.start()
    meet(group.neighbours() + cs + [core])
    copies = []

    def go(a, b, device):
        i = len(copies)
        copies.append(push(a, b, send.at[i], recv.at[i], device))
        return copies[-1]

    for peer in cs:
        go(places, places_all.at[c], peer)
    gather_steps(group, src.at[k], lambda slot: held.at[slot], 176, W_ROWS, send_z, recv_z)
    first.wait()
    low = lax.broadcasted_iota(jnp.int32, (16, HALF), 0) < 8
    for i in range(N):
        for layer in range(LAYERS):
            at, to = layer * W_LAYER + 96, layer * PIECE
            own_rows = held[i, pl.ds(at, 16)].astype(F32)
            shared = held[i // 2 * 2 + c // 4, pl.ds(at, 16)].astype(F32)
            mixed[i, pl.ds(to, 16)] = jnp.where(low, own_rows, shared).astype(BF)
            mixed[i, pl.ds(to + 16, 48)] = held[i, pl.ds(at + 16, 48)]
    turn = [go(mixed.at[peer["ctx"]], got.at[c], peer) for peer in cs]
    got[c] = mixed[c]
    cross = go(held, cols_all.at[k], core)
    keep = [pltpu.make_async_copy(held, cols_all.at[k], own.at[2])]
    keep[0].start()
    for copy in turn:
        copy.wait_recv()
    keep.append(pltpu.make_async_copy(got, pieces_all.at[k], own.at[3]))
    keep[1].start()
    last = go(got, pieces_all.at[k], core)
    for copy in copies[: N - 1] + [cross, last]:
        copy.wait_recv()
    for copy in copies:
        copy.wait_send()
    for copy in keep + [mark]:
        copy.wait()


def gather_weights(src, places, collective_id):
    return pl.pallas_call(
        weights_kernel,
        out_shape=(
            jax.ShapeDtypeStruct((2, N, W_ROWS, HALF), BF),
            jax.ShapeDtypeStruct((2, N, LAYERS * PIECE, HALF), BF),
            jax.ShapeDtypeStruct((N,) + places.shape, places.dtype),
        ),
        in_specs=[ANY] * 2,
        out_specs=[ANY] * 3,
        scratch_shapes=[
            pltpu.VMEM((N, W_ROWS, HALF), BF),
            pltpu.VMEM((N, LAYERS * PIECE, HALF), BF),
            pltpu.VMEM((N, LAYERS * PIECE, HALF), BF),
        ]
        + sems(2 * (N - 1) + 2)
        + sems(GATHERS)
        + [pltpu.SemaphoreType.DMA((4,))],
        compiler_params=params(collective_id),
    )(src, places)


ROWS_A = 112
ROWS = ROWS_A + PIECE
CUT = 96


def grads_kernel(src_a, src_b, out, mine_a, mine_b, their_a, their_b, got, blocks, total, *rest):
    *buffers, send, recv, send_z, recv_z, send_x, recv_x, own = rest
    c, k = lax.axis_index("ctx"), lax.axis_index("dp")
    core = {"dp": 1 - k}
    fsdp, ctx = Group("fsdp"), Group("ctx")
    cs = others("ctx", c)
    loads = [
        pltpu.make_async_copy(src_b.at[k], mine_b, own.at[0]),
        pltpu.make_async_copy(src_a.at[k], mine_a, own.at[1]),
    ]
    for copy in loads:
        copy.start()
    meet([core] + fsdp.neighbours() + cs)
    copies = []

    def go(a, b, device):
        i = len(copies)
        copies.append(push(a, b, send.at[i], recv.at[i], device))
        return copies[-1]

    first_b = go(src_b.at[1 - k], their_b, core)
    first_a = go(src_a.at[1 - k], their_a, core)
    loads[0].wait()
    first_b.wait_recv()
    for i in range(N):
        mine_b[i] = (mine_b[i].astype(F32) + their_b[i].astype(F32)).astype(BF)
    turn = [go(mine_b.at[peer["ctx"]], got.at[c], peer) for peer in cs]
    got[c] = mine_b[c]
    loads[1].wait()
    first_a.wait_recv()
    for i in range(N):
        blocks[i, pl.ds(0, ROWS_A)] = (mine_a[i].astype(F32) + their_a[i].astype(F32)).astype(BF)
    for copy in turn:
        copy.wait_recv()
    low = lax.broadcasted_iota(jnp.int32, (16, HALF), 0) < 8
    for i in range(N):
        rows = got[i, pl.ds(0, 16)].astype(F32)
        pair = got[i + 1 - 2 * (i % 2), pl.ds(0, 16)].astype(F32)
        blocks[i, pl.ds(ROWS_A, 16)] = jnp.where(low, rows, rows + pair).astype(BF)
        blocks[i, pl.ds(ROWS_A + 16, 48)] = got[i, pl.ds(16, 48)]
    total[...] = scatter_steps(fsdp, blocks, CUT, ROWS, buffers, send_z, recv_z).astype(BF)
    keep = pltpu.make_async_copy(total, out.at[k, c], own.at[2])
    keep.start()
    gather_steps(ctx, total, lambda slot: out.at[k, slot], CUT, ROWS, send_x, recv_x)
    keep.wait()
    go(out.at[k], out.at[k], core).wait_recv()
    for copy in copies:
        copy.wait_send()


def reduce_grads(src_a, src_b, collective_id):
    return pl.pallas_call(
        grads_kernel,
        out_shape=jax.ShapeDtypeStruct((2, N, ROWS, HALF), BF),
        in_specs=[ANY] * 2,
        out_specs=ANY,
        scratch_shapes=[
            pltpu.VMEM((N, ROWS_A, HALF), BF),
            pltpu.VMEM((N, PIECE, HALF), BF),
            pltpu.VMEM((N, ROWS_A, HALF), BF),
            pltpu.VMEM((N, PIECE, HALF), BF),
            pltpu.VMEM((N, PIECE, HALF), BF),
            pltpu.VMEM((N, ROWS, HALF), BF),
            pltpu.VMEM((ROWS, HALF), BF),
        ]
        + scatter_scratch(ROWS, CUT, HALF)
        + sems(2 + N - 1 + 1)
        + sems(SCATTERS)
        + sems(GATHERS)
        + [pltpu.SemaphoreType.DMA((3,))],
        compiler_params=params(collective_id),
    )(src_a, src_b)


def rotary_tables(places):
    half_rot = ROT // 2
    frequency = 10000.0 ** (-2.0 * jnp.arange(half_rot, dtype=F32) / ROT)
    angles = places.astype(F32)[:, None] * frequency
    cosine, sine = jnp.cos(angles), jnp.sin(angles)
    count = places.shape[0]
    rest = HEAD_DIM - ROT
    own = jnp.concatenate([cosine, cosine, jnp.ones((count, rest), F32)], axis=1)
    left = jnp.concatenate([jnp.zeros_like(sine), sine, jnp.zeros((count, rest), F32)], axis=1)
    right = jnp.concatenate([-sine, jnp.zeros_like(sine), jnp.zeros((count, rest), F32)], axis=1)
    return tuple(jnp.concatenate([t, t], axis=1) for t in (own, left, right))


def rotate(values, tables):
    own, left, right = tables
    return values * own + jnp.roll(values, 8, axis=1) * left + jnp.roll(values, -8, axis=1) * right


def rotate_back(grads, tables):
    own, left, right = tables
    return grads * own + jnp.roll(grads * left, -8, axis=1) + jnp.roll(grads * right, 8, axis=1)


def norm_part(stream, gain_vec, shift_vec):
    row_mean = jnp.mean(stream, axis=-1, keepdims=True)
    centred = stream - row_mean
    row_var = jnp.mean(centred * centred, axis=-1, keepdims=True)
    return centred * lax.rsqrt(row_var + epsilon) * gain_vec + shift_vec


def gelu_exact(values):
    return jax.nn.gelu(values, approximate=False)


def units_of(pair, s):
    first, second = pair[:, :HEAD_DIM], pair[:, HEAD_DIM:]
    shared = lax.dynamic_slice_in_dim(second, s * (SEQ // 2), SEQ // 2, axis=0)
    return jnp.stack([first[: SEQ // 2], first[SEQ // 2 :], shared])


def pair_of(units, s):
    first = jnp.concatenate([units[0], units[1]], axis=0)
    second = jnp.zeros_like(first)
    second = lax.dynamic_update_slice_in_dim(second, units[2], s * (SEQ // 2), axis=0)
    return jnp.concatenate([first, second], axis=1)


def wide_of(pair):
    first, second = pair[:, :HEAD_DIM], pair[:, HEAD_DIM:]
    return jnp.stack([first, first, second])


def body(
    inputs, positions, cotangent, w_qkv, b_qkv, w_out, b_out, w_up, b_up, w_down, b_down, ln_gain, ln_bias
):
    c = lax.axis_index("ctx")
    p, s = c // 2, lax.rem(c, 2)
    head_a, head_b = 3 * p + 2 * s, 3 * p + 1

    def heads_cols(w):
        grouped = w.reshape(w.shape[:-1] + (12, 3, HEAD_DIM))
        axis = grouped.ndim - 3
        both = jnp.concatenate(
            [
                lax.dynamic_slice_in_dim(grouped, head_a, 1, axis=axis),
                lax.dynamic_slice_in_dim(grouped, head_b, 1, axis=axis),
            ],
            axis=axis,
        )
        return jnp.swapaxes(both, axis, axis + 1).reshape(w.shape[:-1] + (HALF,))

    def hidden_cols(w):
        return lax.dynamic_slice_in_dim(w, c * HALF, HALF, axis=w.ndim - 1)

    f = lax.axis_index("fsdp")
    f_s = lax.rem(f, 2)

    def piece(w, start, count):
        return lax.dynamic_slice_in_dim(w, start, count, axis=1)

    cols = jnp.concatenate([heads_cols(w_qkv), hidden_cols(w_up)], axis=-1)
    first_rows = piece(w_out, jnp.where(f_s == 0, 0, 32) + 8 * c, 8)
    shared_rows = piece(w_out, jnp.where(f_s == 0, 64, -32) + 8 * jnp.where(f_s == 0, c % 4, c), 8)
    down_rows = piece(w_down, 48 * c, 48)
    by_layer = jnp.concatenate([cols, first_rows, shared_rows, down_rows], axis=1)
    vec = jnp.concatenate([b_qkv, b_out, b_up, b_down, ln_gain, ln_bias], axis=1).reshape(-1)
    vec = jnp.pad(vec, (0, 16 * D - vec.shape[0])).reshape(16, D)
    src = jnp.concatenate([by_layer.reshape(LAYERS * W_LAYER, D), vec], axis=0)
    src = jnp.stack([src[:, :HALF], src[:, HALF:]])
    places = jnp.broadcast_to(positions, (8, TOK))
    cols_all, pieces_all, places_all = gather_weights(src, places, 1)
    cols_all = jnp.concatenate([cols_all[0], cols_all[1]], axis=-1)
    pieces_all = jnp.concatenate([pieces_all[0], pieces_all[1]], axis=-1)
    w_cat = [cols_all[:, i * W_LAYER : i * W_LAYER + 96].reshape(D, D) for i in range(LAYERS)]
    w_mix = []
    for i in range(LAYERS):
        one = pieces_all[:, i * PIECE : (i + 1) * PIECE]
        w_mix.append(
            jnp.concatenate(
                [one[:, :8].reshape(64, D), one[:, 8:16].reshape(64, D), one[:, 16:].reshape(HALF, D)], axis=0
            )
        )
    vec_all = cols_all[:, LAYERS * W_LAYER :]
    vec_all = vec_all.reshape(N, -1)[:, : LAYERS * 1056].reshape(N, LAYERS, 1056)
    vec_all = jnp.swapaxes(vec_all, 0, 1).astype(F32)
    starts = (0, 288, 384, 768, 864, 960, 1056)
    b_qkv_all, b_out_all, b_up_all, b_down_all, gain_all, shift_all = (
        vec_all[:, :, starts[i] : starts[i + 1]].reshape(LAYERS, -1) for i in range(6)
    )
    b_cat = jnp.concatenate([heads_cols(b_qkv_all), hidden_cols(b_up_all)], axis=-1)
    b_sum = b_out_all + b_down_all
    places_row = places_all[:, 0, :].reshape(SEQ)
    tables = rotary_tables(places_row)
    causal = places_row[:, None] >= places_row[None, :]
    causal_shared = lax.dynamic_slice_in_dim(causal, s * (SEQ // 2), SEQ // 2, axis=0)
    causal_units = jnp.stack([causal[: SEQ // 2], causal[SEQ // 2 :], causal_shared])

    kept = []
    stream = inputs[0]
    for layer in range(LAYERS):
        normed = norm_part(stream, gain_all[layer], shift_all[layer]).astype(BF)
        normed = gather_ctx(normed, 2 + layer).reshape(SEQ, D)
        pre = dot(normed, w_cat[layer], ((1,), (0,))) + b_cat[layer]
        query = (rotate(pre[:, :128], tables) * HEAD_DIM ** (-0.5)).astype(BF)
        key = rotate(pre[:, 128:256], tables).astype(BF)
        value = pre[:, 256:384].astype(BF)
        hidden_pre = pre[:, HALF:]
        q_units, k_units, v_units = units_of(query, s), wide_of(key), wide_of(value)
        scores = jnp.einsum("uqd,ukd->uqk", q_units, k_units, preferred_element_type=F32)
        scores = jnp.where(causal_units, scores, -jnp.inf)
        row_max = jnp.max(scores, axis=-1, keepdims=True)
        expos = jnp.exp(scores - row_max)
        probs = expos / jnp.sum(expos, axis=-1, keepdims=True)
        probs_low = probs.astype(BF)
        attended = jnp.einsum("uqk,ukd->uqd", probs_low, v_units, preferred_element_type=F32).astype(BF)
        mixed = jnp.concatenate([pair_of(attended, s), gelu_exact(hidden_pre).astype(BF)], axis=1)
        branch = dot(mixed, w_mix[layer], ((1,), (0,))).astype(BF)
        kept.append((stream, normed, q_units, k_units, v_units, probs, probs_low, hidden_pre, mixed))
        stream = stream + (scatter_ctx(branch.reshape(N, TOK, D), 4 + layer) + b_sum[layer])

    grad = cotangent[0]
    done = [None] * LAYERS
    for layer in reversed(range(LAYERS)):
        stream_in, normed, q_units, k_units, v_units, probs, probs_low, hidden_pre, mixed = kept[layer]
        own_low = grad.astype(BF)
        grad_low = gather_ctx(own_low, 6 + layer).reshape(SEQ, D)
        grad_mix = dot(mixed, grad_low, ((0,), (0,)))
        grad_cat = dot(grad_low, w_mix[layer], ((1,), (1,)))
        grad_att = units_of(grad_cat[:, :128].astype(BF), s)
        grad_hidden = jax.vjp(gelu_exact, hidden_pre)[1](grad_cat[:, 128:])[0].astype(BF)
        grad_probs = jnp.einsum("uqd,ukd->uqk", grad_att, v_units, preferred_element_type=F32)
        grad_scores = (
            probs * (grad_probs - jnp.sum(grad_probs * probs, axis=-1, keepdims=True))
        ).astype(BF)
        grad_q = jnp.einsum("uqk,ukd->uqd", grad_scores, k_units, preferred_element_type=F32)
        grad_k = jnp.einsum("uqk,uqd->ukd", grad_scores, q_units, preferred_element_type=F32)
        grad_v = jnp.einsum("uqk,uqd->ukd", probs_low, grad_att, preferred_element_type=F32)
        grad_q = rotate_back(pair_of(grad_q, s) * HEAD_DIM ** (-0.5), tables)
        grad_k = rotate_back(jnp.concatenate([grad_k[0] + grad_k[1], grad_k[2]], axis=1), tables)
        grad_v = jnp.concatenate([grad_v[0] + grad_v[1], grad_v[2]], axis=1)
        grad_pre = jnp.concatenate(
            [grad_q.astype(BF), grad_k.astype(BF), grad_v.astype(BF), grad_hidden], axis=1
        )
        grad_normed = dot(grad_pre, w_cat[layer], ((1,), (1,))).astype(BF)
        grad_normed = scatter_ctx(grad_normed.reshape(N, TOK, D), 8 + layer)
        grad_w = dot(normed, grad_pre, ((0,), (0,)))
        grad_b = jnp.sum(grad_pre.astype(F32), axis=0)
        _, norm_back = jax.vjp(norm_part, stream_in, gain_all[layer], shift_all[layer])
        grad_stream, grad_gain, grad_shift = norm_back(grad_normed)
        grad_branch = jnp.sum(own_low.astype(F32), axis=0)
        grad = grad + grad_stream

        by_head = jnp.swapaxes(grad_b[:HALF].reshape(3, 2, HEAD_DIM), 0, 1)
        all_heads = jnp.zeros((12, 3, HEAD_DIM), F32)
        all_heads = lax.dynamic_update_slice_in_dim(all_heads, by_head[:1], head_a, axis=0)
        all_heads = lax.dynamic_update_slice_in_dim(all_heads, by_head[1:], head_b, axis=0)
        hidden_rows = jnp.where(jnp.arange(N)[:, None] == c, grad_b[HALF:][None], 0.0)
        vectors = jnp.concatenate(
            [
                all_heads.reshape(N, 288),
                grad_branch.reshape(N, 96),
                hidden_rows,
                grad_gain.reshape(N, 96),
                grad_shift.reshape(N, 96),
            ],
            axis=1,
        )
        vectors = jnp.pad(vectors, ((0, 0), (0, 16 * D - 960))).reshape(N, 16, D)
        part_a = jnp.concatenate([grad_w.reshape(N, 96, D).astype(BF), vectors.astype(BF)], axis=1)
        part_b = jnp.concatenate(
            [
                grad_mix[:64].reshape(N, 8, D),
                grad_mix[64:128].reshape(N, 8, D),
                grad_mix[128:].reshape(N, 48, D),
            ],
            axis=1,
        ).astype(BF)
        part_a, part_b = (jnp.stack([t[..., :HALF], t[..., HALF:]]) for t in (part_a, part_b))
        done[layer] = reduce_grads(part_a, part_b, 10 + layer)

    outs = []
    for layer in range(LAYERS):
        got = jnp.concatenate([done[layer][0], done[layer][1]], axis=-1).astype(F32)
        qkv = got[:, :96, :HALF].reshape(4, 2, 96, 3, 2, HEAD_DIM)
        shared = qkv[:, 0, :, :, 1] + qkv[:, 1, :, :, 1]
        qkv = jnp.stack([qkv[:, 0, :, :, 0], shared, qkv[:, 1, :, :, 0]], axis=1)
        g_qkv = jnp.transpose(qkv, (2, 0, 1, 3, 4)).reshape(96, 3 * D)
        g_up = jnp.transpose(got[:, :96, HALF:], (1, 0, 2)).reshape(96, FF)
        vectors = jnp.sum(got[:, 96:98], axis=0).reshape(-1)
        b_cut = (0, 288, 384, 768, 864, 960)
        g_b_qkv, g_branch, g_b_up, g_gain, g_shift = (vectors[b_cut[i] : b_cut[i + 1]] for i in range(5))
        g_down = got[:, ROWS_A + 16 :].reshape(HALF, D)
        first = got[:, ROWS_A : ROWS_A + 8].reshape(64, D)
        shared = got[:, ROWS_A + 8 : ROWS_A + 16].reshape(64, D)
        g_out = jnp.where(
            f_s == 0,
            jnp.concatenate([first, shared[:32]], axis=0),
            jnp.concatenate([shared[32:], first], axis=0),
        )
        outs.append((g_qkv, g_b_qkv, g_out, g_branch, g_up, g_b_up, g_down, g_branch, g_gain, g_shift))
    stacked = tuple(jnp.stack([outs[i][j] for i in range(LAYERS)]) for j in range(10))
    return (stream[None], grad[None]) + stacked


def solution(mesh):
    seqs = ("dp", "fsdp")
    whole = P(None, "fsdp", None)
    row = P(None, "fsdp")
    in_specs = (
        P(seqs, "ctx", None), P(seqs, "ctx"), P(seqs, "ctx", None),
        whole, row, whole, row, whole, row, whole, row, row, row,
    )
    out_specs = (
        P(seqs, "ctx", None), P(seqs, "ctx", None),
        whole, row, whole, row, whole, row, whole, row, row, row,
    )
    return jax.shard_map(body, mesh=mesh, in_specs=in_specs, out_specs=out_specs, check_vma=False)
```

time: 1760 us -> 455 us (0.26)
  waiting for transfers between devices: 1360 us -> 0 us
  Pallas kernels: 0 us -> 271 us
  blocking collectives: 176 us -> 0 us
  matrix products: 138 us -> 52 us
  local copies, waits for them, and re-layouts: 28.1 us -> 64.5 us
  other arithmetic: 29.9 us -> 56 us
    reduce_scatter x12 -> x0, waiting for transfers between devices: 793 us -> none  [the longest x2 182 us: reduce_grads(): lax.psum_scatter(parts[6].astype(jnp.bfloat16), 'fsdp', scatter_dimension...]
    all_gather x12 -> x0, waiting for transfers between devices: 533 us -> none  [the longest x2 136 us: gather_weights(): lax.all_gather(shards[6][index_layer], 'fsdp', axis=0, tiled=True)]
    pallas_call x0 -> x11, Pallas kernels: none -> 271 us  [the longest x2 108 us: reduce_grads(): pl.pallas_call(grads_kernel, out_shape=jax.ShapeDtypeStruct((2, N, ROWS,...]
    dot_general x34 -> x22, matrix products: 125 us -> 38.9 us  [the longest x12 23.7 us: dot(): return lax.dot_general(a, b, (dims, ((), ())), preferred_element_type=F32)]
    unnamed x2 -> x0, blocking collectives: 72.4 us -> none
    all_gather x3 -> x0, blocking collectives: 66.6 us -> none  [the longest x2 52.2 us: gather_weights(): lax.all_gather(shards[5][index_layer], 'fsdp', axis=0, tiled=True)]
    psum x1 -> x0, blocking collectives: 37.1 us -> none  [reduce_grads(): lax.psum(reduced[1].astype(jnp.bfloat16), ('ctx', 'dp')).astype(jnp.float32)]
    psum x1 -> x0, waiting for transfers between devices: 33.7 us -> none  [reduce_grads(): lax.psum(reduced[0].astype(jnp.bfloat16), ('ctx', 'dp')).astype(jnp.float32)]
  transfers between devices with their start and end apart: 25 -> 0, of which waited for: 24 -> 0; matrix products, arithmetic and copies ran while one was open for 9% -> 0% of each run, Pallas kernels for 0% -> 0%
where the time goes in v1:
time: 455 us; the launch traced here: 447 us
  Pallas kernels  271 us (60%)
  local copies, waits for them, and re-layouts  64.5 us (14%)
  other arithmetic  56 us (12%)
  matrix products  52 us (11%)
    pallas_call x2, Pallas kernels, reduce_grads(): pl.pallas_call(grads_kernel, out_shape=jax.ShapeDtypeStruct((2, N, ROWS,...  108 us
    pallas_call x4, Pallas kernels, gather_ctx(): pl.pallas_call(gather_kernel, out_shape=jax.ShapeDtypeStruct((N,) + block...  66.6 us
    pallas_call x4, Pallas kernels, scatter_ctx(): pl.pallas_call(scatter_kernel, out_shape=jax.ShapeDtypeStruct(parts.shape...  56 us
    pallas_call x1, Pallas kernels, gather_weights(): pl.pallas_call(weights_kernel, out_shape=(jax.ShapeDtypeStruct((2, N, W_R...  40.8 us
    unnamed x251, local copies, waits for them, and re-layouts  24.6 us
    dot_general x12, matrix products, dot(): return lax.dot_general(a, b, (dims, ((), ())), preferred_element_type=F32)  23.7 us
    sub x2, matrix products, body(): expos = jnp.exp(scores - row_max)  13.1 us
    another operation x8, other arithmetic, body(): jnp.stack([outs[i][j] for i in range(LAYERS)])  9.55 us

profile of v1, /device:TPU:1, one launch (start us, length us, event | category | flops | bytes accessed | tf_op | source)
XLA Modules:
  0.0 447.1 jit_solution(12361135149759312577)
XLA Ops:
  7.0 40.8 %shard_map.220 = (bf16[2,8,336,384]{3,2,1,0:T(8,128)(2,1)S(1)}, bf16[2,8,128,384]{3,2,1,0:T(8,128)(2,1)S(1)}, s32[8,8,128]{2,1,0:T(8,128)S(1)}) custom-call(bf16[2,336,384]{2,1,0:T(8,128)(2,1)S(1)} %pad_maximum_fusion.22.src, s32[8,128]{1,0:T(8,128)S(1)} %broadcast_in_dim.83.places), custom_call_target="tpu_custom_call" | custom-call | tf_op jit(solution)/shard_map/pallas_call | solution.py:271
  60.3 18.5 %shard_map.221 = bf16[8,128,768]{2,1,0:T(8,128)(2,1)S(1)} custom-call(bf16[128,768]{1,0:T(8,128)(2,1)S(1)} %add_convert_fusion.3.src), custom_call_target="tpu_custom_call" | custom-call | tf_op jit(solution)/shard_map/pallas_call | solution.py:187
  81.3 2.6 fusion.176
  85.6 4.8 %multiply_convert_fusion.3 = (bf16[1024,384]{0,1:T(8,128)(2,1)}, f32[1024,384]{0,1:T(8,128)}) fusion(f32[1024,768]{0,1:T(8,128)S(1)} %get-tuple-element.197), kind=kLoop, calls=%fused_computation.70 | loop fusion | flops 25559040 | bytes 3932160 | tf_op jit(solution)/shard_map/convert_element_type | solution.py:506
  99.4 6.6 %fusion.177 = (f32[3,512]{1,0:T(4,128)}, f32[3,512,1024]{2,1,0:T(8,128)}) fusion(bf16[1,1024,64]{1,2,0:T(8,128)(2,1)S(1)} %get-tuple-element.167, bf16[1,1024,64]{1,2,0:T(8,128)(2,1)S(1)} %get-tuple-element.166, bf16[1,512,64]{1,2,0:T(8,128)(2,1)S(1)} %dynamic-slice_bitcast_fusion.4, bf16[1,512,64]{1,2,0:T(8,128)(2,1)S(1)} %get-tuple-element.165, ...), kind=kOutput, calls=%fused_computation.437 | convolution fusion | flops 209781760 | bytes 8329216 | tf_op jit(solution)/shard_map/sub | solution.py:502
  106.1 4.1 fusion.40
  111.4 16.1 %shard_map.222 = f32[128,768]{1,0:T(8,128)S(1)} custom-call(bf16[8,128,768]{2,1,0:T(8,128)(2,1)S(1)} %bitcast.341), custom_call_target="tpu_custom_call" | custom-call | tf_op jit(solution)/shard_map/pallas_call | solution.py:206
  129.0 16.6 %shard_map.223 = bf16[8,128,768]{2,1,0:T(8,128)(2,1)S(1)} custom-call(bf16[128,768]{1,0:T(8,128)(2,1)S(1)} %add_convert_fusion.2.src), custom_call_target="tpu_custom_call" | custom-call | tf_op jit(solution)/shard_map/pallas_call | solution.py:187
  145.7 4.4 fusion.178
  155.7 6.4 %fusion.180 = (f32[3,512]{1,0:T(4,128)S(1)}, f32[3,512,1024]{2,1,0:T(8,128)}) fusion(bf16[1,1024,64]{1,2,0:T(8,128)(2,1)} %get-tuple-element.163, bf16[1,1024,64]{1,2,0:T(8,128)(2,1)} %get-tuple-element.162, bf16[1,512,64]{1,2,0:T(8,128)(2,1)} %dynamic-slice_bitcast_fusion.3, bf16[1,512,64]{1,2,0:T(8,128)(2,1)} %get-tuple-element.161, ...), kind=kOutput, calls=%fused_computation.440 | convolution fusion | flops 209781760 | bytes 8329216 | tf_op jit(solution)/shard_map/sub | solution.py:502
  163.9 15.2 %shard_map.225 = bf16[8,128,768]{2,1,0:T(8,128)(2,1)S(1)} custom-call(bf16[128,768]{1,0:T(8,128)(2,1)S(1)} %get-tuple-element.59.src), custom_call_target="tpu_custom_call" | custom-call | tf_op jit(solution)/shard_map/pallas_call | solution.py:187
  189.5 3.9 fusion.46
  194.9 13.2 %shard_map.226 = f32[128,768]{1,0:T(8,128)S(1)} custom-call(bf16[8,128,768]{2,1,0:T(8,128)(2,1)S(1)} %bitcast.339), custom_call_target="tpu_custom_call" | custom-call | tf_op jit(solution)/shard_map/pallas_call | solution.py:206
  212.2 13.5 %shard_map.224 = f32[128,768]{1,0:T(8,128)S(1)} custom-call(bf16[8,128,768]{2,1,0:T(8,128)(2,1)S(1)} %bitcast.338), custom_call_target="tpu_custom_call" | custom-call | tf_op jit(solution)/shard_map/pallas_call | solution.py:206
  227.5 16.3 %shard_map.227 = bf16[8,128,768]{2,1,0:T(8,128)(2,1)S(1)} custom-call(bf16[128,768]{1,0:T(8,128)(2,1)S(1)} %get-tuple-element.57.src), custom_call_target="tpu_custom_call" | custom-call | tf_op jit(solution)/shard_map/pallas_call | solution.py:187
  245.0 3.7 multiply_reduce_fusion
  261.4 13.2 %shard_map.228 = f32[128,768]{1,0:T(8,128)S(1)} custom-call(bf16[8,128,768]{2,1,0:T(8,128)(2,1)S(1)} %bitcast.340), custom_call_target="tpu_custom_call" | custom-call | tf_op jit(solution)/shard_map/pallas_call | solution.py:206
  278.7 4.4 fusion.37
  290.4 62.3 %shard_map.230 = bf16[2,8,176,384]{3,2,1,0:T(8,128)(2,1)S(1)} custom-call(bf16[2,8,112,384]{3,2,1,0:T(8,128)(2,1)S(1)} %pad_maximum_fusion.4.src_a, bf16[2,8,64,384]{3,2,1,0:T(8,128)(2,1)S(1)} %pad_maximum_fusion.15.src_b), custom_call_target="tpu_custom_call" | custom-call | tf_op jit(solution)/shard_map/pallas_call | solution.py:348
  355.3 2.9 copy.88
  362.7 3.3 fusion.34
  369.4 45.5 %shard_map.229 = bf16[2,8,176,384]{3,2,1,0:T(8,128)(2,1)S(1)} custom-call(bf16[2,8,112,384]{3,2,1,0:T(8,128)(2,1)S(1)} %pad_maximum_fusion.3.src_a, bf16[2,8,64,384]{3,2,1,0:T(8,128)(2,1)S(1)} %pad_maximum_fusion.13.src_b), custom_call_target="tpu_custom_call" | custom-call | tf_op jit(solution)/shard_map/pallas_call | solution.py:348
  422.4 3.1 copy.95
  439.0 3.3 pad_maximum_fusion.1
  (501 shorter events, 118.8 us)
Async XLA Ops:
  57.4 52.9 %copy-start.36 = (bf16[8,48,768]{2,1,0:T(8,128)(2,1)}, bf16[8,48,768]{2,1,0:T(8,128)(2,1)S(1)}, u32[]{:S(2)}) copy-start(bf16[8,48,768]{2,1,0:T(8,128)(2,1)S(1)} %get-tuple-element.113) | copy-start | bytes 1769476
  59.9 18.9 %copy-start.13 = (bf16[8,336,384]{2,1,0:T(8,128)(2,1)S(1)}, bf16[8,336,384]{2,1,0:T(8,128)(2,1)}, u32[]{:S(2)}) copy-start(bf16[8,336,384]{2,1,0:T(8,128)(2,1)} %copy-done.12) | copy-start | bytes 6193156
  60.0 21.4 %copy-start.94 = (f32[128]{0:T(128)}, f32[128]{0:T(128)S(1)}, u32[]{:S(2)}) copy-start(f32[128]{0:T(128)S(1)} %broadcast_multiply_fusion.1) | copy-start | bytes 1540
  60.2 21.2 %copy-start.105 = (f32[128]{0:T(128)}, f32[128]{0:T(128)S(1)}, u32[]{:S(2)}) copy-start(f32[128]{0:T(128)S(1)} %multiply_reduce_fusion.7) | copy-start | bytes 1540
  60.2 21.2 %copy-start.97 = (f32[128]{0:T(128)}, f32[128]{0:T(128)S(1)}, u32[]{:S(2)}) copy-start(f32[128]{0:T(128)S(1)} %fusion.134) | copy-start | bytes 1540
  111.4 17.2 %copy-start.87 = (f32[8,96]{1,0:T(8,128)S(1)}, f32[8,96]{1,0:T(8,128)}, u32[]{:S(2)}) copy-start(f32[8,96]{1,0:T(8,128)} %get-tuple-element.49) | copy-start | bytes 9220
  128.5 17.1 %copy-start.101 = (f32[768]{0:T(1024)S(1)}, f32[768]{0:T(1024)}, u32[]{:S(2)}) copy-start(f32[768]{0:T(1024)} %get-tuple-element.54) | copy-start | bytes 9220
  128.7 79.5 %copy-start.96 = (f32[128]{0:T(128)}, f32[128]{0:T(128)S(1)}, u32[]{:S(2)}) copy-start(f32[128]{0:T(128)S(1)} %broadcast_multiply_fusion) | copy-start | bytes 1540
  128.9 21.3 %copy-start.107 = (f32[128]{0:T(128)}, f32[128]{0:T(128)S(1)}, u32[]{:S(2)}) copy-start(f32[128]{0:T(128)S(1)} %multiply_reduce_fusion.6) | copy-start | bytes 1540
  128.9 21.2 %copy-start.99 = (f32[128]{0:T(128)}, f32[128]{0:T(128)S(1)}, u32[]{:S(2)}) copy-start(f32[128]{0:T(128)S(1)} %fusion.135) | copy-start | bytes 1540
  162.1 19.4 %copy-start.89 = (f32[3,512]{1,0:T(4,128)}, f32[3,512]{1,0:T(4,128)S(1)}, u32[]{:S(2)}) copy-start(f32[3,512]{1,0:T(4,128)S(1)} %get-tuple-element.204) | copy-start | bytes 18436
  162.1 16.9 %copy-start.49 = (bf16[8,48,768]{2,1,0:T(8,128)(2,1)S(1)}, bf16[8,48,768]{2,1,0:T(8,128)(2,1)}, u32[]{:S(2)}) copy-start(bf16[8,48,768]{2,1,0:T(8,128)(2,1)} %get-tuple-element.112) | copy-start | bytes 1769476
  162.2 16.9 %copy-start.77 = (bf16[64,768]{1,0:T(8,128)(2,1)S(1)}, bf16[64,768]{1,0:T(8,128)(2,1)}, u32[]{:S(2)}) copy-start(bf16[64,768]{1,0:T(8,128)(2,1)} %get-tuple-element.108) | copy-start | bytes 294916
  162.2 16.9 %copy-start.78 = (bf16[64,768]{1,0:T(8,128)(2,1)S(1)}, bf16[64,768]{1,0:T(8,128)(2,1)}, u32[]{:S(2)}) copy-start(bf16[64,768]{1,0:T(8,128)(2,1)} %get-tuple-element.111) | copy-start | bytes 294916
  163.9 16.4 %copy-start.30 = (f32[3,512,1024]{2,1,0:T(8,128)S(1)}, f32[3,512,1024]{2,1,0:T(8,128)}, u32[]{:S(2)}) copy-start(f32[3,512,1024]{2,1,0:T(8,128)} %get-tuple-element.205) | copy-start | bytes 18874372
  194.9 14.0 %copy-start.108 = (f32[128]{0:T(128)S(1)}, f32[128]{0:T(128)}, u32[]{:S(2)}) copy-start(f32[128]{0:T(128)} %copy-done.107) | copy-start | bytes 1540
  227.3 16.5 %copy-start.37 = (bf16[8,48,768]{2,1,0:T(8,128)(2,1)S(1)}, bf16[8,48,768]{2,1,0:T(8,128)(2,1)}, u32[]{:S(2)}) copy-start(bf16[8,48,768]{2,1,0:T(8,128)(2,1)} %copy-done.36) | copy-start | bytes 1769476
  227.3 16.5 %copy-start.52 = (bf16[64,768]{1,0:T(8,128)(2,1)S(1)}, bf16[64,768]{1,0:T(8,128)(2,1)}, u32[]{:S(2)}) copy-start(bf16[64,768]{1,0:T(8,128)(2,1)} %get-tuple-element.109) | copy-start | bytes 294916
  227.3 16.5 %copy-start.54 = (bf16[64,768]{1,0:T(8,128)(2,1)S(1)}, bf16[64,768]{1,0:T(8,128)(2,1)}, u32[]{:S(2)}) copy-start(bf16[64,768]{1,0:T(8,128)(2,1)} %get-tuple-element.110) | copy-start | bytes 294916
  261.4 13.3 %copy-start.95 = (f32[128]{0:T(128)S(1)}, f32[128]{0:T(128)}, u32[]{:S(2)}) copy-start(f32[128]{0:T(128)} %copy-done.94) | copy-start | bytes 1540
  261.4 13.3 %copy-start.98 = (f32[128]{0:T(128)S(1)}, f32[128]{0:T(128)}, u32[]{:S(2)}) copy-start(f32[128]{0:T(128)} %copy-done.97) | copy-start | bytes 1540
  261.4 13.5 %copy-start.106 = (f32[128]{0:T(128)S(1)}, f32[128]{0:T(128)}, u32[]{:S(2)}) copy-start(f32[128]{0:T(128)} %copy-done.105) | copy-start | bytes 1540
  261.4 13.8 %copy-start.35 = (f32[1,128,768]{2,1,0:T(8,128)S(1)}, f32[1,128,768]{2,1,0:T(8,128)}, u32[]{:S(2)}) copy-start(f32[1,128,768]{2,1,0:T(8,128)} %param.15) | copy-start | bytes 1179652
  429.5 16.8 %copy-start.102 = (f32[2,96]{1,0:T(2,128)}, f32[2,96]{1,0:T(2,128)S(1)}, u32[]{:S(2)}) copy-start(f32[2,96]{1,0:T(2,128)S(1)} %get-tuple-element.237) | copy-start | bytes 2308
  (92 other events, 191.1 us)

commit v2 on v1

v2 whole, which is shorter than its diff:
```python
import functools

import jax
import jax.numpy as jnp
from jax import lax
from jax.experimental import pallas as pl
from jax.experimental.pallas import tpu as pltpu
from jax.sharding import PartitionSpec as P

MESH = pl.DeviceIdType.MESH
HEAD_DIM = 64
ROT = 16
LAYERS = 2
D = 768
FF = 3072
N = 8
TOK = 128
SEQ = 1024
HALF = 384
epsilon = 1e-05
BF = jnp.bfloat16
F32 = jnp.float32
ANY = pl.BlockSpec(memory_space=pl.ANY)


def dot(a, b, dims):
    return lax.dot_general(a, b, (dims, ((), ())), preferred_element_type=F32)


def meet(devices):
    barrier = pltpu.get_barrier_semaphore()
    for device in devices:
        pl.semaphore_signal(barrier, inc=1, device_id=device, device_id_type=MESH)
    pl.semaphore_wait(barrier, len(devices))


def push(src, dst, send, recv, device):
    copy = pltpu.make_async_remote_copy(
        src_ref=src, dst_ref=dst, send_sem=send, recv_sem=recv, device_id=device, device_id_type=MESH
    )
    copy.start()
    return copy


def others(axis, index):
    return [{axis: lax.rem(index + d, N)} for d in range(1, N)]


class Group:
    def __init__(self, axis):
        self.axis = axis
        index = lax.axis_index(axis)
        self.r, self.h = (index % 4, index // 4) if axis == "ctx" else (index // 2, index % 2)
        self.right = {axis: self.slot(1, 0)}
        self.left = {axis: self.slot(3, 0)}
        self.pair = {axis: self.slot(0, 1)}

    def slot(self, dr, dh):
        r, h = lax.rem(self.r + dr, 4), lax.rem(self.h + dh, 2)
        return h * 4 + r if self.axis == "ctx" else r * 2 + h

    def neighbours(self):
        return [self.right, self.left, self.pair]


class Lane:
    def __init__(self, sems):
        self.send, self.recv = sems
        self.copies = []

    def go(self, src, dst, device):
        i = len(self.copies)
        self.copies.append(push(src, dst, self.send.at[i], self.recv.at[i], device))
        return self.copies[-1]

    def finish(self):
        for copy in self.copies:
            copy.wait_send()


def run(*steps):
    live = list(steps)
    while live:
        for one in list(live):
            try:
                next(one)
            except StopIteration:
                live.remove(one)


GATHERS = 8


def gather_steps(lane, group, own, at, cut, rows):
    head, tail = pl.ds(0, cut), pl.ds(cut, rows - cut)
    go = lane.go
    me, twin, far = group.slot(0, 0), group.slot(0, 1), group.slot(2, 0)
    c0 = go(own, at(me), group.right)
    c1 = go(own, at(me), group.left)
    c2 = go(own, at(me), group.pair)
    yield
    c0.wait_recv()
    behind = at(group.slot(3, 0)).at[head]
    c3 = go(behind, behind, group.right)
    yield
    c1.wait_recv()
    ahead = at(group.slot(1, 0)).at[tail]
    c4 = go(ahead, ahead, group.left)
    yield
    c2.wait_recv()
    c5 = go(at(twin), at(twin), group.right)
    c6 = go(at(twin), at(twin), group.left)
    yield
    c3.wait_recv()
    yield
    c4.wait_recv()
    c7 = go(at(far), at(far), group.pair)
    for copy in (c5, c6, c7):
        yield
        copy.wait_recv()


SCATTERS = 11


def scatter_scratch(rows, cut, width):
    return [
        pltpu.VMEM((rows, width), BF),
        pltpu.VMEM((rows, width), BF),
        pltpu.VMEM((cut, width), BF),
        pltpu.VMEM((rows - cut, width), BF),
        pltpu.VMEM((cut, width), BF),
        pltpu.VMEM((rows - cut, width), BF),
        pltpu.VMEM((2, rows, width), BF),
        pltpu.VMEM((2, rows, width), BF),
        pltpu.VMEM((rows, width), BF),
        pltpu.VMEM((rows, width), BF),
    ]


SCRATCHES = 10


def scatter_steps(lane, group, src, cut, rows, buffers, take):
    in_far, st_far, in_right, in_left, st_left, st_right, from_right, from_left, st_pair, from_pair = buffers
    head, tail = pl.ds(0, cut), pl.ds(cut, rows - cut)
    go = lane.go
    opposite = go(src.at[group.slot(2, 1)], in_far, group.pair)
    beside = [
        go(src.at[group.slot(3, 1)], from_right.at[0], group.left),
        go(src.at[group.slot(1, 1)], from_left.at[0], group.right),
    ]
    near = [
        go(src.at[group.slot(3, 0)].at[tail], from_right.at[1].at[tail], group.left),
        go(src.at[group.slot(1, 0)].at[head], from_left.at[1].at[head], group.right),
    ]
    yield
    opposite.wait_recv()
    st_far[...] = (src[group.slot(2, 0)].astype(F32) + in_far[...].astype(F32)).astype(BF)
    far_left = go(st_far.at[head], in_right, group.left)
    far_right = go(st_far.at[tail], in_left, group.right)
    for copy in beside:
        yield
        copy.wait_recv()
    total = src[group.slot(0, 1)].astype(F32) + from_right[0].astype(F32) + from_left[0].astype(F32)
    st_pair[...] = total.astype(BF)
    last = go(st_pair, from_pair, group.pair)
    yield
    far_left.wait_recv()
    st_left[...] = (src[group.slot(3, 0), head].astype(F32) + in_right[...].astype(F32)).astype(BF)
    near.append(go(st_left, from_right.at[1].at[head], group.left))
    yield
    far_right.wait_recv()
    st_right[...] = (src[group.slot(1, 0), tail].astype(F32) + in_left[...].astype(F32)).astype(BF)
    near.append(go(st_right, from_left.at[1].at[tail], group.right))
    for copy in near + [last]:
        yield
        copy.wait_recv()
    total = src[group.slot(0, 0)].astype(F32) + from_right[1].astype(F32) + from_left[1].astype(F32)
    take(total + from_pair[...].astype(F32))


def sems(count):
    return [pltpu.SemaphoreType.DMA((count,)), pltpu.SemaphoreType.DMA((count,))]


def params(collective_id):
    return pltpu.CompilerParams(
        collective_id=collective_id, has_side_effects=True, vmem_limit_bytes=32 * 1024 * 1024
    )


def normalize(stream):
    mean = jnp.mean(stream, axis=-1, keepdims=True)
    centred = stream - mean
    scale = lax.rsqrt(jnp.mean(centred * centred, axis=-1, keepdims=True) + epsilon)
    return centred * scale, scale


def norm_back(stream, grad_normed, gain):
    unit, scale = normalize(stream)
    grad_unit = grad_normed * gain
    first = jnp.mean(grad_unit, axis=-1, keepdims=True)
    second = jnp.mean(grad_unit * unit, axis=-1, keepdims=True)
    grad_gain = jnp.sum(grad_normed * unit, axis=0, keepdims=True)
    grad_shift = jnp.sum(grad_normed, axis=0, keepdims=True)
    return scale * (grad_unit - first - unit * second), grad_gain, grad_shift


PIECE = 64
ROWS = 96 + PIECE
CUT = 80
W_FIRST = ROWS + 16
W_CUT = 96
VMEM = pl.BlockSpec(memory_space=pltpu.VMEM)


def shard_scratch(rows):
    return [
        pltpu.VMEM((N, rows, HALF), BF),
        pltpu.VMEM((N, PIECE, HALF), BF),
        pltpu.VMEM((N, PIECE, HALF), BF),
    ]


SHARD_LANE = N - 1 + 3


def shard_steps(lane, lane_z, fsdp, cs, core, src, cut, rows, scratch, outs, own, kept):
    held, mixed, got = scratch
    c, k = lax.axis_index("ctx"), lax.axis_index("dp")
    first = pltpu.make_async_copy(src.at[k], held.at[fsdp.slot(0, 0)], own.at[0])
    first.start()
    yield from gather_steps(lane_z, fsdp, src.at[k], lambda slot: held.at[slot], cut, rows)
    first.wait()
    low = lax.broadcasted_iota(jnp.int32, (16, HALF), 0) < 8
    for i in range(N):
        own_rows = held[i, pl.ds(96, 16)].astype(F32)
        shared = held[i // 2 * 2 + c // 4, pl.ds(96, 16)].astype(F32)
        mixed[i, pl.ds(0, 16)] = jnp.where(low, own_rows, shared).astype(BF)
        mixed[i, pl.ds(16, 48)] = held[i, pl.ds(112, 48)]
    turn = [lane.go(mixed.at[peer["ctx"]], got.at[c], peer) for peer in cs]
    got[c] = mixed[c]
    cross = []

    def share(part, out, sem):
        cross.append(lane.go(part, out.at[k], core))
        keep = pltpu.make_async_copy(part, out.at[k], sem)
        keep.start()
        kept.append(keep)

    share(held.at[:, pl.ds(0, 96)], outs[0], own.at[1])
    if len(outs) > 2:
        share(held.at[:, pl.ds(ROWS, 16)], outs[2], own.at[2])
    for copy in turn:
        yield
        copy.wait_recv()
    share(got, outs[1], own.at[3])
    for copy in cross:
        yield
        copy.wait_recv()


COLS_SHAPE = jax.ShapeDtypeStruct((2, N, 96, HALF), BF)
PIECES_SHAPE = jax.ShapeDtypeStruct((2, N, PIECE, HALF), BF)


def weights_kernel(
    src, places, x, cot, cols_all, pieces_all, vec_all, places_all, unit_all, low_all, *rest
):
    scratch, unit, low_g, rest = rest[:3], rest[3], rest[4], rest[5:]
    lane, lane_z, lane_m, lane_u, lane_g = (Lane(rest[2 * i : 2 * i + 2]) for i in range(5))
    own, keeps = rest[10], rest[11]
    c = lax.axis_index("ctx")
    fsdp, ctx = Group("fsdp"), Group("ctx")
    cs = others("ctx", c)
    core = {"dp": 1 - lax.axis_index("dp")}
    mark = pltpu.make_async_copy(places, places_all.at[c], keeps.at[0])
    mark.start()
    meet(fsdp.neighbours() + cs + [core])
    kept = [mark]
    marks = [lane_m.go(places, places_all.at[c], peer) for peer in cs]

    def tokens():
        unit[...] = normalize(x[...])[0].astype(BF)
        low_g[...] = cot[...].astype(BF)
        keep = pltpu.make_async_copy(unit, unit_all.at[c], keeps.at[1])
        keep.start()
        kept.append(keep)
        yield from gather_steps(lane_u, ctx, unit, lambda slot: unit_all.at[slot], TOK // 2, TOK)
        keep = pltpu.make_async_copy(low_g, low_all.at[c], keeps.at[2])
        keep.start()
        kept.append(keep)
        yield from gather_steps(lane_g, ctx, low_g, lambda slot: low_all.at[slot], TOK // 2, TOK)

    outs = (cols_all, pieces_all, vec_all)
    run(
        shard_steps(lane, lane_z, fsdp, cs, core, src, W_CUT, W_FIRST, scratch, outs, own, kept),
        tokens(),
    )
    for copy in marks:
        copy.wait_recv()
    for each in (lane, lane_z, lane_m, lane_u, lane_g):
        each.finish()
    for copy in kept:
        copy.wait()


def gather_weights(src, places, x, cot, collective_id):
    tokens = jax.ShapeDtypeStruct((N, TOK, D), BF)
    return pl.pallas_call(
        weights_kernel,
        out_shape=(
            COLS_SHAPE,
            PIECES_SHAPE,
            jax.ShapeDtypeStruct((2, N, 16, HALF), BF),
            jax.ShapeDtypeStruct((N,) + places.shape, places.dtype),
            tokens,
            tokens,
        ),
        in_specs=[ANY] * 2 + [VMEM] * 2,
        out_specs=[ANY] * 6,
        scratch_shapes=shard_scratch(W_FIRST)
        + [pltpu.VMEM((TOK, D), BF), pltpu.VMEM((TOK, D), BF)]
        + sems(SHARD_LANE)
        + sems(GATHERS)
        + sems(N - 1)
        + sems(GATHERS)
        + sems(GATHERS)
        + [pltpu.SemaphoreType.DMA((4,)), pltpu.SemaphoreType.DMA((3,))],
        compiler_params=params(collective_id),
    )(src, places, x, cot)


def between_kernel(parts, x, bias, src, x_next, unit_all, cols_all, pieces_all, *rest):
    scratch, unit, rest = rest[:3], rest[3], rest[4:]
    buffers, rest = rest[:SCRATCHES], rest[SCRATCHES:]
    lane, lane_u, lane_w, lane_z = (Lane(rest[2 * i : 2 * i + 2]) for i in range(4))
    own, keeps = rest[8], rest[9]
    ctx, fsdp = Group("ctx"), Group("fsdp")
    cs = others("ctx", lax.axis_index("ctx"))
    core = {"dp": 1 - lax.axis_index("dp")}
    meet(fsdp.neighbours() + cs + [core])
    kept = []

    def tokens():
        def take(total):
            x_next[...] = x[...] + (total + bias[...])

        yield from scatter_steps(lane, ctx, parts, TOK // 2, TOK, buffers, take)
        unit[...] = normalize(x_next[...])[0].astype(BF)
        keep = pltpu.make_async_copy(unit, unit_all.at[ctx.slot(0, 0)], keeps)
        keep.start()
        kept.append(keep)
        yield from gather_steps(lane_u, ctx, unit, lambda slot: unit_all.at[slot], TOK // 2, TOK)

    outs = (cols_all, pieces_all)
    run(
        tokens(),
        shard_steps(lane_w, lane_z, fsdp, cs, core, src, CUT, ROWS, scratch, outs, own, kept),
    )
    for each in (lane, lane_u, lane_w, lane_z):
        each.finish()
    for copy in kept:
        copy.wait()


def between(parts, x, bias, src, collective_id):
    return pl.pallas_call(
        between_kernel,
        out_shape=(
            jax.ShapeDtypeStruct((TOK, D), F32),
            jax.ShapeDtypeStruct((N, TOK, D), BF),
            COLS_SHAPE,
            PIECES_SHAPE,
        ),
        in_specs=[VMEM] * 3 + [ANY],
        out_specs=(VMEM, ANY, ANY, ANY),
        scratch_shapes=shard_scratch(ROWS)
        + [pltpu.VMEM((TOK, D), BF)]
        + scatter_scratch(TOK, TOK // 2, D)
        + sems(SCATTERS)
        + sems(GATHERS)
        + sems(SHARD_LANE)
        + sems(GATHERS)
        + [pltpu.SemaphoreType.DMA((4,)), pltpu.SemaphoreType.DMA],
        compiler_params=params(collective_id),
    )(parts, x, bias, src)


def grads_scratch():
    return [
        pltpu.VMEM((N, 96, HALF), BF),
        pltpu.VMEM((N, PIECE, HALF), BF),
        pltpu.VMEM((N, 96, HALF), BF),
        pltpu.VMEM((N, PIECE, HALF), BF),
        pltpu.VMEM((N, PIECE, HALF), BF),
        pltpu.VMEM((N, ROWS, HALF), BF),
    ] + scatter_scratch(ROWS, CUT, HALF)


GRADS = 6 + SCRATCHES


def grads_steps(lane, lane_z, fsdp, cs, core, src_a, src_b, scratch, own, take):
    mine_a, mine_b, their_a, their_b, got, blocks = scratch[:6]
    c, k = lax.axis_index("ctx"), lax.axis_index("dp")
    loads = [
        pltpu.make_async_copy(src_b.at[k], mine_b, own.at[0]),
        pltpu.make_async_copy(src_a.at[k], mine_a, own.at[1]),
    ]
    for copy in loads:
        copy.start()
    first_b = lane.go(src_b.at[1 - k], their_b, core)
    first_a = lane.go(src_a.at[1 - k], their_a, core)
    yield
    loads[0].wait()
    first_b.wait_recv()
    for i in range(N):
        mine_b[i] = (mine_b[i].astype(F32) + their_b[i].astype(F32)).astype(BF)
    turn = [lane.go(mine_b.at[peer["ctx"]], got.at[c], peer) for peer in cs]
    got[c] = mine_b[c]
    yield
    loads[1].wait()
    first_a.wait_recv()
    for i in range(N):
        blocks[i, pl.ds(0, 96)] = (mine_a[i].astype(F32) + their_a[i].astype(F32)).astype(BF)
    for copy in turn:
        yield
        copy.wait_recv()
    low = lax.broadcasted_iota(jnp.int32, (16, HALF), 0) < 8
    for i in range(N):
        rows = got[i, pl.ds(0, 16)].astype(F32)
        pair = got[i + 1 - 2 * (i % 2), pl.ds(0, 16)].astype(F32)
        blocks[i, pl.ds(96, 16)] = jnp.where(low, rows, rows + pair).astype(BF)
        blocks[i, pl.ds(112, 48)] = got[i, pl.ds(16, 48)]
    yield from scatter_steps(lane_z, fsdp, blocks, CUT, ROWS, scratch[6:], take)


def turn_kernel(
    parts, x, grad, gain, src_a, src_b, grad_next, low_all, vecs, share, low_g, *rest
):
    buffers, rest = rest[:SCRATCHES], rest[SCRATCHES:]
    scratch, rest = rest[:GRADS], rest[GRADS:]
    lane, lane_g, lane_w, lane_z = (Lane(rest[2 * i : 2 * i + 2]) for i in range(4))
    own, keep_sem = rest[8], rest[9]
    ctx, fsdp = Group("ctx"), Group("fsdp")
    cs = others("ctx", lax.axis_index("ctx"))
    core = {"dp": 1 - lax.axis_index("dp")}
    meet(cs + fsdp.neighbours() + [core])
    kept = []

    def tokens():
        def take(total):
            back, grad_gain, grad_shift = norm_back(x[...], total, gain[...])
            grad_next[...] = grad[...] + back
            rounded = grad[...].astype(BF).astype(F32)
            vecs[pl.ds(0, 1)] = jnp.sum(rounded, axis=0, keepdims=True)
            vecs[pl.ds(1, 1)] = grad_gain
            vecs[pl.ds(2, 1)] = grad_shift
            vecs[pl.ds(3, 5)] = jnp.zeros((5, D), F32)

        yield from scatter_steps(lane, ctx, parts, TOK // 2, TOK, buffers, take)
        low_g[...] = grad_next[...].astype(BF)
        keep = pltpu.make_async_copy(low_g, low_all.at[ctx.slot(0, 0)], keep_sem)
        keep.start()
        kept.append(keep)
        yield from gather_steps(lane_g, ctx, low_g, lambda slot: low_all.at[slot], TOK // 2, TOK)

    def weights():
        def take(total):
            share[...] = total.astype(BF)

        yield from grads_steps(lane_w, lane_z, fsdp, cs, core, src_a, src_b, scratch, own, take)

    run(tokens(), weights())
    for each in (lane, lane_g, lane_w, lane_z):
        each.finish()
    for copy in kept:
        copy.wait()


def turn(parts, x, grad, gain, src_a, src_b, collective_id):
    return pl.pallas_call(
        turn_kernel,
        out_shape=(
            jax.ShapeDtypeStruct((TOK, D), F32),
            jax.ShapeDtypeStruct((N, TOK, D), BF),
            jax.ShapeDtypeStruct((8, D), F32),
            jax.ShapeDtypeStruct((ROWS, HALF), BF),
        ),
        in_specs=[VMEM] * 4 + [ANY] * 2,
        out_specs=(VMEM, ANY, VMEM, VMEM),
        scratch_shapes=[pltpu.VMEM((TOK, D), BF)]
        + scatter_scratch(TOK, TOK // 2, D)
        + grads_scratch()
        + sems(SCATTERS)
        + sems(GATHERS)
        + sems(2 + N - 1)
        + sems(SCATTERS)
        + [pltpu.SemaphoreType.DMA((2,)), pltpu.SemaphoreType.DMA],
        compiler_params=params(collective_id),
    )(parts, x, grad, gain, src_a, src_b)


ALL_ROWS = LAYERS * ROWS + 16


def last_kernel(
    parts, x, grad, gain, out_parts, x_last, bias, src_a, src_b, vecs, share,
    grad_next, outputs, out, both, v_mine, v_their, v_all, *rest,
):
    buffers, rest = rest[:SCRATCHES], rest[SCRATCHES:]
    buffers_o, rest = rest[:SCRATCHES], rest[SCRATCHES:]
    scratch, rest = rest[:GRADS], rest[GRADS:]
    lane, lane_o, lane_w, lane_z, lane_v, lane_x = (Lane(rest[2 * i : 2 * i + 2]) for i in range(6))
    own, keep_sem = rest[12], rest[13]
    c, f, k = lax.axis_index("ctx"), lax.axis_index("fsdp"), lax.axis_index("dp")
    ctx, fsdp = Group("ctx"), Group("fsdp")
    cs, fs = others("ctx", c), others("fsdp", f)
    core = {"dp": 1 - k}
    meet(cs + fs + [core])
    kept = []

    def tokens():
        def take(total):
            back, grad_gain, grad_shift = norm_back(x[...], total, gain[...])
            grad_next[...] = grad[...] + back
            rounded = grad[...].astype(BF).astype(F32)
            branch = jnp.sum(rounded, axis=0, keepdims=True)
            mine = jnp.concatenate([vecs[...], branch, grad_gain, grad_shift, jnp.zeros((5, D), F32)], axis=0)
            v_mine[0] = mine[:, :HALF].astype(BF)
            v_mine[1] = mine[:, HALF:].astype(BF)

        yield from scatter_steps(lane, ctx, parts, TOK // 2, TOK, buffers, take)
        cross = lane_v.go(v_mine.at[1 - k], v_their, core)
        yield
        cross.wait_recv()
        v_all[f] = (v_mine[k].astype(F32) + v_their[...].astype(F32)).astype(BF)
        copies = [lane_v.go(v_all.at[f], v_all.at[f], peer) for peer in fs]
        for copy in copies:
            yield
            copy.wait_recv()
        total = v_all[0].astype(F32)
        for i in range(1, N):
            total = total + v_all[i].astype(F32)
        both[pl.ds(LAYERS * ROWS, 16)] = total.astype(BF)

    def weights():
        def take(total):
            both[pl.ds(0, ROWS)] = total.astype(BF)

        both[pl.ds(ROWS, ROWS)] = share[...]
        yield from grads_steps(lane_w, lane_z, fsdp, cs, core, src_a, src_b, scratch, own, take)

    def ends():
        def take(total):
            outputs[...] = x_last[...] + (total + bias[...])

        yield from scatter_steps(lane_o, ctx, out_parts, TOK // 2, TOK, buffers_o, take)

    run(tokens(), weights(), ends())
    keep = pltpu.make_async_copy(both, out.at[k, c], keep_sem)
    keep.start()
    run(gather_steps(lane_x, ctx, both, lambda slot: out.at[k, slot], 176, ALL_ROWS))
    keep.wait()
    lane_x.go(out.at[k], out.at[k], core).wait_recv()
    for each in (lane, lane_o, lane_w, lane_z, lane_v, lane_x):
        each.finish()


def last(parts, x, grad, gain, out_parts, x_last, bias, src_a, src_b, vecs, share, collective_id):
    tokens = jax.ShapeDtypeStruct((TOK, D), F32)
    return pl.pallas_call(
        last_kernel,
        out_shape=(tokens, tokens, jax.ShapeDtypeStruct((2, N, ALL_ROWS, HALF), BF)),
        in_specs=[VMEM] * 7 + [ANY] * 2 + [VMEM] * 2,
        out_specs=(VMEM, VMEM, ANY),
        scratch_shapes=[
            pltpu.VMEM((ALL_ROWS, HALF), BF),
            pltpu.VMEM((2, 16, HALF), BF),
            pltpu.VMEM((16, HALF), BF),
            pltpu.VMEM((N, 16, HALF), BF),
        ]
        + scatter_scratch(TOK, TOK // 2, D)
        + scatter_scratch(TOK, TOK // 2, D)
        + grads_scratch()
        + sems(SCATTERS)
        + sems(SCATTERS)
        + sems(2 + N - 1)
        + sems(SCATTERS)
        + sems(N)
        + sems(GATHERS + 1)
        + [pltpu.SemaphoreType.DMA((2,)), pltpu.SemaphoreType.DMA],
        compiler_params=params(collective_id),
    )(parts, x, grad, gain, out_parts, x_last, bias, src_a, src_b, vecs, share)


def marks_of(places):
    frequency = 10000.0 ** (-2.0 * jnp.arange(ROT // 2, dtype=F32) / ROT)
    where = places.astype(F32).reshape(1, -1)
    angles = frequency[:, None] * where
    return jnp.concatenate([jnp.cos(angles), jnp.sin(angles), jnp.broadcast_to(where, angles.shape)], axis=0)


def tables_kernel(marks, tables, col):
    zero = jnp.zeros((8, TOK), F32)
    one = zero + 1.0
    for i in range(N):
        cosine, sine, where = marks[i, 0:8], marks[i, 8:16], marks[i, 16:24]
        rows = pl.ds(i * TOK, TOK)
        own = [cosine, cosine] + [one] * 6
        left = [zero, sine] + [zero] * 6
        right = [-sine, zero] + [zero] * 6
        for t, tiles in enumerate((own, left, right)):
            tables[t, rows] = jnp.concatenate(tiles + tiles, axis=0).T
        col[rows] = jnp.concatenate([where] * 16, axis=0).T


def rotary_tables(marks):
    return pl.pallas_call(
        tables_kernel,
        out_shape=(jax.ShapeDtypeStruct((3, SEQ, 128), F32), jax.ShapeDtypeStruct((SEQ, 128), F32)),
        in_specs=[VMEM],
        out_specs=[VMEM] * 2,
        compiler_params=pltpu.CompilerParams(vmem_limit_bytes=48 * 1024 * 1024),
    )(marks)


BLOCK = 256
BLOCKS = SEQ // BLOCK


def unit_rows(b):
    s = lax.axis_index("ctx") % 2
    start = jnp.where(b < BLOCKS, b * BLOCK, s * (SEQ // 2) + (b - BLOCKS) * BLOCK)
    start = pl.multiple_of(start, BLOCK)
    lanes = lax.broadcasted_iota(jnp.int32, (BLOCK, 2 * HEAD_DIM), 1) // HEAD_DIM
    return start, lanes == jnp.where(b < BLOCKS, 0, 1)


def forward_kernel(
    unit, gain, shift, w_cat, w_mix, b_cat, col, row, tables,
    branch, normed, query, key, value, slope, mixed, lse, turned,
):
    @pl.loop(0, BLOCKS)
    def _(i):
        rows = pl.ds(pl.multiple_of(i * BLOCK, BLOCK), BLOCK)
        low = (unit[rows].astype(F32) * gain[...] + shift[...]).astype(BF)
        normed[rows] = low
        heads = dot(low, w_cat[0], ((1,), (0,))) + b_cat[:, :HALF]

        def rotate(values):
            return (
                values * tables[0, rows]
                + pltpu.roll(values, 8, axis=1) * tables[1, rows]
                + pltpu.roll(values, 120, axis=1) * tables[2, rows]
            )

        query[rows] = (rotate(heads[:, :128]) * HEAD_DIM ** (-0.5)).astype(BF)
        key[rows] = rotate(heads[:, 128:256]).astype(BF)
        value[rows] = heads[:, 256:].astype(BF)
        pre = dot(low, w_cat[1], ((1,), (0,))) + b_cat[:, HALF:]
        cdf = 0.5 * (1.0 + lax.erf(pre * 0.5**0.5))
        mixed[rows, pl.ds(128, HALF)] = (pre * cdf).astype(BF)
        mixed[rows, pl.ds(0, 128)] = jnp.zeros((BLOCK, 128), BF)
        slope[rows] = cdf + pre * (jnp.exp(-0.5 * pre * pre) * 0.3989422804014327)

    turned[...] = value[...].astype(F32).T.astype(BF)

    @pl.loop(0, BLOCKS + 2)
    def _(b):
        start, mask = unit_rows(b)
        rows = pl.ds(start, BLOCK)
        q = jnp.where(mask, query[rows].astype(F32), 0.0).astype(BF)
        scores = dot(key[...], q, ((1,), (1,)))
        seen = jnp.concatenate([col[...], col[...]], axis=1) <= row[pl.ds(start // BLOCK, 1)]
        scores = jnp.where(seen, scores, -jnp.inf)
        top = jnp.max(scores, axis=0, keepdims=True)
        expos = jnp.exp(scores - top)
        total = jnp.sum(expos, axis=0, keepdims=True)
        lse[pl.ds(b, 1)] = top + jnp.log(total)
        probs = (expos * (1.0 / total)).astype(BF)
        out = dot(turned[...], probs, ((1,), (0,))).T
        mixed[rows, pl.ds(0, 128)] = jnp.where(mask, out, mixed[rows, pl.ds(0, 128)].astype(F32)).astype(BF)

    @pl.loop(0, BLOCKS)
    def _(i):
        rows = pl.ds(pl.multiple_of(i * BLOCK, BLOCK), BLOCK)
        branch[rows] = dot(mixed[rows], w_mix[...], ((1,), (0,))).astype(BF)


def local_params():
    return pltpu.CompilerParams(vmem_limit_bytes=48 * 1024 * 1024)


def forward(unit, gain, shift, w_cat, w_mix, b_cat, col, row, tables):
    shape = jax.ShapeDtypeStruct
    return pl.pallas_call(
        forward_kernel,
        out_shape=(
            shape((SEQ, D), BF),
            shape((SEQ, D), BF),
            shape((SEQ, 128), BF),
            shape((SEQ, 128), BF),
            shape((SEQ, 128), BF),
            shape((SEQ, HALF), F32),
            shape((SEQ, 512), BF),
            shape((8, BLOCK), F32),
        ),
        in_specs=[VMEM] * 9,
        out_specs=[VMEM] * 8,
        scratch_shapes=[pltpu.VMEM((128, SEQ), BF)],
        compiler_params=local_params(),
    )(unit, gain, shift, w_cat, w_mix, b_cat, col, row, tables)


def backward_kernel(
    low, w_mix, w_cat, normed, query, key, value, slope, mixed, lse, col, row, tables,
    grad_normed, part_a, part_b, grad_b,
    grad_att, grad_pre, dq, dk, dv, turned, big,
):
    @pl.loop(0, BLOCKS)
    def _(i):
        rows = pl.ds(pl.multiple_of(i * BLOCK, BLOCK), BLOCK)
        back = dot(low[rows], w_mix[...], ((1,), (1,)))
        grad_att[rows] = back[:, :128].astype(BF)
        grad_pre[rows, pl.ds(HALF, HALF)] = (back[:, 128:] * slope[rows]).astype(BF)

    turned[...] = key[...].astype(F32).T.astype(BF)
    dq[...] = jnp.zeros((SEQ, 128), F32)
    dk[...] = jnp.zeros((SEQ, 128), F32)
    dv[...] = jnp.zeros((SEQ, 128), F32)

    @pl.loop(0, BLOCKS + 2)
    def _(b):
        start, mask = unit_rows(b)
        rows = pl.ds(start, BLOCK)
        q = jnp.where(mask, query[rows].astype(F32), 0.0).astype(BF)
        g = jnp.where(mask, grad_att[rows].astype(F32), 0.0).astype(BF)
        scores = dot(key[...], q, ((1,), (1,)))
        seen = jnp.concatenate([col[...], col[...]], axis=1) <= row[pl.ds(start // BLOCK, 1)]
        probs = jnp.exp(jnp.where(seen, scores, -jnp.inf) - lse[pl.ds(b, 1)])
        grad_probs = dot(value[...], g, ((1,), (1,)))
        mean = jnp.sum(probs * grad_probs, axis=0, keepdims=True)
        grad_scores = (probs * (grad_probs - mean)).astype(BF)
        dq[rows] = jnp.where(mask, dot(turned[...], grad_scores, ((1,), (0,))).T, dq[rows])
        dk[...] += dot(grad_scores, q, ((1,), (0,)))
        dv[...] += dot(probs.astype(BF), g, ((1,), (0,)))

    grad_b[...] = jnp.zeros((1, D), F32)

    @pl.loop(0, BLOCKS)
    def _(i):
        rows = pl.ds(pl.multiple_of(i * BLOCK, BLOCK), BLOCK)

        def rotate_back(grads):
            return (
                grads * tables[0, rows]
                + pltpu.roll(grads * tables[1, rows], 120, axis=1)
                + pltpu.roll(grads * tables[2, rows], 8, axis=1)
            )

        grad_pre[rows, pl.ds(0, 128)] = rotate_back(dq[rows] * HEAD_DIM ** (-0.5)).astype(BF)
        grad_pre[rows, pl.ds(128, 128)] = rotate_back(dk[rows]).astype(BF)
        grad_pre[rows, pl.ds(256, 128)] = dv[rows].astype(BF)
        block = grad_pre[rows]
        grad_b[...] += jnp.sum(block.astype(F32), axis=0, keepdims=True)
        grad_normed[rows] = (
            dot(block[:, :HALF], w_cat[0], ((1,), (1,))) + dot(block[:, HALF:], w_cat[1], ((1,), (1,)))
        ).astype(BF)

    @pl.loop(0, D // BLOCK)
    def _(i):
        cols = pl.ds(pl.multiple_of(i * BLOCK, BLOCK), BLOCK)
        big[cols] = dot(normed[:, cols], grad_pre[...], ((0,), (0,)))

    for f in range(N):
        for h in range(2):
            part_a[h, f] = big[96 * f : 96 * f + 96, HALF * h : HALF * h + HALF].astype(BF)

    @pl.loop(0, 2)
    def _(i):
        cols = pl.ds(pl.multiple_of(i * BLOCK, BLOCK), BLOCK)
        big[cols] = dot(mixed[:, cols], low[...], ((0,), (0,)))

    for j in range(N):
        for h in range(2):
            at = slice(HALF * h, HALF * h + HALF)
            first = big[8 * j : 8 * j + 8, at]
            second = big[64 + 8 * j : 64 + 8 * j + 8, at]
            part_b[h, j, pl.ds(0, 16)] = jnp.concatenate([first, second], axis=0).astype(BF)
            part_b[h, j, pl.ds(16, 48)] = big[128 + 48 * j : 176 + 48 * j, at].astype(BF)


def backward(low, w_mix, w_cat, normed, query, key, value, slope, mixed, lse, col, row, tables):
    shape = jax.ShapeDtypeStruct
    return pl.pallas_call(
        backward_kernel,
        out_shape=(
            shape((SEQ, D), BF),
            shape((2, N, 96, HALF), BF),
            shape((2, N, PIECE, HALF), BF),
            shape((1, D), F32),
        ),
        in_specs=[VMEM] * 13,
        out_specs=[VMEM] * 4,
        scratch_shapes=[
            pltpu.VMEM((SEQ, 128), BF),
            pltpu.VMEM((SEQ, D), BF),
            pltpu.VMEM((SEQ, 128), F32),
            pltpu.VMEM((SEQ, 128), F32),
            pltpu.VMEM((SEQ, 128), F32),
            pltpu.VMEM((128, SEQ), BF),
            pltpu.VMEM((D, D), F32),
        ],
        compiler_params=local_params(),
    )(low, w_mix, w_cat, normed, query, key, value, slope, mixed, lse, col, row, tables)


def spread_kernel(got, g_qkv, g_out, g_up, g_down):
    odd = lax.axis_index("fsdp") % 2
    for layer in range(LAYERS):
        base = layer * ROWS

        def heads(i):
            return got[0, i, pl.ds(base, 96)].astype(F32)

        chunks = []
        for p in range(4):
            one, two = heads(2 * p), heads(2 * p + 1)
            both = one + two
            for values, lane in ((one, 0), (both, HEAD_DIM), (two, 0)):
                chunks += [values[:, 128 * i + lane : 128 * i + lane + HEAD_DIM] for i in range(3)]
        for i in range(len(chunks) // 2):
            g_qkv[layer, :, pl.ds(128 * i, 128)] = jnp.concatenate(chunks[2 * i : 2 * i + 2], axis=1)
        for i in range(N):
            g_up[layer, :, pl.ds(HALF * i, HALF)] = got[1, i, pl.ds(base, 96)].astype(F32)
            for h in range(2):
                cols = pl.ds(HALF * h, HALF)
                g_down[layer, pl.ds(48 * i, 48), cols] = got[h, i, pl.ds(base + 112, 48)].astype(F32)
        for h in range(2):
            cols = pl.ds(HALF * h, HALF)
            rows = [got[h, i, pl.ds(base + 96, 16)].astype(F32) for i in range(N)]
            first = [r[:8] for r in rows]
            even = jnp.concatenate(first + [r[8:] for r in rows[:4]], axis=0)
            uneven = jnp.concatenate([r[8:] for r in rows[4:]] + first, axis=0)
            g_out[layer, :, cols] = jnp.where(odd == 0, even, uneven)


def spread(got):
    shape = jax.ShapeDtypeStruct
    return pl.pallas_call(
        spread_kernel,
        out_shape=(
            shape((LAYERS, 96, 3 * D), F32),
            shape((LAYERS, 96, D), F32),
            shape((LAYERS, 96, FF), F32),
            shape((LAYERS, HALF, D), F32),
        ),
        in_specs=[VMEM],
        out_specs=[VMEM] * 4,
        compiler_params=local_params(),
    )(got)


def body(
    inputs, positions, cotangent, w_qkv, b_qkv, w_out, b_out, w_up, b_up, w_down, b_down, ln_gain, ln_bias
):
    c = lax.axis_index("ctx")
    p, s = c // 2, lax.rem(c, 2)
    head_a, head_b = 3 * p + 2 * s, 3 * p + 1

    def heads_cols(w):
        grouped = w.reshape(w.shape[:-1] + (12, 3, HEAD_DIM))
        axis = grouped.ndim - 3
        both = jnp.concatenate(
            [
                lax.dynamic_slice_in_dim(grouped, head_a, 1, axis=axis),
                lax.dynamic_slice_in_dim(grouped, head_b, 1, axis=axis),
            ],
            axis=axis,
        )
        return jnp.swapaxes(both, axis, axis + 1).reshape(w.shape[:-1] + (HALF,))

    def hidden_cols(w):
        return lax.dynamic_slice_in_dim(w, c * HALF, HALF, axis=w.ndim - 1)

    f = lax.axis_index("fsdp")
    f_s = lax.rem(f, 2)

    def piece(w, start, count):
        return lax.dynamic_slice_in_dim(w, start, count, axis=1)

    cols = jnp.concatenate([heads_cols(w_qkv), hidden_cols(w_up)], axis=-1)
    first_rows = piece(w_out, jnp.where(f_s == 0, 0, 32) + 8 * c, 8)
    shared_rows = piece(w_out, jnp.where(f_s == 0, 64, -32) + 8 * jnp.where(f_s == 0, c % 4, c), 8)
    down_rows = piece(w_down, 48 * c, 48)
    by_layer = jnp.concatenate([cols, first_rows, shared_rows, down_rows], axis=1)
    vec = jnp.concatenate([b_qkv, b_out, b_up, b_down, ln_gain, ln_bias], axis=1).reshape(-1)
    vec = jnp.pad(vec, (0, 16 * D - vec.shape[0])).reshape(16, D)
    stream, cot = inputs[0], cotangent[0]
    src = [jnp.concatenate([by_layer[0], vec], axis=0), by_layer[1]]
    src = [jnp.stack([one[:, :HALF], one[:, HALF:]]) for one in src]
    cols, pieces, vec_all, marks, unit, low_last = gather_weights(
        src[0], marks_of(positions), stream, cot, 1
    )

    def mix_of(pieces):
        one = jnp.concatenate([pieces[0], pieces[1]], axis=-1)
        return jnp.concatenate(
            [one[:, :8].reshape(64, D), one[:, 8:16].reshape(64, D), one[:, 16:].reshape(HALF, D)], axis=0
        )

    w_cat, w_mix = [cols.reshape(2, D, HALF)], [mix_of(pieces)]
    vec_all = jnp.concatenate([vec_all[0], vec_all[1]], axis=-1)
    vec_all = vec_all.reshape(N, -1)[:, : LAYERS * 1056].reshape(N, LAYERS, 1056)
    vec_all = jnp.swapaxes(vec_all, 0, 1).astype(F32)
    starts = (0, 288, 384, 768, 864, 960, 1056)
    b_qkv_all, b_out_all, b_up_all, b_down_all, gain_all, shift_all = (
        vec_all[:, :, starts[i] : starts[i + 1]].reshape(LAYERS, -1) for i in range(6)
    )
    b_cat = jnp.concatenate([heads_cols(b_qkv_all), hidden_cols(b_up_all)], axis=-1)
    b_sum = b_out_all + b_down_all
    tables, col = rotary_tables(marks)
    row = marks[:, 16].reshape(BLOCKS, BLOCK)

    def ahead(layer, unit):
        return forward(
            unit.reshape(SEQ, D), gain_all[layer][None], shift_all[layer][None], w_cat[layer], w_mix[layer],
            b_cat[layer][None], col, row, tables,
        )

    def back(layer, low, kept):
        return backward(low.reshape(SEQ, D), w_mix[layer], w_cat[layer], *kept, col, row, tables)

    branch, *kept_first = ahead(0, unit)
    x_last, unit, cols, pieces = between(branch.reshape(N, TOK, D), stream, b_sum[0][None], src[1], 2)
    w_cat.append(cols.reshape(2, D, HALF))
    w_mix.append(mix_of(pieces))
    branch, *kept_last = ahead(1, unit)
    grad_normed, part_a, part_b, grad_b_last = back(1, low_last, kept_last)
    grad, low, vecs, share = turn(
        grad_normed.reshape(N, TOK, D), x_last, cot, gain_all[1][None], part_a, part_b, 3
    )
    grad_normed, part_a, part_b, grad_b_first = back(0, low, kept_first)
    vecs = jnp.concatenate([vecs[:3], grad_b_last, grad_b_first, jnp.zeros((3, D), F32)], axis=0)
    grad, outputs, got = last(
        grad_normed.reshape(N, TOK, D), stream, grad, gain_all[0][None], branch.reshape(N, TOK, D), x_last,
        b_sum[1][None], part_a, part_b, vecs, share, 4,
    )
    g_qkv, g_out, g_up, g_down = spread(got)

    rows = jnp.concatenate([got[0, :, LAYERS * ROWS :], got[1, :, LAYERS * ROWS :]], axis=-1).astype(F32)
    summed = jnp.sum(rows, axis=0)

    def cut(vector, width):
        return lax.dynamic_slice_in_dim(vector, f * width, width, axis=vector.ndim - 1)

    def own_vectors(biases):
        qkv = biases[:, :HALF].reshape(4, 2, 3, 2, HEAD_DIM)
        shared = qkv[:, 0, :, 1] + qkv[:, 1, :, 1]
        qkv = jnp.stack([qkv[:, 0, :, 0], shared, qkv[:, 1, :, 0]], axis=1).reshape(3 * D)
        up = lax.dynamic_index_in_dim(biases[:, HALF:], f, axis=0, keepdims=False)
        return cut(qkv, 288), up

    pairs = [own_vectors(rows[:, 4]), own_vectors(rows[:, 3])]
    g_b_qkv = jnp.stack([pair[0] for pair in pairs])
    g_b_up = jnp.stack([pair[1] for pair in pairs])
    g_branch, g_gain, g_shift = (cut(jnp.stack([summed[8 + i], summed[i]]), 96) for i in range(3))
    return (
        outputs[None], grad[None], g_qkv, g_b_qkv, g_out, g_branch, g_up, g_b_up, g_down, g_branch, g_gain, g_shift,
    )


def solution(mesh):
    seqs = ("dp", "fsdp")
    whole = P(None, "fsdp", None)
    row = P(None, "fsdp")
    in_specs = (
        P(seqs, "ctx", None), P(seqs, "ctx"), P(seqs, "ctx", None),
        whole, row, whole, row, whole, row, whole, row, row, row,
    )
    out_specs = (
        P(seqs, "ctx", None), P(seqs, "ctx", None),
        whole, row, whole, row, whole, row, whole, row, row, row,
    )
    return jax.shard_map(body, mesh=mesh, in_specs=in_specs, out_specs=out_specs, check_vma=False)
```

time: 455 us -> 300 us (0.66); the launches traced: 447 us -> 297 us
  matrix products: 52 us -> 0 us
  other arithmetic: 56 us -> 5.5 us
  local copies, waits for them, and re-layouts: 64.5 us -> 31.8 us
  Pallas kernels: 271 us -> 259 us
    dot_general x22 -> x0, matrix products: 38.9 us -> none  [the longest x12 23.7 us: dot(): return lax.dot_general(a, b, (dims, ((), ())), preferred_element_type=F32)]
    another operation x32 -> x4, local copies, waits for them, and re-layouts: 13.3 us -> 0.05 us  [the longest x1 0.03 us: body(): src = [jnp.stack([one[:, :HALF], one[:, HALF:]]) for one in src]]
    sub x2 -> x0, matrix products: 13.1 us -> none  [body(): expos = jnp.exp(scores - row_max)]
    convert_element_type x11 -> x1, other arithmetic: 12.3 us -> 0.03 us  [body(): jnp.concatenate([got[0, :, LAYERS * ROWS:], got[1, :, LAYERS * ROWS:]], a...]
    pallas_call x11 -> x10, Pallas kernels: 271 us -> 259 us  [the longest x1 72.6 us: last(): pl.pallas_call(last_kernel, out_shape=(tokens, tokens, jax.ShapeDtypeStru...]
    slice x41 -> x15, local copies, waits for them, and re-layouts: 11.6 us -> 1.61 us  [the longest x2 1.09 us: body(): b_sum[1][None]]
    another operation x17 -> x10, other arithmetic: 11.8 us -> 2.65 us  [the longest x3 1.36 us: body(): jnp.stack([summed[8 + i], summed[i]])]
    concatenate x10 -> x7, other arithmetic: 8.88 us -> 0.3 us  [the longest x2 0.11 us: mix_of(): jnp.concatenate([one[:, :8].reshape(64, D), one[:, 8:16].reshape(64, D),...]
where the time goes in v2:
time: 300 us; the launch traced here: 297 us
  Pallas kernels  259 us (86%)
  local copies, waits for them, and re-layouts  31.8 us (11%)
  other arithmetic  5.5 us (2%)
    pallas_call x1, Pallas kernels, last(): pl.pallas_call(last_kernel, out_shape=(tokens, tokens, jax.ShapeDtypeStru...  72.6 us
    pallas_call x1, Pallas kernels, gather_weights(): pl.pallas_call(weights_kernel, out_shape=(COLS_SHAPE, PIECES_SHAPE, jax.S...  45.6 us
    pallas_call x1, Pallas kernels, between(): pl.pallas_call(between_kernel, out_shape=(jax.ShapeDtypeStruct((TOK, D),...  38.7 us
    pallas_call x2, Pallas kernels, backward(): pl.pallas_call(backward_kernel, out_shape=(shape((SEQ, D), BF), shape((2,...  36.5 us
    pallas_call x1, Pallas kernels, turn(): pl.pallas_call(turn_kernel, out_shape=(jax.ShapeDtypeStruct((TOK, D), F32...  34.4 us
    pallas_call x2, Pallas kernels, forward(): pl.pallas_call(forward_kernel, out_shape=(shape((SEQ, D), BF), shape((SEQ...  27.2 us
    unnamed x49, local copies, waits for them, and re-layouts  18.8 us

profile of v2, /device:TPU:1, one launch (start us, length us, event | category | flops | bytes accessed | tf_op | source)
XLA Modules:
  0.0 297.5 jit_solution(8144543013967397870)
XLA Ops:
  3.5 1.6 constant_dynamic-slice_fusion.8
  7.9 45.6 %shard_map.220 = (bf16[2,8,96,384]{3,2,1,0:T(8,128)(2,1)S(1)}, bf16[2,8,64,384]{3,2,1,0:T(8,128)(2,1)S(1)}, bf16[2,8,16,384]{3,2,1,0:T(8,128)(2,1)S(1)}, f32[8,2...) custom-call(bf16[2,176,384]{2,1,0:T(8,128)(2,1)S(1)} %pad_maximum_fusion.5.src, ...), custom_call_target="tpu_custom_call" | custom-call | tf_op jit(solution)/shard_map/pallas_call | solution.py:311
  53.5 1.1 copy-done.9
  54.7 1.1 copy-done.11
  55.8 0.9 copy-done.14
  57.4 1.2 slice_bitcast_fusion.11
  59.3 1.6 reshape.187
  61.7 1.0 slice_reduce_fusion
  66.3 1.2 slice_bitcast_fusion.3
  68.3 1.1 copy-done.1
  69.4 13.6 %shard_map.222 = (bf16[1024,768]{1,0:T(8,128)(2,1)S(1)}, bf16[1024,768]{1,0:T(8,128)(2,1)}, bf16[1024,128]{1,0:T(8,128)(2,1)S(1)}, bf16[1024,128]{1,0:T(8,128)(2...) custom-call(bf16[1024,768]{1,0:T(8,128)(2,1)} %bitcast.98, ...), custom_call_target="tpu_custom_call" | custom-call | tf_op jit(solution)/shard_map/pallas_call | solution.py:699
  83.0 38.7 %shard_map.223 = (f32[128,768]{1,0:T(8,128)S(1)}, bf16[8,128,768]{2,1,0:T(8,128)(2,1)S(1)}, bf16[2,8,96,384]{3,2,1,0:T(8,128)(2,1)S(1)}, bf16[2,8,64,384]{3,2,1,0:T(8,128)(2,1)S(1)}) custom-call(bf16[8,128,768]{2,1,0:T(8,128)(2,1)S(1)} %bitcast.95, f32[128,768]{1,0:T(8,128)S(1)} %bitcast.92, f32[1,768]{1,0:T(1,128)S(1)} %slice.213.bias, ...), custom_call_target="tpu_custom_call" | custom-call | tf_op jit(solution)/shard_map/pallas_call | solution.py:369
  121.9 0.9 copy-done.10
  123.4 13.6 %shard_map.224 = (bf16[1024,768]{1,0:T(8,128)(2,1)S(1)}, bf16[1024,768]{1,0:T(8,128)(2,1)}, bf16[1024,128]{1,0:T(8,128)(2,1)S(1)}, bf16[1024,128]{1,0:T(8,128)(2...) custom-call(bf16[1024,768]{1,0:T(8,128)(2,1)} %bitcast.99, ...), custom_call_target="tpu_custom_call" | custom-call | tf_op jit(solution)/shard_map/pallas_call | solution.py:699
  137.0 18.3 %shard_map.225 = (bf16[1024,768]{1,0:T(8,128)(2,1)}, bf16[2,8,96,384]{3,2,1,0:T(8,128)(2,1)S(1)}, bf16[2,8,64,384]{3,2,1,0:T(8,128)(2,1)S(1)}, f32[1,768]{1,0:T(1,128)S(1)}) custom-call(bf16[1024,768]{1,0:T(8,128)(2,1)} %bitcast.100, bf16[512,768]{1,0:T(8,128)(2,1)S(1)} %pad_maximum_fusion.1.w_mix, bf16[2,768,384]{2,1,0:T(8,128)(2,1)} %bitcast.90, ...), custom_call_target="tpu_custom_call" | custom-call | tf_op jit(solution)/shard_map/pallas_call | solution.py:798
  155.2 1.4 copy-done.7
  156.7 34.4 %shard_map.226 = (f32[128,768]{1,0:T(8,128)S(1)}, bf16[8,128,768]{2,1,0:T(8,128)(2,1)S(1)}, f32[8,768]{1,0:T(8,128)S(1)}, bf16[160,384]{1,0:T(8,128)(2,1)S(1)}) custom-call(bf16[8,128,768]{2,1,0:T(8,128)(2,1)S(1)} %bitcast.94, f32[128,768]{1,0:T(8,128)S(1)} %get-tuple-element.79.x.x_last, f32[128,768]{1,0:T(8,128)S(1)} %bitcast.97, ...), custom_call_target="tpu_custom_call" | custom-call | tf_op jit(solution)/shard_map/pallas_call | solution.py:484
  191.1 1.1 copy-done.13
  192.2 18.2 %shard_map.227 = (bf16[1024,768]{1,0:T(8,128)(2,1)}, bf16[2,8,96,384]{3,2,1,0:T(8,128)(2,1)S(1)}, bf16[2,8,64,384]{3,2,1,0:T(8,128)(2,1)S(1)}, f32[1,768]{1,0:T(1,128)S(1)}) custom-call(bf16[1024,768]{1,0:T(8,128)(2,1)} %bitcast.103, bf16[512,768]{1,0:T(8,128)(2,1)S(1)} %pad_maximum_fusion.w_mix, bf16[2,768,384]{2,1,0:T(8,128)(2,1)} %bitcast.88, ...), custom_call_target="tpu_custom_call" | custom-call | tf_op jit(solution)/shard_map/pallas_call | solution.py:798
  210.6 1.4 copy-done.12
  212.0 72.6 %shard_map.228 = (f32[128,768]{1,0:T(8,128)S(1)}, f32[128,768]{1,0:T(8,128)S(1)}, bf16[2,8,336,384]{3,2,1,0:T(8,128)(2,1)S(1)}) custom-call(bf16[8,128,768]{2,1,0:T(8,128)(2,1)S(1)} %bitcast.102, f32[128,768]{1,0:T(8,128)S(1)} %bitcast.93, f32[128,768]{1,0:T(8,128)S(1)} %get-tuple-element.91.grad, f32[1,768]{1,0:T(1,128)S(1)} %slice.198.gain, ...), custom_call_target="tpu_custom_call" | custom-call | tf_op jit(solution)/shard_map/pallas_call | solution.py:574
  284.6 1.9 copy-done.4
  289.9 2.2 copy-done.5
  292.1 3.4 %shard_map.229 = (f32[2,96,2304]{2,1,0:T(8,128)}, f32[2,96,768]{2,1,0:T(8,128)}, f32[2,96,3072]{2,1,0:T(8,128)}, f32[2,384,768]{2,1,0:T(8,128)}) custom-call(bf16[2,8,336,384]{3,2,1,0:T(8,128)(2,1)S(1)} %copy-done.5), custom_call_target="tpu_custom_call" | custom-call | tf_op jit(solution)/shard_map/pallas_call | solution.py:853
  (121 shorter events, 18.0 us)
Async XLA Ops:
  0.6 2.8 copy-start
  0.7 4.4 %copy-start.16 = (bf16[2,96,2304]{2,1,0:T(8,128)(2,1)S(1)}, bf16[2,96,2304]{2,1,0:T(8,128)(2,1)}, u32[]{:S(2)}) copy-start(bf16[2,96,2304]{2,1,0:T(8,128)(2,1)} %param.16) | copy-start | bytes 2654212
  5.8 0.9 copy-start.17
  6.8 1.0 copy-start.6
  6.8 1.1 copy-start.8
  53.5 1.1 copy-start.9
  54.7 1.1 copy-start.11
  55.8 0.9 copy-start.14
  56.7 0.7 copy-start.15
  57.4 12.0 %copy-start.2 = (bf16[2,8,96,384]{3,2,1,0:T(8,128)(2,1)}, bf16[2,8,96,384]{3,2,1,0:T(8,128)(2,1)S(1)}, u32[]{:S(2)}) copy-start(bf16[2,8,96,384]{3,2,1,0:T(8,128)(2,1)S(1)} %get-tuple-element.62) | copy-start | bytes 3538948
  68.3 1.1 copy-start.1
  121.7 1.1 copy-start.10
  121.7 1.6 copy-start.3
  155.2 1.4 copy-start.7
  191.1 1.1 copy-start.13
  210.6 1.4 copy-start.12
  284.6 1.9 copy-start.4
  287.3 8.2 %copy-start.18 = (f32[2,96]{1,0:T(2,128)}, f32[2,96]{1,0:T(2,128)S(1)}, u32[]{:S(2)}) copy-start(f32[2,96]{1,0:T(2,128)S(1)} %fusion.9) | copy-start | bytes 2308
  289.9 2.2 copy-start.5

commit v3 on v2

v3 whole, which is shorter than its diff:
```python
import functools

import jax
import jax.numpy as jnp
from jax import lax
from jax.experimental import pallas as pl
from jax.experimental.pallas import tpu as pltpu
from jax.sharding import PartitionSpec as P

MESH = pl.DeviceIdType.MESH
HEAD_DIM = 64
ROT = 16
LAYERS = 2
D = 768
FF = 3072
N = 8
TOK = 128
SEQ = 1024
HALF = 384
epsilon = 1e-05
BF = jnp.bfloat16
F32 = jnp.float32
ANY = pl.BlockSpec(memory_space=pl.ANY)


def dot(a, b, dims):
    return lax.dot_general(a, b, (dims, ((), ())), preferred_element_type=F32)


def meet(devices):
    barrier = pltpu.get_barrier_semaphore()
    for device in devices:
        pl.semaphore_signal(barrier, inc=1, device_id=device, device_id_type=MESH)
    pl.semaphore_wait(barrier, len(devices))


def push(src, dst, send, recv, device):
    copy = pltpu.make_async_remote_copy(
        src_ref=src, dst_ref=dst, send_sem=send, recv_sem=recv, device_id=device, device_id_type=MESH
    )
    copy.start()
    return copy


def others(axis, index):
    return [{axis: lax.rem(index + d, N)} for d in range(1, N)]


class Group:
    def __init__(self, axis):
        self.axis = axis
        index = lax.axis_index(axis)
        self.r, self.h = (index % 4, index // 4) if axis == "ctx" else (index // 2, index % 2)
        self.right = {axis: self.slot(1, 0)}
        self.left = {axis: self.slot(3, 0)}
        self.pair = {axis: self.slot(0, 1)}

    def slot(self, dr, dh):
        r, h = lax.rem(self.r + dr, 4), lax.rem(self.h + dh, 2)
        return h * 4 + r if self.axis == "ctx" else r * 2 + h

    def neighbours(self):
        return [self.right, self.left, self.pair]


class Lane:
    def __init__(self, sems):
        self.send, self.recv = sems
        self.copies = []

    def go(self, src, dst, device):
        i = len(self.copies)
        self.copies.append(push(src, dst, self.send.at[i], self.recv.at[i], device))
        return self.copies[-1]

    def finish(self):
        for copy in self.copies:
            copy.wait_send()


def run(*steps):
    live = list(steps)
    while live:
        for one in list(live):
            try:
                next(one)
            except StopIteration:
                live.remove(one)


GATHERS = 8


def gather_steps(lane, group, own, at, cut, rows):
    head, tail = pl.ds(0, cut), pl.ds(cut, rows - cut)
    go = lane.go
    me, twin, far = group.slot(0, 0), group.slot(0, 1), group.slot(2, 0)
    c0 = go(own, at(me), group.right)
    c1 = go(own, at(me), group.left)
    c2 = go(own, at(me), group.pair)
    yield
    c0.wait_recv()
    behind = at(group.slot(3, 0)).at[head]
    c3 = go(behind, behind, group.right)
    yield
    c1.wait_recv()
    ahead = at(group.slot(1, 0)).at[tail]
    c4 = go(ahead, ahead, group.left)
    yield
    c2.wait_recv()
    c5 = go(at(twin), at(twin), group.right)
    c6 = go(at(twin), at(twin), group.left)
    yield
    c3.wait_recv()
    yield
    c4.wait_recv()
    c7 = go(at(far), at(far), group.pair)
    for copy in (c5, c6, c7):
        yield
        copy.wait_recv()


SCATTERS = 11


def scatter_scratch(rows, cut, width):
    return [
        pltpu.VMEM((rows, width), BF),
        pltpu.VMEM((rows, width), BF),
        pltpu.VMEM((cut, width), BF),
        pltpu.VMEM((rows - cut, width), BF),
        pltpu.VMEM((cut, width), BF),
        pltpu.VMEM((rows - cut, width), BF),
        pltpu.VMEM((2, rows, width), BF),
        pltpu.VMEM((2, rows, width), BF),
        pltpu.VMEM((rows, width), BF),
        pltpu.VMEM((rows, width), BF),
    ]


SCRATCHES = 10


def scatter_steps(lane, group, src, cut, rows, buffers, take):
    in_far, st_far, in_right, in_left, st_left, st_right, from_right, from_left, st_pair, from_pair = buffers
    head, tail = pl.ds(0, cut), pl.ds(cut, rows - cut)
    go = lane.go
    opposite = go(src.at[group.slot(2, 1)], in_far, group.pair)
    beside = [
        go(src.at[group.slot(3, 1)], from_right.at[0], group.left),
        go(src.at[group.slot(1, 1)], from_left.at[0], group.right),
    ]
    near = [
        go(src.at[group.slot(3, 0)].at[tail], from_right.at[1].at[tail], group.left),
        go(src.at[group.slot(1, 0)].at[head], from_left.at[1].at[head], group.right),
    ]
    yield
    opposite.wait_recv()
    st_far[...] = (src[group.slot(2, 0)].astype(F32) + in_far[...].astype(F32)).astype(BF)
    far_left = go(st_far.at[head], in_right, group.left)
    far_right = go(st_far.at[tail], in_left, group.right)
    for copy in beside:
        yield
        copy.wait_recv()
    total = src[group.slot(0, 1)].astype(F32) + from_right[0].astype(F32) + from_left[0].astype(F32)
    st_pair[...] = total.astype(BF)
    last = go(st_pair, from_pair, group.pair)
    yield
    far_left.wait_recv()
    st_left[...] = (src[group.slot(3, 0), head].astype(F32) + in_right[...].astype(F32)).astype(BF)
    near.append(go(st_left, from_right.at[1].at[head], group.left))
    yield
    far_right.wait_recv()
    st_right[...] = (src[group.slot(1, 0), tail].astype(F32) + in_left[...].astype(F32)).astype(BF)
    near.append(go(st_right, from_left.at[1].at[tail], group.right))
    for copy in near + [last]:
        yield
        copy.wait_recv()
    total = src[group.slot(0, 0)].astype(F32) + from_right[1].astype(F32) + from_left[1].astype(F32)
    take(total + from_pair[...].astype(F32))


def sems(count):
    return [pltpu.SemaphoreType.DMA((count,)), pltpu.SemaphoreType.DMA((count,))]


def params(collective_id):
    return pltpu.CompilerParams(
        collective_id=collective_id, has_side_effects=True, vmem_limit_bytes=56 * 1024 * 1024
    )


def normalize(stream):
    mean = jnp.mean(stream, axis=-1, keepdims=True)
    centred = stream - mean
    scale = lax.rsqrt(jnp.mean(centred * centred, axis=-1, keepdims=True) + epsilon)
    return centred * scale, scale


def norm_back(stream, grad_normed, gain):
    unit, scale = normalize(stream)
    grad_unit = grad_normed * gain
    first = jnp.mean(grad_unit, axis=-1, keepdims=True)
    second = jnp.mean(grad_unit * unit, axis=-1, keepdims=True)
    grad_gain = jnp.sum(grad_normed * unit, axis=0, keepdims=True)
    grad_shift = jnp.sum(grad_normed, axis=0, keepdims=True)
    return scale * (grad_unit - first - unit * second), grad_gain, grad_shift


PIECE = 64
ROWS = 96 + PIECE
CUT = 80
W_FIRST = ROWS + 16
W_CUT = 96
VMEM = pl.BlockSpec(memory_space=pltpu.VMEM)


def shard_scratch(rows):
    return [
        pltpu.VMEM((N, rows, HALF), BF),
        pltpu.VMEM((N, PIECE, HALF), BF),
        pltpu.VMEM((N, PIECE, HALF), BF),
    ]


SHARD_LANE = N - 1 + 3


def shard_steps(lane, lane_z, fsdp, cs, core, src, cut, rows, scratch, outs, own, kept):
    held, mixed, got = scratch
    c, k = lax.axis_index("ctx"), lax.axis_index("dp")
    first = pltpu.make_async_copy(src.at[k], held.at[fsdp.slot(0, 0)], own.at[0])
    first.start()
    yield from gather_steps(lane_z, fsdp, src.at[k], lambda slot: held.at[slot], cut, rows)
    first.wait()
    low = lax.broadcasted_iota(jnp.int32, (16, HALF), 0) < 8
    for i in range(N):
        own_rows = held[i, pl.ds(96, 16)].astype(F32)
        shared = held[i // 2 * 2 + c // 4, pl.ds(96, 16)].astype(F32)
        mixed[i, pl.ds(0, 16)] = jnp.where(low, own_rows, shared).astype(BF)
        mixed[i, pl.ds(16, 48)] = held[i, pl.ds(112, 48)]
    turn = [lane.go(mixed.at[peer["ctx"]], got.at[c], peer) for peer in cs]
    got[c] = mixed[c]
    cross = []

    def share(part, out, sem):
        cross.append(lane.go(part, out.at[k], core))
        keep = pltpu.make_async_copy(part, out.at[k], sem)
        keep.start()
        kept.append(keep)

    share(held.at[:, pl.ds(0, 96)], outs[0], own.at[1])
    if len(outs) > 2:
        share(held.at[:, pl.ds(ROWS, 16)], outs[2], own.at[2])
    for copy in turn:
        yield
        copy.wait_recv()
    share(got, outs[1], own.at[3])
    for copy in cross:
        yield
        copy.wait_recv()


COLS_SHAPE = jax.ShapeDtypeStruct((2, N, 96, HALF), BF)
PIECES_SHAPE = jax.ShapeDtypeStruct((2, N, PIECE, HALF), BF)


def weights_kernel(
    src, places, x, cols_all, pieces_all, vec_all, places_all, unit_all, *rest
):
    scratch, unit, rest = rest[:3], rest[3], rest[4:]
    lane, lane_z, lane_m, lane_u = (Lane(rest[2 * i : 2 * i + 2]) for i in range(4))
    own, keeps = rest[8], rest[9]
    c = lax.axis_index("ctx")
    fsdp, ctx = Group("fsdp"), Group("ctx")
    cs = others("ctx", c)
    core = {"dp": 1 - lax.axis_index("dp")}
    mark = pltpu.make_async_copy(places, places_all.at[c], keeps.at[0])
    mark.start()
    meet(fsdp.neighbours() + cs + [core])
    kept = [mark]
    marks = [lane_m.go(places, places_all.at[c], peer) for peer in cs]

    def tokens():
        unit[...] = normalize(x[...])[0].astype(BF)
        keep = pltpu.make_async_copy(unit, unit_all.at[c], keeps.at[1])
        keep.start()
        kept.append(keep)
        yield from gather_steps(lane_u, ctx, unit, lambda slot: unit_all.at[slot], TOK // 2, TOK)

    outs = (cols_all, pieces_all, vec_all)
    run(
        shard_steps(lane, lane_z, fsdp, cs, core, src, W_CUT, W_FIRST, scratch, outs, own, kept),
        tokens(),
    )
    for copy in marks:
        copy.wait_recv()
    for each in (lane, lane_z, lane_m, lane_u):
        each.finish()
    for copy in kept:
        copy.wait()


def gather_weights(src, places, x, collective_id):
    tokens = jax.ShapeDtypeStruct((N, TOK, D), BF)
    return pl.pallas_call(
        weights_kernel,
        out_shape=(
            COLS_SHAPE,
            PIECES_SHAPE,
            jax.ShapeDtypeStruct((2, N, 16, HALF), BF),
            jax.ShapeDtypeStruct((N,) + places.shape, places.dtype),
            tokens,
        ),
        in_specs=[ANY] * 2 + [VMEM],
        out_specs=[ANY] * 5,
        scratch_shapes=shard_scratch(W_FIRST)
        + [pltpu.VMEM((TOK, D), BF)]
        + sems(SHARD_LANE)
        + sems(GATHERS)
        + sems(N - 1)
        + sems(GATHERS)
        + [pltpu.SemaphoreType.DMA((4,)), pltpu.SemaphoreType.DMA((2,))],
        compiler_params=params(collective_id),
    )(src, places, x)


def marks_of(places):
    frequency = 10000.0 ** (-2.0 * jnp.arange(ROT // 2, dtype=F32) / ROT)
    where = places.astype(F32).reshape(1, -1)
    angles = frequency[:, None] * where
    return jnp.concatenate([jnp.cos(angles), jnp.sin(angles), jnp.broadcast_to(where, angles.shape)], axis=0)


def prepare_kernel(marks, vectors, tables, col, rows_out):
    zero = jnp.zeros((8, TOK), F32)
    one = zero + 1.0
    for i in range(N):
        cosine, sine, where = marks[i, 0:8], marks[i, 8:16], marks[i, 16:24]
        rows = pl.ds(i * TOK, TOK)
        own = [cosine, cosine] + [one] * 6
        left = [zero, sine] + [zero] * 6
        right = [-sine, zero] + [zero] * 6
        for t, tiles in enumerate((own, left, right)):
            tables[t, rows] = jnp.concatenate(tiles + tiles, axis=0).T
        col[rows] = jnp.concatenate([where] * 16, axis=0).T

    c = lax.axis_index("ctx")
    head_a, head_b = 3 * (c // 2) + 2 * (c % 2), 3 * (c // 2) + 1

    def place(values, column, width, cut):
        shard = jnp.zeros((1, width), jnp.int32)
        for t in range(1, N):
            shard = shard + jnp.where(column >= cut * t, 1, 0)
        inner = column - cut * shard
        pick = lax.broadcasted_iota(jnp.int32, (HALF, width), 0) == inner
        spread_ = dot(values.astype(BF), jnp.where(pick, 1.0, 0.0).astype(BF), ((1,), (0,)))
        mine = lax.broadcasted_iota(jnp.int32, (N, width), 0) == shard
        return jnp.sum(jnp.where(mine, spread_, 0.0), axis=0, keepdims=True)

    lanes = lax.broadcasted_iota(jnp.int32, (1, D), 1)
    lane = lax.broadcasted_iota(jnp.int32, (1, HALF), 1)
    third = jnp.where(lane >= 128, 1, 0) + jnp.where(lane >= 256, 1, 0)
    within = lane - 128 * third
    second = jnp.where(within >= HEAD_DIM, 1, 0)
    head = jnp.where(second == 1, head_b, head_a)
    column = 192 * head + HEAD_DIM * third + (within - HEAD_DIM * second)
    for layer in range(LAYERS):
        shards = [vectors[layer, i].astype(F32) for i in range(N)]

        def row(r):
            return jnp.concatenate([one_shard[r : r + 1] for one_shard in shards], axis=0)

        rows_out[layer, 0:1] = place(row(2), lanes, D, 96)
        rows_out[layer, 1:2] = place(row(3), lanes, D, 96)
        rows_out[layer, 2:3] = place(row(4), lanes, D, 96) + place(row(5), lanes, D, 96)
        rows_out[layer, 3:4, pl.ds(0, HALF)] = place(row(0), column, HALF, 288)
        rows_out[layer, 3:4, pl.ds(HALF, HALF)] = vectors[layer, c].astype(F32)[1:2]
        rows_out[layer, 4:8] = jnp.zeros((4, D), F32)


def prepare(marks, vectors):
    return pl.pallas_call(
        prepare_kernel,
        out_shape=(
            jax.ShapeDtypeStruct((3, SEQ, 128), F32),
            jax.ShapeDtypeStruct((SEQ, 128), F32),
            jax.ShapeDtypeStruct((LAYERS, 8, D), F32),
        ),
        in_specs=[VMEM] * 2,
        out_specs=[VMEM] * 3,
        compiler_params=pltpu.CompilerParams(vmem_limit_bytes=48 * 1024 * 1024),
    )(marks, vectors)


BLOCK = 256
BLOCKS = SEQ // BLOCK


def unit_rows(b):
    s = lax.axis_index("ctx") % 2
    start = jnp.where(b < BLOCKS, b * BLOCK, s * (SEQ // 2) + (b - BLOCKS) * BLOCK)
    start = pl.multiple_of(start, BLOCK)
    lanes = lax.broadcasted_iota(jnp.int32, (BLOCK, 2 * HEAD_DIM), 1) // HEAD_DIM
    return start, lanes == jnp.where(b < BLOCKS, 0, 1)


def mix_rows(pieces, w_mix):
    for h in range(2):
        cols = pl.ds(HALF * h, HALF)
        rows = [pieces[h, j, pl.ds(0, 16)].astype(F32) for j in range(N)]
        heads = [r[:8] for r in rows] + [r[8:] for r in rows]
        w_mix[pl.ds(0, 128), cols] = jnp.concatenate(heads, axis=0).astype(BF)
        for j in range(N):
            w_mix[pl.ds(128 + 48 * j, 48), cols] = pieces[h, j, pl.ds(16, 48)]


def forward_steps(
    unit, vectors, w_cat, pieces, col, row, tables,
    branch, normed, query, key, value, slope, mixed, lse, w_mix, turned,
):
    mix_rows(pieces, w_mix)

    @pl.loop(0, BLOCKS)
    def _(i):
        rows = pl.ds(pl.multiple_of(i * BLOCK, BLOCK), BLOCK)
        low = (unit[rows].astype(F32) * vectors[0:1] + vectors[1:2]).astype(BF)
        normed[rows] = low
        heads = dot(low, w_cat[0], ((1,), (0,))) + vectors[3:4, :HALF]

        def rotate(values):
            return (
                values * tables[0, rows]
                + pltpu.roll(values, 8, axis=1) * tables[1, rows]
                + pltpu.roll(values, 120, axis=1) * tables[2, rows]
            )

        query[rows] = (rotate(heads[:, :128]) * HEAD_DIM ** (-0.5)).astype(BF)
        key[rows] = rotate(heads[:, 128:256]).astype(BF)
        value[rows] = heads[:, 256:].astype(BF)
        pre = dot(low, w_cat[1], ((1,), (0,))) + vectors[3:4, HALF:]
        cdf = 0.5 * (1.0 + lax.erf(pre * 0.5**0.5))
        mixed[rows, pl.ds(128, HALF)] = (pre * cdf).astype(BF)
        mixed[rows, pl.ds(0, 128)] = jnp.zeros((BLOCK, 128), BF)
        slope[rows] = cdf + pre * (jnp.exp(-0.5 * pre * pre) * 0.3989422804014327)

    turned[...] = value[...].astype(F32).T.astype(BF)
    yield
    for n in range(3):

        @pl.loop(2 * n, 2 * n + 2)
        def _(b):
            start, mask = unit_rows(b)
            rows = pl.ds(start, BLOCK)
            q = jnp.where(mask, query[rows].astype(F32), 0.0).astype(BF)
            scores = dot(key[...], q, ((1,), (1,)))
            seen = jnp.concatenate([col[...], col[...]], axis=1) <= row[pl.ds(start // BLOCK, 1)]
            scores = jnp.where(seen, scores, -jnp.inf)
            top = jnp.max(scores, axis=0, keepdims=True)
            expos = jnp.exp(scores - top)
            total = jnp.sum(expos, axis=0, keepdims=True)
            lse[pl.ds(b, 1)] = top + jnp.log(total)
            probs = (expos * (1.0 / total)).astype(BF)
            out = dot(turned[...], probs, ((1,), (0,))).T
            mixed[rows, pl.ds(0, 128)] = jnp.where(mask, out, mixed[rows, pl.ds(0, 128)].astype(F32)).astype(BF)

        yield
    for i in range(N):
        rows = pl.ds(i * TOK, TOK)
        branch[i] = dot(mixed[rows], w_mix[...], ((1,), (0,))).astype(BF)


def forward_shapes():
    shape = jax.ShapeDtypeStruct
    return (
        shape((N, TOK, D), BF),
        shape((SEQ, D), BF),
        shape((SEQ, 128), BF),
        shape((SEQ, 128), BF),
        shape((SEQ, 128), BF),
        shape((SEQ, HALF), F32),
        shape((SEQ, 512), BF),
        shape((8, BLOCK), F32),
        shape((512, D), BF),
    )


FORWARDS = 9


def local_params():
    return pltpu.CompilerParams(vmem_limit_bytes=56 * 1024 * 1024)


def forward_kernel(*refs):
    run(forward_steps(*refs))


def forward(*args):
    return pl.pallas_call(
        forward_kernel,
        out_shape=forward_shapes(),
        in_specs=[VMEM] * len(args),
        out_specs=[VMEM] * FORWARDS,
        scratch_shapes=[pltpu.VMEM((128, SEQ), BF)],
        compiler_params=local_params(),
    )(*args)


def forward_between_kernel(*refs):
    args, (x, cot, src), refs = refs[:7], refs[7:10], refs[10:]
    outs, refs = refs[:FORWARDS], refs[FORWARDS:]
    (x_next, unit_all, low_all, cols_all, pieces_all), refs = refs[:5], refs[5:]
    turned, unit, low_g, scratch, rest = refs[0], refs[1], refs[2], refs[3:6], refs[6:]
    buffers, rest = rest[:SCRATCHES], rest[SCRATCHES:]
    lane, lane_u, lane_g, lane_w, lane_z = (Lane(rest[2 * i : 2 * i + 2]) for i in range(5))
    own, keeps = rest[10], rest[11]
    ctx, fsdp = Group("ctx"), Group("fsdp")
    cs = others("ctx", lax.axis_index("ctx"))
    core = {"dp": 1 - lax.axis_index("dp")}
    meet(fsdp.neighbours() + cs + [core])
    kept = []
    branch, vectors = outs[0], args[1]

    def tokens():
        yield from forward_steps(*args, *outs, turned)

        def take(total):
            x_next[...] = x[...] + (total + vectors[2:3])

        yield from scatter_steps(lane, ctx, branch, TOK // 2, TOK, buffers, take)
        unit[...] = normalize(x_next[...])[0].astype(BF)
        keep = pltpu.make_async_copy(unit, unit_all.at[ctx.slot(0, 0)], keeps.at[0])
        keep.start()
        kept.append(keep)
        yield from gather_steps(lane_u, ctx, unit, lambda slot: unit_all.at[slot], TOK // 2, TOK)

    def later():
        low_g[...] = cot[...].astype(BF)
        keep = pltpu.make_async_copy(low_g, low_all.at[ctx.slot(0, 0)], keeps.at[1])
        keep.start()
        kept.append(keep)
        yield from gather_steps(lane_g, ctx, low_g, lambda slot: low_all.at[slot], TOK // 2, TOK)

    outs_w = (cols_all, pieces_all)
    run(
        shard_steps(lane_w, lane_z, fsdp, cs, core, src, CUT, ROWS, scratch, outs_w, own, kept),
        later(),
        tokens(),
    )
    for each in (lane, lane_u, lane_g, lane_w, lane_z):
        each.finish()
    for copy in kept:
        copy.wait()


def forward_between(args, x, cot, src, collective_id):
    tokens = jax.ShapeDtypeStruct((N, TOK, D), BF)
    return pl.pallas_call(
        forward_between_kernel,
        out_shape=forward_shapes()
        + (jax.ShapeDtypeStruct((TOK, D), F32), tokens, tokens, COLS_SHAPE, PIECES_SHAPE),
        in_specs=[VMEM] * 9 + [ANY],
        out_specs=[VMEM] * (FORWARDS + 1) + [ANY] * 4,
        scratch_shapes=[
            pltpu.VMEM((128, SEQ), BF),
            pltpu.VMEM((TOK, D), BF),
            pltpu.VMEM((TOK, D), BF),
        ]
        + shard_scratch(ROWS)
        + scatter_scratch(TOK, TOK // 2, D)
        + sems(SCATTERS)
        + sems(GATHERS)
        + sems(GATHERS)
        + sems(SHARD_LANE)
        + sems(GATHERS)
        + [pltpu.SemaphoreType.DMA((4,)), pltpu.SemaphoreType.DMA((2,))],
        compiler_params=params(collective_id),
    )(*args, x, cot, src)


BACK_ARGS = 12


def backward_scratch():
    return [
        pltpu.VMEM((SEQ, 128), BF),
        pltpu.VMEM((SEQ, D), BF),
        pltpu.VMEM((SEQ, 128), F32),
        pltpu.VMEM((SEQ, 128), F32),
        pltpu.VMEM((SEQ, 128), F32),
        pltpu.VMEM((128, SEQ), BF),
        pltpu.VMEM((D, D), F32),
        pltpu.VMEM((N, TOK, D), BF),
        pltpu.VMEM((2, N, 96, HALF), BF),
        pltpu.VMEM((2, N, PIECE, HALF), BF),
    ]


BACKS = 10


def backward_steps(
    ready, low, w_cat, normed, query, key, value, slope, mixed, lse, w_mix, col, row, tables, grad_b,
    grad_att, grad_pre, dq, dk, dv, turned, big, grad_normed, part_a, part_b,
):
    @pl.loop(0, 2)
    def _(i):
        cols = pl.ds(pl.multiple_of(i * BLOCK, BLOCK), BLOCK)
        big[cols] = dot(mixed[:, cols], low[...], ((0,), (0,)))

    for j in range(N):
        for h in range(2):
            at = slice(HALF * h, HALF * h + HALF)
            first = big[8 * j : 8 * j + 8, at]
            second = big[64 + 8 * j : 64 + 8 * j + 8, at]
            part_b[h, j, pl.ds(0, 16)] = jnp.concatenate([first, second], axis=0).astype(BF)
            part_b[h, j, pl.ds(16, 48)] = big[128 + 48 * j : 176 + 48 * j, at].astype(BF)
    ready.add("b")
    yield

    @pl.loop(0, BLOCKS)
    def _(i):
        rows = pl.ds(pl.multiple_of(i * BLOCK, BLOCK), BLOCK)
        back = dot(low[rows], w_mix[...], ((1,), (1,)))
        grad_att[rows] = back[:, :128].astype(BF)
        grad_pre[rows, pl.ds(HALF, HALF)] = (back[:, 128:] * slope[rows]).astype(BF)

    turned[...] = key[...].astype(F32).T.astype(BF)
    dq[...] = jnp.zeros((SEQ, 128), F32)
    dk[...] = jnp.zeros((SEQ, 128), F32)
    dv[...] = jnp.zeros((SEQ, 128), F32)
    yield
    for n in range(3):

        @pl.loop(2 * n, 2 * n + 2)
        def _(b):
            start, mask = unit_rows(b)
            rows = pl.ds(start, BLOCK)
            q = jnp.where(mask, query[rows].astype(F32), 0.0).astype(BF)
            g = jnp.where(mask, grad_att[rows].astype(F32), 0.0).astype(BF)
            scores = dot(key[...], q, ((1,), (1,)))
            seen = jnp.concatenate([col[...], col[...]], axis=1) <= row[pl.ds(start // BLOCK, 1)]
            probs = jnp.exp(jnp.where(seen, scores, -jnp.inf) - lse[pl.ds(b, 1)])
            grad_probs = dot(value[...], g, ((1,), (1,)))
            mean = jnp.sum(probs * grad_probs, axis=0, keepdims=True)
            grad_scores = (probs * (grad_probs - mean)).astype(BF)
            dq[rows] = jnp.where(mask, dot(turned[...], grad_scores, ((1,), (0,))).T, dq[rows])
            dk[...] += dot(grad_scores, q, ((1,), (0,)))
            dv[...] += dot(probs.astype(BF), g, ((1,), (0,)))

        yield
    grad_b[...] = jnp.zeros((1, D), F32)

    @pl.loop(0, N)
    def _(i):
        rows = pl.ds(pl.multiple_of(i * TOK, TOK), TOK)

        def rotate_back(grads):
            return (
                grads * tables[0, rows]
                + pltpu.roll(grads * tables[1, rows], 120, axis=1)
                + pltpu.roll(grads * tables[2, rows], 8, axis=1)
            )

        grad_pre[rows, pl.ds(0, 128)] = rotate_back(dq[rows] * HEAD_DIM ** (-0.5)).astype(BF)
        grad_pre[rows, pl.ds(128, 128)] = rotate_back(dk[rows]).astype(BF)
        grad_pre[rows, pl.ds(256, 128)] = dv[rows].astype(BF)
        block = grad_pre[rows]
        grad_b[...] += jnp.sum(block.astype(F32), axis=0, keepdims=True)
        grad_normed[i] = (
            dot(block[:, :HALF], w_cat[0], ((1,), (1,))) + dot(block[:, HALF:], w_cat[1], ((1,), (1,)))
        ).astype(BF)

    ready.add("normed")
    yield

    @pl.loop(0, D // BLOCK)
    def _(i):
        cols = pl.ds(pl.multiple_of(i * BLOCK, BLOCK), BLOCK)
        big[cols] = dot(normed[:, cols], grad_pre[...], ((0,), (0,)))

    for f in range(N):
        for h in range(2):
            part_a[h, f] = big[96 * f : 96 * f + 96, HALF * h : HALF * h + HALF].astype(BF)
    ready.add("a")


def grads_scratch():
    return [
        pltpu.VMEM((N, 96, HALF), BF),
        pltpu.VMEM((N, PIECE, HALF), BF),
        pltpu.VMEM((N, PIECE, HALF), BF),
        pltpu.VMEM((N, ROWS, HALF), BF),
    ] + scatter_scratch(ROWS, CUT, HALF)


GRADS = 4 + SCRATCHES


def grads_steps(ready, lane, lane_z, fsdp, cs, core, part_a, part_b, scratch, take):
    their_a, their_b, got, blocks = scratch[:4]
    c, k = lax.axis_index("ctx"), lax.axis_index("dp")
    while "b" not in ready:
        yield
    first_b = lane.go(part_b.at[1 - k], their_b, core)
    yield
    first_b.wait_recv()
    for i in range(N):
        their_b[i] = (part_b[k, i].astype(F32) + their_b[i].astype(F32)).astype(BF)
    turn = [lane.go(their_b.at[peer["ctx"]], got.at[c], peer) for peer in cs]
    got[c] = their_b[c]
    while "a" not in ready:
        yield
    first_a = lane.go(part_a.at[1 - k], their_a, core)
    for copy in turn:
        copy.wait_recv()
    low = lax.broadcasted_iota(jnp.int32, (16, HALF), 0) < 8
    for i in range(N):
        rows = got[i, pl.ds(0, 16)].astype(F32)
        pair = got[i + 1 - 2 * (i % 2), pl.ds(0, 16)].astype(F32)
        blocks[i, pl.ds(96, 16)] = jnp.where(low, rows, rows + pair).astype(BF)
        blocks[i, pl.ds(112, 48)] = got[i, pl.ds(16, 48)]
    yield
    first_a.wait_recv()
    for i in range(N):
        blocks[i, pl.ds(0, 96)] = (part_a[k, i].astype(F32) + their_a[i].astype(F32)).astype(BF)
    yield from scatter_steps(lane_z, fsdp, blocks, CUT, ROWS, scratch[4:], take)


def turn_kernel(*refs):
    (low, *args), refs = refs[:13], refs[13:]
    (x, grad, vectors, out_parts, bias), refs = refs[:5], refs[5:]
    (outputs, grad_next, low_all, vecs, share), refs = refs[:5], refs[5:]
    (low_g, grad_b), refs = refs[:2], refs[2:]
    back, refs = refs[:BACKS], refs[BACKS:]
    buffers, refs = refs[:SCRATCHES], refs[SCRATCHES:]
    buffers_o, refs = refs[:SCRATCHES], refs[SCRATCHES:]
    scratch, rest = refs[:GRADS], refs[GRADS:]
    lane, lane_g, lane_w, lane_z, lane_o = (Lane(rest[2 * i : 2 * i + 2]) for i in range(5))
    keep_sem = rest[10]
    ctx, fsdp = Group("ctx"), Group("fsdp")
    cs = others("ctx", lax.axis_index("ctx"))
    core = {"dp": 1 - lax.axis_index("dp")}
    meet(cs + fsdp.neighbours() + [core])
    kept, ready = [], set()

    def tokens():
        def take(total):
            back_, grad_gain, grad_shift = norm_back(x[...], total, vectors[0:1])
            grad_next[...] = grad[...] + back_
            rounded = grad[...].astype(BF).astype(F32)
            vecs[pl.ds(0, 1)] = jnp.sum(rounded, axis=0, keepdims=True)
            vecs[pl.ds(1, 1)] = grad_gain
            vecs[pl.ds(2, 1)] = grad_shift
            vecs[pl.ds(3, 1)] = grad_b[...]
            vecs[pl.ds(4, 4)] = jnp.zeros((4, D), F32)

        while "normed" not in ready:
            yield
        yield from scatter_steps(lane, ctx, back[7], TOK // 2, TOK, buffers, take)
        low_g[...] = grad_next[...].astype(BF)
        keep = pltpu.make_async_copy(low_g, low_all.at[ctx.slot(0, 0)], keep_sem)
        keep.start()
        kept.append(keep)
        yield from gather_steps(lane_g, ctx, low_g, lambda slot: low_all.at[slot], TOK // 2, TOK)

    def weights():
        def take(total):
            share[...] = total.astype(BF)

        yield from grads_steps(ready, lane_w, lane_z, fsdp, cs, core, back[8], back[9], scratch, take)

    def ends():
        def take(total):
            outputs[...] = x[...] + (total + bias[2:3])

        yield from scatter_steps(lane_o, ctx, out_parts, TOK // 2, TOK, buffers_o, take)

    run(ends(), backward_steps(ready, low, *args, grad_b, *back), tokens(), weights())
    for each in (lane, lane_g, lane_w, lane_z, lane_o):
        each.finish()
    for copy in kept:
        copy.wait()


def turn(args, x, grad, vectors, out_parts, collective_id):
    tokens = jax.ShapeDtypeStruct((TOK, D), F32)
    return pl.pallas_call(
        turn_kernel,
        out_shape=(
            tokens,
            tokens,
            jax.ShapeDtypeStruct((N, TOK, D), BF),
            jax.ShapeDtypeStruct((8, D), F32),
            jax.ShapeDtypeStruct((ROWS, HALF), BF),
        ),
        in_specs=[VMEM] * 18,
        out_specs=(VMEM, VMEM, ANY, VMEM, VMEM),
        scratch_shapes=[pltpu.VMEM((TOK, D), BF), pltpu.VMEM((1, D), F32)]
        + backward_scratch()
        + scatter_scratch(TOK, TOK // 2, D)
        + scatter_scratch(TOK, TOK // 2, D)
        + grads_scratch()
        + sems(SCATTERS)
        + sems(GATHERS)
        + sems(2 + N - 1)
        + sems(SCATTERS)
        + sems(SCATTERS)
        + [pltpu.SemaphoreType.DMA],
        compiler_params=params(collective_id),
    )(*args, x, grad, vectors, out_parts, vectors)


FIRST_ROWS = ROWS + 16


def last_kernel(*refs):
    (low, *args), refs = refs[:13], refs[13:]
    (x, grad, vectors, vecs, share), refs = refs[:5], refs[5:]
    (grad_next, out_first, out_last), refs = refs[:3], refs[3:]
    (both, v_mine, v_their, v_all, grad_b), refs = refs[:5], refs[5:]
    back, refs = refs[:BACKS], refs[BACKS:]
    buffers, refs = refs[:SCRATCHES], refs[SCRATCHES:]
    scratch, rest = refs[:GRADS], refs[GRADS:]
    lane, lane_w, lane_z, lane_v, lane_x, lane_s = (Lane(rest[2 * i : 2 * i + 2]) for i in range(6))
    keeps = rest[12]
    c, f, k = lax.axis_index("ctx"), lax.axis_index("fsdp"), lax.axis_index("dp")
    ctx, fsdp = Group("ctx"), Group("fsdp")
    cs, fs = others("ctx", c), others("fsdp", f)
    core = {"dp": 1 - k}
    meet(cs + fs + [core])
    ready = set()

    def tokens():
        def take(total):
            back_, grad_gain, grad_shift = norm_back(x[...], total, vectors[0:1])
            grad_next[...] = grad[...] + back_
            rounded = grad[...].astype(BF).astype(F32)
            branch = jnp.sum(rounded, axis=0, keepdims=True)
            mine = [vecs[...], branch, grad_gain, grad_shift, grad_b[...], jnp.zeros((4, D), F32)]
            mine = jnp.concatenate(mine, axis=0)
            v_mine[0] = mine[:, :HALF].astype(BF)
            v_mine[1] = mine[:, HALF:].astype(BF)

        while "normed" not in ready:
            yield
        yield from scatter_steps(lane, ctx, back[7], TOK // 2, TOK, buffers, take)
        cross = lane_v.go(v_mine.at[1 - k], v_their, core)
        yield
        cross.wait_recv()
        v_all[f] = (v_mine[k].astype(F32) + v_their[...].astype(F32)).astype(BF)
        copies = [lane_v.go(v_all.at[f], v_all.at[f], peer) for peer in fs]
        yield
        for copy in copies:
            copy.wait_recv()
        total = v_all[0].astype(F32)
        for i in range(1, N):
            total = total + v_all[i].astype(F32)
        both[pl.ds(ROWS, 16)] = total.astype(BF)

    def weights():
        def take(total):
            both[pl.ds(0, ROWS)] = total.astype(BF)

        yield from grads_steps(ready, lane_w, lane_z, fsdp, cs, core, back[8], back[9], scratch, take)

    kept = []

    def older():
        keep = pltpu.make_async_copy(share, out_last.at[k, c], keeps.at[0])
        keep.start()
        kept.append(keep)
        yield from gather_steps(lane_s, ctx, share, lambda slot: out_last.at[k, slot], CUT, ROWS)
        keep.wait()
        copy = lane_s.go(out_last.at[k], out_last.at[k], core)
        yield
        copy.wait_recv()

    run(older(), backward_steps(ready, low, *args, grad_b, *back), tokens(), weights())
    keep = pltpu.make_async_copy(both, out_first.at[k, c], keeps.at[1])
    keep.start()
    run(gather_steps(lane_x, ctx, both, lambda slot: out_first.at[k, slot], W_CUT, FIRST_ROWS))
    keep.wait()
    lane_x.go(out_first.at[k], out_first.at[k], core).wait_recv()
    for each in (lane, lane_w, lane_z, lane_v, lane_x, lane_s):
        each.finish()


def last(args, x, grad, vectors, vecs, share, collective_id):
    return pl.pallas_call(
        last_kernel,
        out_shape=(
            jax.ShapeDtypeStruct((TOK, D), F32),
            jax.ShapeDtypeStruct((2, N, FIRST_ROWS, HALF), BF),
            jax.ShapeDtypeStruct((2, N, ROWS, HALF), BF),
        ),
        in_specs=[VMEM] * 18,
        out_specs=(VMEM, ANY, ANY),
        scratch_shapes=[
            pltpu.VMEM((FIRST_ROWS, HALF), BF),
            pltpu.VMEM((2, 16, HALF), BF),
            pltpu.VMEM((16, HALF), BF),
            pltpu.VMEM((N, 16, HALF), BF),
            pltpu.VMEM((1, D), F32),
        ]
        + backward_scratch()
        + scatter_scratch(TOK, TOK // 2, D)
        + grads_scratch()
        + sems(SCATTERS)
        + sems(2 + N - 1)
        + sems(SCATTERS)
        + sems(N)
        + sems(GATHERS + 1)
        + sems(GATHERS + 1)
        + [pltpu.SemaphoreType.DMA((2,))],
        compiler_params=params(collective_id),
    )(*args, x, grad, vectors, vecs, share)


def spread_kernel(got_first, got_last, g_qkv, g_out, g_up, g_down):
    odd = lax.axis_index("fsdp") % 2
    for layer in range(LAYERS):
        got, base = (got_first, got_last)[layer], 0

        def heads(i, got=got, base=base):
            return got[0, i, pl.ds(base, 96)].astype(F32)

        chunks = []
        for p in range(4):
            one, two = heads(2 * p), heads(2 * p + 1)
            both = one + two
            for values, lane in ((one, 0), (both, HEAD_DIM), (two, 0)):
                chunks += [values[:, 128 * i + lane : 128 * i + lane + HEAD_DIM] for i in range(3)]
        for i in range(len(chunks) // 2):
            g_qkv[layer, :, pl.ds(128 * i, 128)] = jnp.concatenate(chunks[2 * i : 2 * i + 2], axis=1)
        for i in range(N):
            g_up[layer, :, pl.ds(HALF * i, HALF)] = got[1, i, pl.ds(base, 96)].astype(F32)
            for h in range(2):
                cols = pl.ds(HALF * h, HALF)
                g_down[layer, pl.ds(48 * i, 48), cols] = got[h, i, pl.ds(base + 112, 48)].astype(F32)
        for h in range(2):
            cols = pl.ds(HALF * h, HALF)
            rows = [got[h, i, pl.ds(base + 96, 16)].astype(F32) for i in range(N)]
            first = [r[:8] for r in rows]
            even = jnp.concatenate(first + [r[8:] for r in rows[:4]], axis=0)
            uneven = jnp.concatenate([r[8:] for r in rows[4:]] + first, axis=0)
            g_out[layer, :, cols] = jnp.where(odd == 0, even, uneven)


def spread(got_first, got_last):
    shape = jax.ShapeDtypeStruct
    return pl.pallas_call(
        spread_kernel,
        out_shape=(
            shape((LAYERS, 96, 3 * D), F32),
            shape((LAYERS, 96, D), F32),
            shape((LAYERS, 96, FF), F32),
            shape((LAYERS, HALF, D), F32),
        ),
        in_specs=[VMEM] * 2,
        out_specs=[VMEM] * 4,
        compiler_params=local_params(),
    )(got_first, got_last)


def body(
    inputs, positions, cotangent, w_qkv, b_qkv, w_out, b_out, w_up, b_up, w_down, b_down, ln_gain, ln_bias
):
    c = lax.axis_index("ctx")
    p, s = c // 2, lax.rem(c, 2)
    head_a, head_b = 3 * p + 2 * s, 3 * p + 1

    def heads_cols(w):
        grouped = w.reshape(w.shape[:-1] + (12, 3, HEAD_DIM))
        axis = grouped.ndim - 3
        both = jnp.concatenate(
            [
                lax.dynamic_slice_in_dim(grouped, head_a, 1, axis=axis),
                lax.dynamic_slice_in_dim(grouped, head_b, 1, axis=axis),
            ],
            axis=axis,
        )
        return jnp.swapaxes(both, axis, axis + 1).reshape(w.shape[:-1] + (HALF,))

    def hidden_cols(w):
        return lax.dynamic_slice_in_dim(w, c * HALF, HALF, axis=w.ndim - 1)

    f = lax.axis_index("fsdp")
    f_s = lax.rem(f, 2)

    def piece(w, start, count):
        return lax.dynamic_slice_in_dim(w, start, count, axis=1)

    cols = jnp.concatenate([heads_cols(w_qkv), hidden_cols(w_up)], axis=-1)
    first_rows = piece(w_out, jnp.where(f_s == 0, 0, 32) + 8 * c, 8)
    shared_rows = piece(w_out, jnp.where(f_s == 0, 64, -32) + 8 * jnp.where(f_s == 0, c % 4, c), 8)
    down_rows = piece(w_down, 48 * c, 48)
    by_layer = jnp.concatenate([cols, first_rows, shared_rows, down_rows], axis=1)
    def wide(vector):
        return jnp.pad(vector, ((0, 0), (0, HALF - vector.shape[1])))

    vec = jnp.stack([wide(v) for v in (b_qkv, b_up, ln_gain, ln_bias, b_out, b_down)], axis=1)
    vec = jnp.pad(vec, ((0, 0), (0, 10), (0, 0)))
    src = [jnp.stack([one[:, :HALF], one[:, HALF:]]) for one in (by_layer[0], by_layer[1])]
    src[0] = jnp.concatenate([src[0], vec], axis=1)
    stream, cot = inputs[0], cotangent[0]
    cols, pieces, vec_all, marks, unit = gather_weights(src[0], marks_of(positions), stream, 1)
    tables, col, vectors = prepare(marks, vec_all)
    row = marks[:, 16].reshape(BLOCKS, BLOCK)
    w_first = cols.reshape(2, D, HALF)
    branch, *kept_first, x_last, unit, low_last, cols, pieces_last = forward_between(
        (unit.reshape(SEQ, D), vectors[0], w_first, pieces, col, row, tables), stream, cot, src[1], 2
    )
    w_last = cols.reshape(2, D, HALF)
    branch, *kept_last = forward(
        unit.reshape(SEQ, D), vectors[1], w_last, pieces_last, col, row, tables
    )
    outputs, grad, low, vecs, share = turn(
        (low_last.reshape(SEQ, D), w_last, *kept_last, col, row, tables), x_last, cot, vectors[1], branch, 3
    )
    grad, got_first, got_last = last(
        (low.reshape(SEQ, D), w_first, *kept_first, col, row, tables), stream, grad, vectors[0], vecs, share, 4
    )
    g_qkv, g_out, g_up, g_down = spread(got_first, got_last)

    rows = jnp.concatenate([got_first[0, :, ROWS:], got_first[1, :, ROWS:]], axis=-1).astype(F32)
    summed = jnp.sum(rows, axis=0)

    def cut(vector, width):
        return lax.dynamic_slice_in_dim(vector, f * width, width, axis=vector.ndim - 1)

    def own_vectors(biases):
        qkv = biases[:, :HALF].reshape(4, 2, 3, 2, HEAD_DIM)
        shared = qkv[:, 0, :, 1] + qkv[:, 1, :, 1]
        qkv = jnp.stack([qkv[:, 0, :, 0], shared, qkv[:, 1, :, 0]], axis=1).reshape(3 * D)
        up = lax.dynamic_index_in_dim(biases[:, HALF:], f, axis=0, keepdims=False)
        return cut(qkv, 288), up

    pairs = [own_vectors(rows[:, 11]), own_vectors(rows[:, 3])]
    g_b_qkv = jnp.stack([pair[0] for pair in pairs])
    g_b_up = jnp.stack([pair[1] for pair in pairs])
    g_branch, g_gain, g_shift = (cut(jnp.stack([summed[8 + i], summed[i]]), 96) for i in range(3))
    return (
        outputs[None], grad[None], g_qkv, g_b_qkv, g_out, g_branch, g_up, g_b_up, g_down, g_branch, g_gain, g_shift,
    )


def solution(mesh):
    seqs = ("dp", "fsdp")
    whole = P(None, "fsdp", None)
    row = P(None, "fsdp")
    in_specs = (
        P(seqs, "ctx", None), P(seqs, "ctx"), P(seqs, "ctx", None),
        whole, row, whole, row, whole, row, whole, row, row, row,
    )
    out_specs = (
        P(seqs, "ctx", None), P(seqs, "ctx", None),
        whole, row, whole, row, whole, row, whole, row, row, row,
    )
    return jax.shard_map(body, mesh=mesh, in_specs=in_specs, out_specs=out_specs, check_vma=False)
```

time: 300 us -> 265 us (0.88)
  local copies, waits for them, and re-layouts: 31.8 us -> 12.6 us
  Pallas kernels: 259 us -> 246 us
    unnamed x49 -> x40, local copies, waits for them, and re-layouts: 18.8 us -> 7.62 us
    pallas_call x1, Pallas kernels: 45.6 us -> 35.9 us  [gather_weights(): pl.pallas_call(weights_kernel, out_shape=(COLS_SHAPE, PIECES_SHAPE, jax.S...]
    pallas_call x8 -> x5, Pallas kernels: 210 us -> 204 us  [the longest x1 69.6 us: last(): pl.pallas_call(last_kernel, out_shape=(jax.ShapeDtypeStruct((TOK, D), F32...]
where the time goes in v3:
time: 265 us; the launch traced here: 264 us
  Pallas kernels  246 us (93%)
  local copies, waits for them, and re-layouts  12.6 us (5%)
  other arithmetic  4.9 us (2%)
    pallas_call x1, Pallas kernels, last(): pl.pallas_call(last_kernel, out_shape=(jax.ShapeDtypeStruct((TOK, D), F32...  69.6 us
    pallas_call x1, Pallas kernels, turn(): pl.pallas_call(turn_kernel, out_shape=(tokens, tokens, jax.ShapeDtypeStru...  63.9 us
    pallas_call x1, Pallas kernels, forward_between(): pl.pallas_call(forward_between_kernel, out_shape=forward_shapes() + (jax....  55.8 us
    pallas_call x1, Pallas kernels, gather_weights(): pl.pallas_call(weights_kernel, out_shape=(COLS_SHAPE, PIECES_SHAPE, jax.S...  35.9 us
    pallas_call x1, Pallas kernels, forward(): pl.pallas_call(forward_kernel, out_shape=forward_shapes(), in_specs=[VMEM...  13.9 us
    unnamed x40, local copies, waits for them, and re-layouts  7.62 us
    pallas_call x1, Pallas kernels, spread(): pl.pallas_call(spread_kernel, out_shape=(shape((LAYERS, 96, 3 * D), F32),...  5.64 us

profile of v3, /device:TPU:1, one launch (start us, length us, event | category | flops | bytes accessed | tf_op | source)
XLA Modules:
  0.0 264.3 jit_solution(15603873663882674661)
XLA Ops:
  0.7 1.7 copy.34
  2.7 0.8 constant_dynamic-slice_fusion.4
  3.6 0.9 constant_dynamic-slice_fusion.5
  5.0 0.7 fusion.1.src
  5.8 0.6 pad_maximum_fusion.4.places
  6.5 35.9 %shard_map.220 = (bf16[2,8,96,384]{3,2,1,0:T(8,128)(2,1)}, bf16[2,8,64,384]{3,2,1,0:T(8,128)(2,1)}, bf16[2,8,16,384]{3,2,1,0:T(8,128)(2,1)}, f32[8,24,128]{2,1,0:T(8,128)}, bf16[8,128,768]{2,1,0:T(8,128)(2,1)}) custom-call(bf16[2,176,384]{2,1,0:T(8,128)(2,1)} %fusion.1.src, f32[24,128]{1,0:T(8,128)} %pad_maximum_fusion.4.places, f32[128,768]{1,0:T(8,128)} %bitcast.73), custom_call_target="tpu_custom_call" | custom-call | tf_op jit(solution)/shard_map/pallas_call | solution.py:306
  42.4 0.9 copy-done.3
  43.3 0.9 copy-done.4
  44.2 0.9 shard_map.221
  45.1 1.1 copy-done.1
  46.3 0.8 copy-done.2
  47.1 0.6 slice_bitcast_fusion.8
  47.7 0.6 reshape_squeeze.3.refs_5_.refs_11_
  48.3 0.7 pad_maximum_fusion.1.refs_9_
  49.0 55.8 %shard_map.222 = (bf16[8,128,768]{2,1,0:T(8,128)(2,1)}, bf16[1024,768]{1,0:T(8,128)(2,1)}, bf16[1024,128]{1,0:T(8,128)(2,1)}, bf16[1024,128]{1,0:T(8,128)(2,1)},...) custom-call(bf16[1024,768]{1,0:T(8,128)(2,1)} %bitcast.77, ...), custom_call_target="tpu_custom_call" | custom-call | tf_op jit(solution)/shard_map/pallas_call | solution.py:559
  104.8 13.9 %shard_map.223 = (bf16[8,128,768]{2,1,0:T(8,128)(2,1)}, bf16[1024,768]{1,0:T(8,128)(2,1)}, bf16[1024,128]{1,0:T(8,128)(2,1)}, bf16[1024,128]{1,0:T(8,128)(2,1)},...) custom-call(bf16[1024,768]{1,0:T(8,128)(2,1)} %bitcast.78, ...), custom_call_target="tpu_custom_call" | custom-call | tf_op jit(solution)/shard_map/pallas_call | solution.py:500
  118.7 63.9 %shard_map.224 = (f32[128,768]{1,0:T(8,128)}, f32[128,768]{1,0:T(8,128)}, bf16[8,128,768]{2,1,0:T(8,128)(2,1)}, f32[8,768]{1,0:T(8,128)}, bf16[160,384]{1,0:T(8,128)(2,1)}) custom-call(bf16[1024,768]{1,0:T(8,128)(2,1)} %bitcast.79, bf16[2,768,384]{2,1,0:T(8,128)(2,1)} %bitcast.72, bf16[1024,768]{1,0:T(8,128)(2,1)} %get-tuple-element.66.refs_2_, ...), custom_call_target="tpu_custom_call" | custom-call | tf_op jit(solution)/shard_map/pallas_call | solution.py:789
  182.6 69.6 %shard_map.225 = (f32[128,768]{1,0:T(8,128)}, bf16[2,8,176,384]{3,2,1,0:T(8,128)(2,1)}, bf16[2,8,160,384]{3,2,1,0:T(8,128)(2,1)}) custom-call(bf16[1024,768]{1,0:T(8,128)(2,1)} %bitcast.80, bf16[2,768,384]{2,1,0:T(8,128)(2,1)} %bitcast.70, bf16[1024,768]{1,0:T(8,128)(2,1)} %get-tuple-element.78.refs_2_, bf16[1024,128]{1,0:T(8,128)(2,1)} %get-tuple-element.79.refs_3_, ...), custom_call_target="tpu_custom_call" | custom-call | tf_op jit(solution)/shard_map/pallas_call | solution.py:891
  252.2 1.0 slice_bitcast_fusion.7
  253.2 0.6 fusion.5
  253.9 0.6 fusion.6
  256.6 5.6 %shard_map.226 = (f32[2,96,2304]{2,1,0:T(8,128)}, f32[2,96,768]{2,1,0:T(8,128)}, f32[2,96,3072]{2,1,0:T(8,128)}, f32[2,384,768]{2,1,0:T(8,128)}) custom-call(bf16[2,8,176,384]{3,2,1,0:T(8,128)(2,1)} %get-tuple-element.90.got_first, bf16[2,8,160,384]{3,2,1,0:T(8,128)(2,1)} %get-tuple-element.91.got_last), custom_call_target="tpu_custom_call" | custom-call | tf_op jit(solution)/shard_map/pallas_call | solution.py:953
  262.8 0.7 copy.86
  263.6 0.7 copy.87
  (83 shorter events, 3.2 us)
Async XLA Ops:
  0.6 2.9 %copy-start = (bf16[2,384,768]{2,1,0:T(8,128)(2,1)S(1)}, bf16[2,384,768]{2,1,0:T(8,128)(2,1)}, u32[]{:S(2)}) copy-start(bf16[2,384,768]{2,1,0:T(8,128)(2,1)} %param.22) | copy-start | bytes 3538948
  3.5 1.2 copy-start.8
  3.5 1.2 copy-start.10
  3.5 1.2 copy-start.11
  3.6 1.3 copy-start.12
  3.6 1.3 copy-start.13
  3.6 1.3 copy-start.9
  4.5 1.2 copy-start.14
  42.4 0.9 copy-start.3
  43.3 0.9 copy-start.4
  45.1 1.1 copy-start.1
  46.3 0.8 copy-start.2
  255.3 6.9 %copy-start.7 = (f32[2,96]{1,0:T(2,128)}, f32[2,96]{1,0:T(2,128)S(1)}, u32[]{:S(2)}) copy-start(f32[2,96]{1,0:T(2,128)S(1)} %fusion.7) | copy-start | bytes 2308
  256.6 6.2 %copy-start.5 = (f32[128,768]{1,0:T(8,128)S(1)}, f32[128,768]{1,0:T(8,128)}, u32[]{:S(2)}) copy-start(f32[128,768]{1,0:T(8,128)} %get-tuple-element.76) | copy-start | bytes 1179652
  256.6 7.0 %copy-start.6 = (f32[128,768]{1,0:T(8,128)S(1)}, f32[128,768]{1,0:T(8,128)}, u32[]{:S(2)}) copy-start(f32[128,768]{1,0:T(8,128)} %get-tuple-element.89) | copy-start | bytes 1179652

commit v4 on v3

--- a/solution.py
+++ b/solution.py
@@ -186,7 +186,7 @@
 
 def params(collective_id):
     return pltpu.CompilerParams(
-        collective_id=collective_id, has_side_effects=True, vmem_limit_bytes=56 * 1024 * 1024
+        collective_id=collective_id, has_side_effects=True, vmem_limit_bytes=36 * 1024 * 1024
     )
 
 
@@ -489,7 +489,7 @@
 
 
 def local_params():
-    return pltpu.CompilerParams(vmem_limit_bytes=56 * 1024 * 1024)
+    return pltpu.CompilerParams(vmem_limit_bytes=36 * 1024 * 1024)
 
 
 def forward_kernel(*refs):

time: 265 us -> 250 us (0.943)
  Pallas kernels: 246 us -> 224 us
  local copies, waits for them, and re-layouts: 12.6 us -> 19 us
    unnamed x40 -> x68, local copies, waits for them, and re-layouts: 7.62 us -> 15.5 us
    pallas_call x1, Pallas kernels: 69.6 us -> 63.2 us  [last(): pl.pallas_call(last_kernel, out_shape=(jax.ShapeDtypeStruct((TOK, D), F32...]
    pallas_call x1, Pallas kernels: 63.9 us -> 58.7 us  [turn(): pl.pallas_call(turn_kernel, out_shape=(tokens, tokens, jax.ShapeDtypeStru...]
    pallas_call x1, Pallas kernels: 13.9 us -> 10.1 us  [forward(): pl.pallas_call(forward_kernel, out_shape=forward_shapes(), in_specs=[VMEM...]
    pallas_call x1, Pallas kernels: 55.8 us -> 52.4 us  [forward_between(): pl.pallas_call(forward_between_kernel, out_shape=forward_shapes() + (jax....]
where the time goes in v4:
time: 250 us; the launch traced here: 248 us
  Pallas kernels  224 us (90%)
  local copies, waits for them, and re-layouts  19 us (8%)
  other arithmetic  3.81 us (2%)
    pallas_call x1, Pallas kernels, last(): pl.pallas_call(last_kernel, out_shape=(jax.ShapeDtypeStruct((TOK, D), F32...  63.2 us
    pallas_call x1, Pallas kernels, turn(): pl.pallas_call(turn_kernel, out_shape=(tokens, tokens, jax.ShapeDtypeStru...  58.7 us
    pallas_call x1, Pallas kernels, forward_between(): pl.pallas_call(forward_between_kernel, out_shape=forward_shapes() + (jax....  52.4 us
    pallas_call x1, Pallas kernels, gather_weights(): pl.pallas_call(weights_kernel, out_shape=(COLS_SHAPE, PIECES_SHAPE, jax.S...  35.3 us
    unnamed x68, local copies, waits for them, and re-layouts  15.5 us
    pallas_call x1, Pallas kernels, forward(): pl.pallas_call(forward_kernel, out_shape=forward_shapes(), in_specs=[VMEM...  10.1 us

profile of v4, /device:TPU:1, one launch (start us, length us, event | category | flops | bytes accessed | tf_op | source)
XLA Modules:
  0.0 248.2 jit_solution(17502382353175096928)
XLA Ops:
  0.7 1.7 copy.34
  2.7 0.8 constant_dynamic-slice_fusion.4
  3.6 0.9 constant_dynamic-slice_fusion.5
  4.7 0.7 slice_bitcast_fusion.3
  5.8 35.3 %shard_map.220 = (bf16[2,8,96,384]{3,2,1,0:T(8,128)(2,1)S(1)}, bf16[2,8,64,384]{3,2,1,0:T(8,128)(2,1)S(1)}, bf16[2,8,16,384]{3,2,1,0:T(8,128)(2,1)S(1)}, f32[8,2...) custom-call(bf16[2,176,384]{2,1,0:T(8,128)(2,1)S(1)} %fusion.1.src, f32[24,128]{1,0:T(8,128)S(1)} %pad_maximum_fusion.4.places, ...), custom_call_target="tpu_custom_call" | custom-call | tf_op jit(solution)/shard_map/pallas_call | solution.py:306
  41.2 1.1 copy-done.8
  42.3 0.9 copy-done.11
  43.2 0.9 shard_map.221
  44.1 1.1 copy-done.1
  45.3 0.9 pad_maximum_fusion.1.refs_9_
  46.2 1.4 copy-done.9
  47.6 1.0 copy-done.10
  48.6 1.1 copy-done.12
  49.8 52.4 %shard_map.222 = (bf16[8,128,768]{2,1,0:T(8,128)(2,1)}, bf16[1024,768]{1,0:T(8,128)(2,1)S(1)}, bf16[1024,128]{1,0:T(8,128)(2,1)S(1)}, bf16[1024,128]{1,0:T(8,128...) custom-call(bf16[1024,768]{1,0:T(8,128)(2,1)S(1)} %bitcast.76, ...), custom_call_target="tpu_custom_call" | custom-call | tf_op jit(solution)/shard_map/pallas_call | solution.py:559
  102.2 10.1 %shard_map.223 = (bf16[8,128,768]{2,1,0:T(8,128)(2,1)S(1)}, bf16[1024,768]{1,0:T(8,128)(2,1)S(1)}, bf16[1024,128]{1,0:T(8,128)(2,1)S(1)}, bf16[1024,128]{1,0:T(8...) custom-call(bf16[1024,768]{1,0:T(8,128)(2,1)S(1)} %bitcast.77, ...), custom_call_target="tpu_custom_call" | custom-call | tf_op jit(solution)/shard_map/pallas_call | solution.py:500
  112.3 58.7 %shard_map.224 = (f32[128,768]{1,0:T(8,128)S(1)}, f32[128,768]{1,0:T(8,128)S(1)}, bf16[8,128,768]{2,1,0:T(8,128)(2,1)S(1)}, f32[8,768]{1,0:T(8,128)S(1)}, bf16[160,384]{1,0:T(8,128)(2,1)S(1)}) custom-call(bf16[1024,768]{1,0:T(8,128)(2,1)S(1)} %bitcast.78, bf16[2,768,384]{2,1,0:T(8,128)(2,1)S(1)} %bitcast.72, ...), custom_call_target="tpu_custom_call" | custom-call | tf_op jit(solution)/shard_map/pallas_call | solution.py:789
  171.1 63.2 %shard_map.225 = (f32[128,768]{1,0:T(8,128)S(1)}, bf16[2,8,176,384]{3,2,1,0:T(8,128)(2,1)S(1)}, bf16[2,8,160,384]{3,2,1,0:T(8,128)(2,1)S(1)}) custom-call(bf16[1024,768]{1,0:T(8,128)(2,1)S(1)} %bitcast.79, bf16[2,768,384]{2,1,0:T(8,128)(2,1)S(1)} %bitcast.70, bf16[1024,768]{1,0:T(8,128)(2,1)S(1)} %get-tuple-element.78.refs_2_, ...), custom_call_target="tpu_custom_call" | custom-call | tf_op jit(solution)/shard_map/pallas_call | solution.py:891
  234.3 1.3 copy-done.6
  235.6 0.7 copy-done.15
  236.4 1.3 copy-done.4
  241.1 1.6 copy-done.5
  242.7 3.4 %shard_map.226 = (f32[2,96,2304]{2,1,0:T(8,128)}, f32[2,96,768]{2,1,0:T(8,128)}, f32[2,96,3072]{2,1,0:T(8,128)}, f32[2,384,768]{2,1,0:T(8,128)}) custom-call(bf16[2,8,176,384]{3,2,1,0:T(8,128)(2,1)S(1)} %copy-done.5, bf16[2,8,160,384]{3,2,1,0:T(8,128)(2,1)S(1)} %copy-done.7), custom_call_target="tpu_custom_call" | custom-call | tf_op jit(solution)/shard_map/pallas_call | solution.py:953
  246.7 0.7 copy.86
  247.4 0.7 copy.87
  (111 shorter events, 4.6 us)
Async XLA Ops:
  0.6 2.9 %copy-start = (bf16[2,384,768]{2,1,0:T(8,128)(2,1)S(1)}, bf16[2,384,768]{2,1,0:T(8,128)(2,1)}, u32[]{:S(2)}) copy-start(bf16[2,384,768]{2,1,0:T(8,128)(2,1)} %param.22) | copy-start | bytes 3538948
  3.5 1.8 copy-start.22
  3.5 1.9 copy-start.24
  3.5 1.9 copy-start.25
  3.6 1.9 copy-start.26
  3.6 1.9 copy-start.27
  3.6 2.0 copy-start.23
  4.6 1.3 copy-start.3
  41.2 1.1 copy-start.8
  44.1 1.1 copy-start.1
  46.2 1.4 copy-start.9
  49.8 52.4 %copy-start.2 = (f32[3,1024,128]{2,1,0:T(8,128)S(1)}, f32[3,1024,128]{2,1,0:T(8,128)}, u32[]{:S(2)}) copy-start(f32[3,1024,128]{2,1,0:T(8,128)} %copy-done.1) | copy-start | bytes 4718596
  102.1 10.1 %copy-start.17 = (bf16[1024,128]{1,0:T(8,128)(2,1)}, bf16[1024,128]{1,0:T(8,128)(2,1)S(1)}, u32[]{:S(2)}) copy-start(bf16[1024,128]{1,0:T(8,128)(2,1)S(1)} %get-tuple-element.80.refs_4_) | copy-start | bytes 786436
  102.2 10.1 %copy-start.19 = (bf16[1024,128]{1,0:T(8,128)(2,1)}, bf16[1024,128]{1,0:T(8,128)(2,1)S(1)}, u32[]{:S(2)}) copy-start(bf16[1024,128]{1,0:T(8,128)(2,1)S(1)} %get-tuple-element.81.refs_5_) | copy-start | bytes 786436
  112.3 58.8 %copy-start.18 = (bf16[1024,128]{1,0:T(8,128)(2,1)S(1)}, bf16[1024,128]{1,0:T(8,128)(2,1)}, u32[]{:S(2)}) copy-start(bf16[1024,128]{1,0:T(8,128)(2,1)} %copy-done.17) | copy-start | bytes 786436
  112.3 58.8 %copy-start.20 = (bf16[1024,128]{1,0:T(8,128)(2,1)S(1)}, bf16[1024,128]{1,0:T(8,128)(2,1)}, u32[]{:S(2)}) copy-start(bf16[1024,128]{1,0:T(8,128)(2,1)} %copy-done.19) | copy-start | bytes 786436
  171.1 63.3 %copy-start.13 = (f32[128,768]{1,0:T(8,128)}, f32[128,768]{1,0:T(8,128)S(1)}, u32[]{:S(2)}) copy-start(f32[128,768]{1,0:T(8,128)S(1)} %get-tuple-element.76) | copy-start | bytes 1179652
  234.3 1.3 copy-start.6
  235.6 5.5 %copy-start.7 = (bf16[2,8,160,384]{3,2,1,0:T(8,128)(2,1)S(1)}, bf16[2,8,160,384]{3,2,1,0:T(8,128)(2,1)}, u32[]{:S(2)}) copy-start(bf16[2,8,160,384]{3,2,1,0:T(8,128)(2,1)} %copy-done.6) | copy-start | bytes 5898244
  236.3 1.3 copy-start.4
  239.9 6.2 %copy-start.21 = (f32[2,96]{1,0:T(2,128)}, f32[2,96]{1,0:T(2,128)S(1)}, u32[]{:S(2)}) copy-start(f32[2,96]{1,0:T(2,128)S(1)} %fusion.7) | copy-start | bytes 2308
  241.1 1.6 copy-start.5
  242.7 3.9 %copy-start.14 = (f32[128,768]{1,0:T(8,128)S(1)}, f32[128,768]{1,0:T(8,128)}, u32[]{:S(2)}) copy-start(f32[128,768]{1,0:T(8,128)} %copy-done.13) | copy-start | bytes 1179652
  242.7 4.7 %copy-start.16 = (f32[128,768]{1,0:T(8,128)S(1)}, f32[128,768]{1,0:T(8,128)}, u32[]{:S(2)}) copy-start(f32[128,768]{1,0:T(8,128)} %copy-done.15) | copy-start | bytes 1179652
  (5 other events, 4.8 us)

commit v5 on v4

--- a/solution.py
+++ b/solution.py
@@ -120,6 +120,32 @@
         copy.wait_recv()
 
 
+def gather_few_steps(lane, group, own, at, cut, rows):
+    head, tail = pl.ds(0, cut), pl.ds(cut, rows - cut)
+    go = lane.go
+    me, twin, far = group.slot(0, 0), group.slot(0, 1), group.slot(2, 0)
+    c0 = go(own, at(me), group.right)
+    c1 = go(own, at(me), group.left)
+    c2 = go(own, at(me), group.pair)
+    yield
+    c0.wait_recv()
+    behind = at(group.slot(3, 0)).at[head]
+    c3 = go(behind, behind, group.right)
+    c1.wait_recv()
+    ahead = at(group.slot(1, 0)).at[tail]
+    c4 = go(ahead, ahead, group.left)
+    c2.wait_recv()
+    c5 = go(at(twin), at(twin), group.right)
+    c6 = go(at(twin), at(twin), group.left)
+    yield
+    c3.wait_recv()
+    c4.wait_recv()
+    c7 = go(at(far), at(far), group.pair)
+    yield
+    for copy in (c5, c6, c7):
+        copy.wait_recv()
+
+
 SCATTERS = 11
 
 
@@ -226,12 +252,12 @@
 SHARD_LANE = N - 1 + 3
 
 
-def shard_steps(lane, lane_z, fsdp, cs, core, src, cut, rows, scratch, outs, own, kept):
+def shard_steps(lane, lane_z, fsdp, cs, core, src, cut, rows, scratch, outs, own, kept, gather=gather_steps):
     held, mixed, got = scratch
     c, k = lax.axis_index("ctx"), lax.axis_index("dp")
     first = pltpu.make_async_copy(src.at[k], held.at[fsdp.slot(0, 0)], own.at[0])
     first.start()
-    yield from gather_steps(lane_z, fsdp, src.at[k], lambda slot: held.at[slot], cut, rows)
+    yield from gather(lane_z, fsdp, src.at[k], lambda slot: held.at[slot], cut, rows)
     first.wait()
     low = lax.broadcasted_iota(jnp.int32, (16, HALF), 0) < 8
     for i in range(N):
@@ -286,11 +312,13 @@
         keep = pltpu.make_async_copy(unit, unit_all.at[c], keeps.at[1])
         keep.start()
         kept.append(keep)
-        yield from gather_steps(lane_u, ctx, unit, lambda slot: unit_all.at[slot], TOK // 2, TOK)
+        yield from gather_few_steps(lane_u, ctx, unit, lambda slot: unit_all.at[slot], TOK // 2, TOK)
 
     outs = (cols_all, pieces_all, vec_all)
     run(
-        shard_steps(lane, lane_z, fsdp, cs, core, src, W_CUT, W_FIRST, scratch, outs, own, kept),
+        shard_steps(
+            lane, lane_z, fsdp, cs, core, src, W_CUT, W_FIRST, scratch, outs, own, kept, gather_few_steps
+        ),
         tokens(),
     )
     for copy in marks:
@@ -470,6 +498,66 @@
         branch[i] = dot(mixed[rows], w_mix[...], ((1,), (0,))).astype(BF)
 
 
+def unit_rows_of(b):
+    s = lax.axis_index("ctx") % 2
+    lanes = lax.broadcasted_iota(jnp.int32, (BLOCK, 2 * HEAD_DIM), 1)
+    if b < BLOCKS:
+        return b * BLOCK, lanes < HEAD_DIM
+    return pl.multiple_of(s * (SEQ // 2) + (b - BLOCKS) * BLOCK, BLOCK), lanes >= HEAD_DIM
+
+
+def forward_unrolled(
+    unit, vectors, w_cat, pieces, col, row, tables,
+    branch, normed, query, key, value, slope, mixed, lse, w_mix, turned,
+):
+    mix_rows(pieces, w_mix)
+    for i in range(BLOCKS):
+        rows = pl.ds(i * BLOCK, BLOCK)
+        low = (unit[rows].astype(F32) * vectors[0:1] + vectors[1:2]).astype(BF)
+        normed[rows] = low
+        heads = dot(low, w_cat[0], ((1,), (0,))) + vectors[3:4, :HALF]
+
+        def rotate(values, rows=rows):
+            return (
+                values * tables[0, rows]
+                + pltpu.roll(values, 8, axis=1) * tables[1, rows]
+                + pltpu.roll(values, 120, axis=1) * tables[2, rows]
+            )
+
+        query[rows] = (rotate(heads[:, :128]) * HEAD_DIM ** (-0.5)).astype(BF)
+        key[rows] = rotate(heads[:, 128:256]).astype(BF)
+        value[rows] = heads[:, 256:].astype(BF)
+        pre = dot(low, w_cat[1], ((1,), (0,))) + vectors[3:4, HALF:]
+        cdf = 0.5 * (1.0 + lax.erf(pre * 0.5**0.5))
+        mixed[rows, pl.ds(128, HALF)] = (pre * cdf).astype(BF)
+        mixed[rows, pl.ds(0, 128)] = jnp.zeros((BLOCK, 128), BF)
+        slope[rows] = cdf + pre * (jnp.exp(-0.5 * pre * pre) * 0.3989422804014327)
+        yield
+
+    turned[...] = value[...].astype(F32).T.astype(BF)
+    for b in range(BLOCKS + 2):
+        start, mask = unit_rows_of(b)
+        rows = pl.ds(start, BLOCK)
+        q = jnp.where(mask, query[rows].astype(F32), 0.0).astype(BF)
+        scores = dot(key[...], q, ((1,), (1,)))
+        seen = jnp.concatenate([col[...], col[...]], axis=1) <= row[pl.ds(start // BLOCK, 1)]
+        scores = jnp.where(seen, scores, -jnp.inf)
+        top = jnp.max(scores, axis=0, keepdims=True)
+        expos = jnp.exp(scores - top)
+        total = jnp.sum(expos, axis=0, keepdims=True)
+        lse[pl.ds(b, 1)] = top + jnp.log(total)
+        probs = (expos * (1.0 / total)).astype(BF)
+        out = dot(turned[...], probs, ((1,), (0,))).T
+        mixed[rows, pl.ds(0, 128)] = jnp.where(mask, out, mixed[rows, pl.ds(0, 128)].astype(F32)).astype(BF)
+        yield
+    for i in range(BLOCKS):
+        rows = pl.ds(i * BLOCK, BLOCK)
+        out = dot(mixed[rows], w_mix[...], ((1,), (0,))).astype(BF)
+        branch[2 * i] = out[:TOK]
+        branch[2 * i + 1] = out[TOK:]
+        yield
+
+
 def forward_shapes():
     shape = jax.ShapeDtypeStruct
     return (
@@ -493,7 +581,7 @@
 
 
 def forward_kernel(*refs):
-    run(forward_steps(*refs))
+    run(forward_unrolled(*refs))
 
 
 def forward(*args):

time: 250 us -> 244 us (0.976)
  Pallas kernels: 224 us -> 218 us
    pallas_call x1, Pallas kernels: 35.3 us -> 32.2 us  [gather_weights(): pl.pallas_call(weights_kernel, out_shape=(COLS_SHAPE, PIECES_SHAPE, jax.S...]
where the time goes in v5:
time: 244 us; the launch traced here: 242 us
  Pallas kernels  218 us (89%)
  local copies, waits for them, and re-layouts  19 us (8%)
  other arithmetic  3.81 us (2%)
    pallas_call x1, Pallas kernels, last(): pl.pallas_call(last_kernel, out_shape=(jax.ShapeDtypeStruct((TOK, D), F32...  64.1 us
    pallas_call x1, Pallas kernels, turn(): pl.pallas_call(turn_kernel, out_shape=(tokens, tokens, jax.ShapeDtypeStru...  58 us
    pallas_call x1, Pallas kernels, forward_between(): pl.pallas_call(forward_between_kernel, out_shape=forward_shapes() + (jax....  51.7 us
    pallas_call x1, Pallas kernels, gather_weights(): pl.pallas_call(weights_kernel, out_shape=(COLS_SHAPE, PIECES_SHAPE, jax.S...  32.2 us
    unnamed x68, local copies, waits for them, and re-layouts  15.5 us
    pallas_call x1, Pallas kernels, forward(): pl.pallas_call(forward_kernel, out_shape=forward_shapes(), in_specs=[VMEM...  8.16 us

profile of v5, /device:TPU:1, one launch (start us, length us, event | category | flops | bytes accessed | tf_op | source)
XLA Modules:
  0.0 242.5 jit_solution(4236027212890661553)
XLA Ops:
  0.7 1.7 copy.34
  2.7 0.8 constant_dynamic-slice_fusion.4
  3.6 0.9 constant_dynamic-slice_fusion.5
  4.7 0.7 slice_bitcast_fusion.3
  5.8 32.2 %shard_map.220 = (bf16[2,8,96,384]{3,2,1,0:T(8,128)(2,1)S(1)}, bf16[2,8,64,384]{3,2,1,0:T(8,128)(2,1)S(1)}, bf16[2,8,16,384]{3,2,1,0:T(8,128)(2,1)S(1)}, f32[8,2...) custom-call(bf16[2,176,384]{2,1,0:T(8,128)(2,1)S(1)} %fusion.1.src, f32[24,128]{1,0:T(8,128)S(1)} %pad_maximum_fusion.4.places, ...), custom_call_target="tpu_custom_call" | custom-call | tf_op jit(solution)/shard_map/pallas_call | solution.py:334
  38.0 1.1 copy-done.8
  39.2 0.9 copy-done.11
  40.0 0.9 shard_map.221
  41.0 1.1 copy-done.1
  42.1 0.9 pad_maximum_fusion.1.refs_9_
  43.1 1.4 copy-done.9
  44.5 1.0 copy-done.10
  45.5 1.1 copy-done.12
  46.6 51.7 %shard_map.222 = (bf16[8,128,768]{2,1,0:T(8,128)(2,1)}, bf16[1024,768]{1,0:T(8,128)(2,1)S(1)}, bf16[1024,128]{1,0:T(8,128)(2,1)S(1)}, bf16[1024,128]{1,0:T(8,128...) custom-call(bf16[1024,768]{1,0:T(8,128)(2,1)S(1)} %bitcast.76, ...), custom_call_target="tpu_custom_call" | custom-call | tf_op jit(solution)/shard_map/pallas_call | solution.py:647
  98.3 8.2 %shard_map.223 = (bf16[8,128,768]{2,1,0:T(8,128)(2,1)S(1)}, bf16[1024,768]{1,0:T(8,128)(2,1)S(1)}, bf16[1024,128]{1,0:T(8,128)(2,1)S(1)}, bf16[1024,128]{1,0:T(8...) custom-call(bf16[1024,768]{1,0:T(8,128)(2,1)S(1)} %bitcast.77, ...), custom_call_target="tpu_custom_call" | custom-call | tf_op jit(solution)/shard_map/pallas_call | solution.py:588
  106.5 58.0 %shard_map.224 = (f32[128,768]{1,0:T(8,128)S(1)}, f32[128,768]{1,0:T(8,128)S(1)}, bf16[8,128,768]{2,1,0:T(8,128)(2,1)S(1)}, f32[8,768]{1,0:T(8,128)S(1)}, bf16[160,384]{1,0:T(8,128)(2,1)S(1)}) custom-call(bf16[1024,768]{1,0:T(8,128)(2,1)S(1)} %bitcast.78, bf16[2,768,384]{2,1,0:T(8,128)(2,1)S(1)} %bitcast.72, ...), custom_call_target="tpu_custom_call" | custom-call | tf_op jit(solution)/shard_map/pallas_call | solution.py:877
  164.5 64.1 %shard_map.225 = (f32[128,768]{1,0:T(8,128)S(1)}, bf16[2,8,176,384]{3,2,1,0:T(8,128)(2,1)S(1)}, bf16[2,8,160,384]{3,2,1,0:T(8,128)(2,1)S(1)}) custom-call(bf16[1024,768]{1,0:T(8,128)(2,1)S(1)} %bitcast.79, bf16[2,768,384]{2,1,0:T(8,128)(2,1)S(1)} %bitcast.70, bf16[1024,768]{1,0:T(8,128)(2,1)S(1)} %get-tuple-element.78.refs_2_, ...), custom_call_target="tpu_custom_call" | custom-call | tf_op jit(solution)/shard_map/pallas_call | solution.py:979
  228.6 1.3 copy-done.6
  229.9 0.7 copy-done.15
  230.6 1.3 copy-done.4
  235.4 1.6 copy-done.5
  237.0 3.4 %shard_map.226 = (f32[2,96,2304]{2,1,0:T(8,128)}, f32[2,96,768]{2,1,0:T(8,128)}, f32[2,96,3072]{2,1,0:T(8,128)}, f32[2,384,768]{2,1,0:T(8,128)}) custom-call(bf16[2,8,176,384]{3,2,1,0:T(8,128)(2,1)S(1)} %copy-done.5, bf16[2,8,160,384]{3,2,1,0:T(8,128)(2,1)S(1)} %copy-done.7), custom_call_target="tpu_custom_call" | custom-call | tf_op jit(solution)/shard_map/pallas_call | solution.py:1041
  241.0 0.7 copy.86
  241.7 0.7 copy.87
  (111 shorter events, 4.6 us)
Async XLA Ops:
  0.6 2.9 %copy-start = (bf16[2,384,768]{2,1,0:T(8,128)(2,1)S(1)}, bf16[2,384,768]{2,1,0:T(8,128)(2,1)}, u32[]{:S(2)}) copy-start(bf16[2,384,768]{2,1,0:T(8,128)(2,1)} %param.22) | copy-start | bytes 3538948
  3.5 1.8 copy-start.22
  3.5 1.9 copy-start.24
  3.5 1.9 copy-start.25
  3.6 1.9 copy-start.26
  3.6 1.9 copy-start.27
  3.6 2.0 copy-start.23
  4.6 1.3 copy-start.3
  38.0 1.1 copy-start.8
  40.9 1.1 copy-start.1
  43.1 1.4 copy-start.9
  46.6 51.7 %copy-start.2 = (f32[3,1024,128]{2,1,0:T(8,128)S(1)}, f32[3,1024,128]{2,1,0:T(8,128)}, u32[]{:S(2)}) copy-start(f32[3,1024,128]{2,1,0:T(8,128)} %copy-done.1) | copy-start | bytes 4718596
  98.3 8.2 %copy-start.17 = (bf16[1024,128]{1,0:T(8,128)(2,1)}, bf16[1024,128]{1,0:T(8,128)(2,1)S(1)}, u32[]{:S(2)}) copy-start(bf16[1024,128]{1,0:T(8,128)(2,1)S(1)} %get-tuple-element.80.refs_4_) | copy-start | bytes 786436
  98.3 8.2 %copy-start.19 = (bf16[1024,128]{1,0:T(8,128)(2,1)}, bf16[1024,128]{1,0:T(8,128)(2,1)S(1)}, u32[]{:S(2)}) copy-start(bf16[1024,128]{1,0:T(8,128)(2,1)S(1)} %get-tuple-element.81.refs_5_) | copy-start | bytes 786436
  106.5 58.0 %copy-start.18 = (bf16[1024,128]{1,0:T(8,128)(2,1)S(1)}, bf16[1024,128]{1,0:T(8,128)(2,1)}, u32[]{:S(2)}) copy-start(bf16[1024,128]{1,0:T(8,128)(2,1)} %copy-done.17) | copy-start | bytes 786436
  106.5 58.0 %copy-start.20 = (bf16[1024,128]{1,0:T(8,128)(2,1)S(1)}, bf16[1024,128]{1,0:T(8,128)(2,1)}, u32[]{:S(2)}) copy-start(bf16[1024,128]{1,0:T(8,128)(2,1)} %copy-done.19) | copy-start | bytes 786436
  164.5 64.1 %copy-start.13 = (f32[128,768]{1,0:T(8,128)}, f32[128,768]{1,0:T(8,128)S(1)}, u32[]{:S(2)}) copy-start(f32[128,768]{1,0:T(8,128)S(1)} %get-tuple-element.76) | copy-start | bytes 1179652
  228.6 1.3 copy-start.6
  229.9 5.5 %copy-start.7 = (bf16[2,8,160,384]{3,2,1,0:T(8,128)(2,1)S(1)}, bf16[2,8,160,384]{3,2,1,0:T(8,128)(2,1)}, u32[]{:S(2)}) copy-start(bf16[2,8,160,384]{3,2,1,0:T(8,128)(2,1)} %copy-done.6) | copy-start | bytes 5898244
  230.6 1.3 copy-start.4
  234.1 6.2 %copy-start.21 = (f32[2,96]{1,0:T(2,128)}, f32[2,96]{1,0:T(2,128)S(1)}, u32[]{:S(2)}) copy-start(f32[2,96]{1,0:T(2,128)S(1)} %fusion.7) | copy-start | bytes 2308
  235.4 1.6 copy-start.5
  237.0 3.9 %copy-start.14 = (f32[128,768]{1,0:T(8,128)S(1)}, f32[128,768]{1,0:T(8,128)}, u32[]{:S(2)}) copy-start(f32[128,768]{1,0:T(8,128)} %copy-done.13) | copy-start | bytes 1179652
  237.0 4.7 %copy-start.16 = (f32[128,768]{1,0:T(8,128)S(1)}, f32[128,768]{1,0:T(8,128)}, u32[]{:S(2)}) copy-start(f32[128,768]{1,0:T(8,128)} %copy-done.15) | copy-start | bytes 1179652
  (5 other events, 4.8 us)

commit v6 on v5

--- a/solution.py
+++ b/solution.py
@@ -621,18 +621,18 @@
         keep = pltpu.make_async_copy(unit, unit_all.at[ctx.slot(0, 0)], keeps.at[0])
         keep.start()
         kept.append(keep)
-        yield from gather_steps(lane_u, ctx, unit, lambda slot: unit_all.at[slot], TOK // 2, TOK)
+        yield from gather_few_steps(lane_u, ctx, unit, lambda slot: unit_all.at[slot], TOK // 2, TOK)
 
     def later():
         low_g[...] = cot[...].astype(BF)
         keep = pltpu.make_async_copy(low_g, low_all.at[ctx.slot(0, 0)], keeps.at[1])
         keep.start()
         kept.append(keep)
-        yield from gather_steps(lane_g, ctx, low_g, lambda slot: low_all.at[slot], TOK // 2, TOK)
+        yield from gather_few_steps(lane_g, ctx, low_g, lambda slot: low_all.at[slot], TOK // 2, TOK)
 
     outs_w = (cols_all, pieces_all)
     run(
-        shard_steps(lane_w, lane_z, fsdp, cs, core, src, CUT, ROWS, scratch, outs_w, own, kept),
+        shard_steps(lane_w, lane_z, fsdp, cs, core, src, CUT, ROWS, scratch, outs_w, own, kept, gather_few_steps),
         later(),
         tokens(),
     )
@@ -851,7 +851,7 @@
         keep = pltpu.make_async_copy(low_g, low_all.at[ctx.slot(0, 0)], keep_sem)
         keep.start()
         kept.append(keep)
-        yield from gather_steps(lane_g, ctx, low_g, lambda slot: low_all.at[slot], TOK // 2, TOK)
+        yield from gather_few_steps(lane_g, ctx, low_g, lambda slot: low_all.at[slot], TOK // 2, TOK)
 
     def weights():
         def take(total):

time: 244 us -> 249 us (1.020)
  Pallas kernels: 218 us -> 224 us
    pallas_call x1, Pallas kernels: 51.7 us -> 56.2 us  [forward_between(): pl.pallas_call(forward_between_kernel, out_shape=forward_shapes() + (jax....]
where the time goes in v6:
time: 249 us; the launch traced here: 248 us
  Pallas kernels  224 us (90%)
  local copies, waits for them, and re-layouts  19 us (8%)
  other arithmetic  3.81 us (2%)
    pallas_call x1, Pallas kernels, last(): pl.pallas_call(last_kernel, out_shape=(jax.ShapeDtypeStruct((TOK, D), F32...  64.2 us
    pallas_call x1, Pallas kernels, turn(): pl.pallas_call(turn_kernel, out_shape=(tokens, tokens, jax.ShapeDtypeStru...  59.1 us
    pallas_call x1, Pallas kernels, forward_between(): pl.pallas_call(forward_between_kernel, out_shape=forward_shapes() + (jax....  56.2 us
    pallas_call x1, Pallas kernels, gather_weights(): pl.pallas_call(weights_kernel, out_shape=(COLS_SHAPE, PIECES_SHAPE, jax.S...  32.2 us
    unnamed x68, local copies, waits for them, and re-layouts  15.5 us
    pallas_call x1, Pallas kernels, forward(): pl.pallas_call(forward_kernel, out_shape=forward_shapes(), in_specs=[VMEM...  8.16 us

profile of v6, /device:TPU:1, one launch (start us, length us, event | category | flops | bytes accessed | tf_op | source)
XLA Modules:
  0.0 248.3 jit_solution(17787499259049589511)
XLA Ops:
  0.7 1.7 copy.34
  2.7 0.8 constant_dynamic-slice_fusion.4
  3.6 0.9 constant_dynamic-slice_fusion.5
  4.7 0.7 slice_bitcast_fusion.3
  5.8 32.2 %shard_map.220 = (bf16[2,8,96,384]{3,2,1,0:T(8,128)(2,1)S(1)}, bf16[2,8,64,384]{3,2,1,0:T(8,128)(2,1)S(1)}, bf16[2,8,16,384]{3,2,1,0:T(8,128)(2,1)S(1)}, f32[8,2...) custom-call(bf16[2,176,384]{2,1,0:T(8,128)(2,1)S(1)} %fusion.1.src, f32[24,128]{1,0:T(8,128)S(1)} %pad_maximum_fusion.4.places, ...), custom_call_target="tpu_custom_call" | custom-call | tf_op jit(solution)/shard_map/pallas_call | solution.py:334
  38.0 1.1 copy-done.8
  39.2 0.9 copy-done.11
  40.0 0.9 shard_map.221
  41.0 1.1 copy-done.1
  42.1 0.9 pad_maximum_fusion.1.refs_9_
  43.1 1.4 copy-done.9
  44.5 1.0 copy-done.10
  45.5 1.1 copy-done.12
  46.6 56.2 %shard_map.222 = (bf16[8,128,768]{2,1,0:T(8,128)(2,1)}, bf16[1024,768]{1,0:T(8,128)(2,1)S(1)}, bf16[1024,128]{1,0:T(8,128)(2,1)S(1)}, bf16[1024,128]{1,0:T(8,128...) custom-call(bf16[1024,768]{1,0:T(8,128)(2,1)S(1)} %bitcast.76, ...), custom_call_target="tpu_custom_call" | custom-call | tf_op jit(solution)/shard_map/pallas_call | solution.py:647
  102.8 8.2 %shard_map.223 = (bf16[8,128,768]{2,1,0:T(8,128)(2,1)S(1)}, bf16[1024,768]{1,0:T(8,128)(2,1)S(1)}, bf16[1024,128]{1,0:T(8,128)(2,1)S(1)}, bf16[1024,128]{1,0:T(8...) custom-call(bf16[1024,768]{1,0:T(8,128)(2,1)S(1)} %bitcast.77, ...), custom_call_target="tpu_custom_call" | custom-call | tf_op jit(solution)/shard_map/pallas_call | solution.py:588
  111.0 59.1 %shard_map.224 = (f32[128,768]{1,0:T(8,128)S(1)}, f32[128,768]{1,0:T(8,128)S(1)}, bf16[8,128,768]{2,1,0:T(8,128)(2,1)S(1)}, f32[8,768]{1,0:T(8,128)S(1)}, bf16[160,384]{1,0:T(8,128)(2,1)S(1)}) custom-call(bf16[1024,768]{1,0:T(8,128)(2,1)S(1)} %bitcast.78, bf16[2,768,384]{2,1,0:T(8,128)(2,1)S(1)} %bitcast.72, ...), custom_call_target="tpu_custom_call" | custom-call | tf_op jit(solution)/shard_map/pallas_call | solution.py:877
  170.2 64.2 %shard_map.225 = (f32[128,768]{1,0:T(8,128)S(1)}, bf16[2,8,176,384]{3,2,1,0:T(8,128)(2,1)S(1)}, bf16[2,8,160,384]{3,2,1,0:T(8,128)(2,1)S(1)}) custom-call(bf16[1024,768]{1,0:T(8,128)(2,1)S(1)} %bitcast.79, bf16[2,768,384]{2,1,0:T(8,128)(2,1)S(1)} %bitcast.70, bf16[1024,768]{1,0:T(8,128)(2,1)S(1)} %get-tuple-element.78.refs_2_, ...), custom_call_target="tpu_custom_call" | custom-call | tf_op jit(solution)/shard_map/pallas_call | solution.py:979
  234.5 1.3 copy-done.6
  235.7 0.7 copy-done.15
  236.5 1.3 copy-done.4
  241.2 1.6 copy-done.5
  242.8 3.4 %shard_map.226 = (f32[2,96,2304]{2,1,0:T(8,128)}, f32[2,96,768]{2,1,0:T(8,128)}, f32[2,96,3072]{2,1,0:T(8,128)}, f32[2,384,768]{2,1,0:T(8,128)}) custom-call(bf16[2,8,176,384]{3,2,1,0:T(8,128)(2,1)S(1)} %copy-done.5, bf16[2,8,160,384]{3,2,1,0:T(8,128)(2,1)S(1)} %copy-done.7), custom_call_target="tpu_custom_call" | custom-call | tf_op jit(solution)/shard_map/pallas_call | solution.py:1041
  246.8 0.7 copy.86
  247.5 0.7 copy.87
  (111 shorter events, 4.6 us)
Async XLA Ops:
  0.6 2.9 %copy-start = (bf16[2,384,768]{2,1,0:T(8,128)(2,1)S(1)}, bf16[2,384,768]{2,1,0:T(8,128)(2,1)}, u32[]{:S(2)}) copy-start(bf16[2,384,768]{2,1,0:T(8,128)(2,1)} %param.22) | copy-start | bytes 3538948
  3.5 1.8 copy-start.22
  3.5 1.9 copy-start.24
  3.5 1.9 copy-start.25
  3.6 1.9 copy-start.26
  3.6 1.9 copy-start.27
  3.6 2.0 copy-start.23
  4.6 1.3 copy-start.3
  38.0 1.1 copy-start.8
  40.9 1.1 copy-start.1
  43.1 1.4 copy-start.9
  46.6 56.2 %copy-start.2 = (f32[3,1024,128]{2,1,0:T(8,128)S(1)}, f32[3,1024,128]{2,1,0:T(8,128)}, u32[]{:S(2)}) copy-start(f32[3,1024,128]{2,1,0:T(8,128)} %copy-done.1) | copy-start | bytes 4718596
  102.8 8.2 %copy-start.17 = (bf16[1024,128]{1,0:T(8,128)(2,1)}, bf16[1024,128]{1,0:T(8,128)(2,1)S(1)}, u32[]{:S(2)}) copy-start(bf16[1024,128]{1,0:T(8,128)(2,1)S(1)} %get-tuple-element.80.refs_4_) | copy-start | bytes 786436
  102.8 8.2 %copy-start.19 = (bf16[1024,128]{1,0:T(8,128)(2,1)}, bf16[1024,128]{1,0:T(8,128)(2,1)S(1)}, u32[]{:S(2)}) copy-start(bf16[1024,128]{1,0:T(8,128)(2,1)S(1)} %get-tuple-element.81.refs_5_) | copy-start | bytes 786436
  111.0 59.1 %copy-start.18 = (bf16[1024,128]{1,0:T(8,128)(2,1)S(1)}, bf16[1024,128]{1,0:T(8,128)(2,1)}, u32[]{:S(2)}) copy-start(bf16[1024,128]{1,0:T(8,128)(2,1)} %copy-done.17) | copy-start | bytes 786436
  111.0 59.1 %copy-start.20 = (bf16[1024,128]{1,0:T(8,128)(2,1)S(1)}, bf16[1024,128]{1,0:T(8,128)(2,1)}, u32[]{:S(2)}) copy-start(bf16[1024,128]{1,0:T(8,128)(2,1)} %copy-done.19) | copy-start | bytes 786436
  170.2 64.3 %copy-start.13 = (f32[128,768]{1,0:T(8,128)}, f32[128,768]{1,0:T(8,128)S(1)}, u32[]{:S(2)}) copy-start(f32[128,768]{1,0:T(8,128)S(1)} %get-tuple-element.76) | copy-start | bytes 1179652
  234.4 1.3 copy-start.6
  235.7 5.5 %copy-start.7 = (bf16[2,8,160,384]{3,2,1,0:T(8,128)(2,1)S(1)}, bf16[2,8,160,384]{3,2,1,0:T(8,128)(2,1)}, u32[]{:S(2)}) copy-start(bf16[2,8,160,384]{3,2,1,0:T(8,128)(2,1)} %copy-done.6) | copy-start | bytes 5898244
  236.5 1.3 copy-start.4
  240.0 6.2 %copy-start.21 = (f32[2,96]{1,0:T(2,128)}, f32[2,96]{1,0:T(2,128)S(1)}, u32[]{:S(2)}) copy-start(f32[2,96]{1,0:T(2,128)S(1)} %fusion.7) | copy-start | bytes 2308
  241.2 1.6 copy-start.5
  242.8 3.9 %copy-start.14 = (f32[128,768]{1,0:T(8,128)S(1)}, f32[128,768]{1,0:T(8,128)}, u32[]{:S(2)}) copy-start(f32[128,768]{1,0:T(8,128)} %copy-done.13) | copy-start | bytes 1179652
  242.8 4.7 %copy-start.16 = (f32[128,768]{1,0:T(8,128)S(1)}, f32[128,768]{1,0:T(8,128)}, u32[]{:S(2)}) copy-start(f32[128,768]{1,0:T(8,128)} %copy-done.15) | copy-start | bytes 1179652
  (5 other events, 4.8 us)
